TPU v7x, 512 devices: a whole 4x8x8 slice. The times are simulated.
512 devices in a mesh: lat: 8 (over z), lon: 16 (over y_lo, x, core), obs: 4 (over y_hi).
Axes of the slice: x: 4, y: 8 (y_hi: 4, y_lo: 2; y = y_hi * 2 + y_lo), z: 8, core: 2. Of those that a mesh axis runs over, the one named last changes fastest.
Arguments:
- control: float32 [4, 25, 64, 2048], P('obs', None, 'lat', 'lon'), may hold values from -6 to 6
- residual: float32 [4, 25, 64, 2048], P('obs', None, 'lat', 'lon'), may hold values from -6 to 6
- direction: float32 [4, 25, 64, 2048], P('obs', None, 'lat', 'lon'), may hold values from -6 to 6
- land_mask: int32 [64, 2048], P('lat', 'lon'), may hold values 0 or 1
- kappa_east: float32 [64, 2048], P('lat', 'lon'), may hold values from 0.25 to 4
- kappa_north: float32 [64, 2048], P('lat', 'lon'), may hold values from 0.25 to 4
- sigma: float32 [4, 64, 2048], P('obs', 'lat', 'lon'), may hold values from 0.5 to 2
- obs_weight: float32 [4, 25, 32768], P('obs', None, ('lat', 'lon')), may hold values from -6 to 6
- obs_cell: int32 [32768], P(('lat', 'lon')), may hold values from 0 to 1023
- obs_owner: int32 [32768, 1], P(('lat', 'lon')), may hold values from 0 to 127; in each aligned block of 256 rows (0 to 255, 256 to 511, ...) at most 4 rows name the same one
- error_inverse: float32 [128, 25, 25], P(('lat', 'lon')), may hold values from -1 to 2, as said below
Outputs:
- control_next: float32 [4, 25, 64, 2048], P('obs', None, 'lat', 'lon')
- residual_next: float32 [4, 25, 64, 2048], P('obs', None, 'lat', 'lon')
- direction_next: float32 [4, 25, 64, 2048], P('obs', None, 'lat', 'lon')
Inputs may be any that keep to these rules, and one draw needn't show every extreme that they name: `obs_owner`: in the rows of one device no owner is named by more than 4 rows. `error_inverse`: each matrix is symmetric with positive diagonal exceeding the sum of magnitudes of its row's other entries.
All inputs are finite; a program needn't handle non-finite values. No bound on the sum of `land_mask` on one device may be relied on, other than what follows from the above.
Results may differ from a plain program's by a relative error of at most 0.000078.
Values sent between devices are 32-bit elements; how exact they have to be, the bound alone decides.
No kernel may reach another device: no remote copies, remote signals or barrier semaphores. Data moves between devices by JAX's collectives and lax.ppermute only.
A program may use at most 64 MiB of HBM per device.

v0:
```python
import jax
import jax.numpy as jnp
from jax import lax
from jax.sharding import PartitionSpec as P

SWEEPS = 4


def padded_2(shard, sides, width, wrap):
    for axis, dim in sides:
        devices, length = (lax.axis_size(axis), shard.shape[dim])
        up = [(i, (i + 1) % devices) for i in range(devices if wrap else devices - 1)]
        down = [(j, i) for i, j in up]
        last = lax.slice_in_dim(shard, length - width, length, axis=dim)
        initial = lax.slice_in_dim(shard, 0, width, axis=dim)
        before = lax.ppermute(last, axis, up)
        after = lax.ppermute(initial, axis, down)
        shard = jnp.concatenate([before, shard, after], axis=dim)
    return shard


def stencil(iterate, source, c_east, c_west, c_north, c_south):
    scale = 1.0 + c_east + c_west + c_north + c_south
    near = (
        c_east * iterate[:, 1:-1, 2:]
        + c_west * iterate[:, 1:-1, :-2]
        + c_north * iterate[:, 2:, 1:-1]
        + c_south * iterate[:, :-2, 1:-1]
    )
    return (source + near) / scale


def diffuse(source, faces):
    rows, cols = (source.shape[1], source.shape[2])
    inner = SWEEPS - 1
    cut = [face[inner : inner + rows, inner : inner + cols] for face in faces]
    iterate = jnp.zeros_like(source)
    for sweep in range(SWEEPS):
        padded = padded_2(iterate, (("lon", 2),), 1, True)
        padded = padded_2(padded, (("lat", 1),), 1, False)
        iterate = stencil(padded, source, cut[0], cut[1], cut[2], cut[3])
    return iterate


def local(
    control,
    residual,
    direction,
    land_mask,
    kappa_east,
    kappa_north,
    sigma,
    obs_weight,
    obs_cell,
    obs_owner,
    error_inverse,
):
    fields_dev, levels, rows, cols = direction.shape
    flags = land_mask.astype(jnp.float32)
    stacked = jnp.stack([flags, kappa_east, kappa_north])
    stacked = padded_2(stacked, (("lon", 2),), SWEEPS, True)
    stacked = padded_2(stacked, (("lat", 1),), SWEEPS, False)
    wide_flags, east, north = (stacked[0], stacked[1], stacked[2])
    east_face = east[:, :-1] * wide_flags[:, :-1] * wide_flags[:, 1:]
    north_face = north[:-1] * wide_flags[:-1] * wide_flags[1:]
    faces = (east_face[1:-1, 1:], east_face[1:-1, :-1], north_face[1:, 1:-1], north_face[:-1, 1:-1])
    flat_shape = (fields_dev * levels, rows, cols)
    spread = (sigma * flags[None])[:, None]
    state = spread * diffuse(direction.reshape(flat_shape), faces).reshape(direction.shape)
    flat_state = state.reshape(fields_dev, levels, rows * cols)
    picked = flat_state[:, :, obs_cell]
    partial_column = jnp.sum(obs_weight * picked, axis=0)
    owner = obs_owner[:, 0]
    owners = lax.axis_size(("lat", "lon"))
    slots = obs_cell.shape[0]
    capacity = max(2, 2 * slots // owners)
    onehot = (owner[:, None] == jnp.arange(owners, dtype=jnp.int32)[None, :]).astype(jnp.int32)
    before = jnp.cumsum(onehot, axis=0) - onehot
    rank = jnp.sum(before * onehot, axis=1)
    position = owner * capacity + rank
    outgoing = (
        jnp.zeros((levels, owners * capacity), jnp.float32).at[:, position].set(partial_column)
    )
    received = lax.all_to_all(outgoing, ("lat", "lon"), split_axis=1, concat_axis=1, tiled=True)
    full_column = lax.psum(received, "obs")
    weighted_all = jnp.dot(
        error_inverse[0],
        full_column,
        precision=lax.Precision.HIGHEST,
        preferred_element_type=jnp.float32,
    )
    returned = lax.all_to_all(weighted_all, ("lat", "lon"), split_axis=1, concat_axis=1, tiled=True)
    weighted = returned[:, position]
    adjoint = (
        jnp.zeros((fields_dev, levels, rows * cols), jnp.float32)
        .at[:, :, obs_cell]
        .add(obs_weight * weighted[None])
    )
    adjoint = adjoint.reshape(direction.shape)
    image = direction + diffuse((spread * adjoint).reshape(flat_shape), faces).reshape(
        direction.shape
    )
    norm_now, curve = lax.psum(
        (jnp.sum(residual * residual), jnp.sum(direction * image)), ("lat", "lon", "obs")
    )
    alpha = norm_now / curve
    control_next = control + alpha * direction
    residual_next = residual - alpha * image
    norm_next = lax.psum(jnp.sum(residual_next * residual_next), ("lat", "lon", "obs"))
    direction_next = residual_next + norm_next / norm_now * direction
    return (control_next, residual_next, direction_next)


def solution(mesh):
    placed = (
        P("obs", None, "lat", "lon"),
        P("obs", None, "lat", "lon"),
        P("obs", None, "lat", "lon"),
        P("lat", "lon"),
        P("lat", "lon"),
        P("lat", "lon"),
        P("obs", "lat", "lon"),
        P("obs", None, ("lat", "lon")),
        P(("lat", "lon")),
        P(("lat", "lon"), None),
        P(("lat", "lon"), None, None),
    )
    return jax.shard_map(
        local,
        mesh=mesh,
        in_specs=placed,
        out_specs=(
            P("obs", None, "lat", "lon"),
            P("obs", None, "lat", "lon"),
            P("obs", None, "lat", "lon"),
        ),
        check_vma=False,
    )
```

profile of v0, /device:TPU:1, one launch (start us, length us, event | category | flops | bytes accessed | tf_op | source)
XLA Modules:
  0.0 425.2 jit_solution(99607301253511955)
XLA Ops:
  0.7 8.8 %collective-permute-start.4 = (f32[25,8,1]{2,1,0:T(8,128)S(1)}, f32[25,8,1]{2,1,0:T(8,128)S(1)}, u32[]{:S(2)}, u32[]{:S(2)}) collective-permute-start(f32[25,8,1]{2,1,0:T(8,128)S(1)} %broadcast.57), channel_id=1, source_target_pairs={{4,0},{8,4},{12,8},{16,12},{20,16},{24,20},{28,24},{32,28},{36,32}... | collective-permute-start | bytes 2408 | tf_op jit(solution)/shard_map/ppermute | solution.py:17
  13.9 3.2 collective-permute-start
  21.3 4.0 collective-permute-start.2
  29.6 3.6 collective-permute-done.6
  33.5 7.9 %collective-permute-start.8 = (f32[25,8,1]{2,1,0:T(8,128)S(1)}, f32[25,8,1]{2,1,0:T(8,128)S(1)}, u32[]{:S(2)}, u32[]{:S(2)}) collective-permute-start(f32[25,8,1]{2,1,0:T(8,128)S(1)} %get-tuple-element.38), channel_id=1, source_target_pairs={{4,0},{8,4},{12,8},{16,12},{20,16},{24,20},{28,24},{32,28},{36,32}... | collective-permute-start | bytes 2408 | tf_op jit(solution)/shard_map/ppermute | solution.py:17
  45.3 5.2 %collective-permute-start.11 = (f32[25,1,130]{2,1,0:T(1,128)S(1)}, f32[25,1,130]{2,1,0:T(1,128)S(1)}, u32[]{:S(2)}, u32[]{:S(2)}) collective-permute-start(f32[25,1,130]{2,1,0:T(1,128)S(1)} %get-tuple-element.22), channel_id=1, source_target_pairs={{0,64},{64,128},{128,192},{192,256},{256,320},{320,384},{384,448},... | collective-permute-start | bytes 39008 | tf_op jit(solution)/shard_map/ppermute | solution.py:16
  51.8 3.5 collective-permute-done.10
  55.7 7.6 %collective-permute-start.12 = (f32[25,8,1]{2,1,0:T(8,128)S(1)}, f32[25,8,1]{2,1,0:T(8,128)S(1)}, u32[]{:S(2)}, u32[]{:S(2)}) collective-permute-start(f32[25,8,1]{2,1,0:T(8,128)S(1)} %get-tuple-element.36), channel_id=1, source_target_pairs={{4,0},{8,4},{12,8},{16,12},{20,16},{24,20},{28,24},{32,28},{36,32}... | collective-permute-start | bytes 2408 | tf_op jit(solution)/shard_map/ppermute | solution.py:17
  67.1 4.8 %collective-permute-start.15 = (f32[25,1,130]{2,1,0:T(1,128)S(1)}, f32[25,1,130]{2,1,0:T(1,128)S(1)}, u32[]{:S(2)}, u32[]{:S(2)}) collective-permute-start(f32[25,1,130]{2,1,0:T(1,128)S(1)} %get-tuple-element.20), channel_id=1, source_target_pairs={{0,64},{64,128},{128,192},{192,256},{256,320},{320,384},{384,448},... | collective-permute-start | bytes 39008 | tf_op jit(solution)/shard_map/ppermute | solution.py:16
  73.3 3.5 collective-permute-done.14
  77.2 7.6 %collective-permute-start.16 = (f32[25,8,1]{2,1,0:T(8,128)S(1)}, f32[25,8,1]{2,1,0:T(8,128)S(1)}, u32[]{:S(2)}, u32[]{:S(2)}) collective-permute-start(f32[25,8,1]{2,1,0:T(8,128)S(1)} %get-tuple-element.34), channel_id=1, source_target_pairs={{4,0},{8,4},{12,8},{16,12},{20,16},{24,20},{28,24},{32,28},{36,32}... | collective-permute-start | bytes 2408 | tf_op jit(solution)/shard_map/ppermute | solution.py:17
  88.6 3.6 collective-permute-start.19
  93.7 3.1 collective-permute-done.18
  99.3 24.2 %all_to_all.24 = f32[25,128,4]{0,2,1:T(4,128)S(1)} all-to-all(f32[25,128,4]{0,2,1:T(4,128)S(1)} %bitcast.82), channel_id=1, replica_groups=mesh['lat'=8,'lon'=16,'obs'=4] {'lat','lon'}, dimensions={1} | all-to-all | bytes 102400 | tf_op jit(solution)/shard_map/all_to_all | solution.py:84
  123.5 22.5 %psum.29 = f32[25,512]{0,1:T(8,128)S(1)} all-reduce(f32[25,512]{0,1:T(8,128)S(1)} %bitcast.83), channel_id=1, replica_groups=mesh['lat'=8,'lon'=16,'obs'=4] {'obs'}, use_global_device_ids=true, to_apply=%region_6.7 | all-reduce | flops 12800 | bytes 102400 | tf_op jit(solution)/shard_map/psum | solution.py:85
  147.2 9.5 %all-to-all-start.1 = ((f32[25,128,4]{0,2,1:T(4,128)}), f32[25,128,4]{0,2,1:T(4,128)S(1)}, u32[]{:S(2)}, u32[]{:S(2)}) async-start(f32[25,128,4]{0,2,1:T(4,128)} %bitcast.23), calls=%async_computation.1 | async-start | bytes 524288 | tf_op jit(solution)/shard_map/all_to_all | solution.py:92
  156.7 12.8 %all-to-all-done.1 = f32[25,128,4]{0,2,1:T(4,128)S(1)} async-done(((f32[25,128,4]{0,2,1:T(4,128)}), f32[25,128,4]{0,2,1:T(4,128)S(1)}, u32[]{:S(2)}, u32[]{:S(2)}) %all-to-all-start.1) | async-done | bytes 51232 | tf_op jit(solution)/shard_map/all_to_all | solution.py:92
  174.8 3.4 collective-permute-start.21
  184.3 3.3 collective-permute-done.22
  188.0 8.4 %collective-permute-start.24 = (f32[25,8,1]{2,1,0:T(8,128)S(1)}, f32[25,8,1]{2,1,0:T(8,128)S(1)}, u32[]{:S(2)}, u32[]{:S(2)}) collective-permute-start(f32[25,8,1]{2,1,0:T(8,128)S(1)} %get-tuple-element.30), channel_id=1, source_target_pairs={{4,0},{8,4},{12,8},{16,12},{20,16},{24,20},{28,24},{32,28},{36,32}... | collective-permute-start | bytes 2408 | tf_op jit(solution)/shard_map/ppermute | solution.py:17
  203.2 3.3 collective-permute-done.26
  206.8 7.9 %collective-permute-start.28 = (f32[25,8,1]{2,1,0:T(8,128)S(1)}, f32[25,8,1]{2,1,0:T(8,128)S(1)}, u32[]{:S(2)}, u32[]{:S(2)}) collective-permute-start(f32[25,8,1]{2,1,0:T(8,128)S(1)} %get-tuple-element.28), channel_id=1, source_target_pairs={{4,0},{8,4},{12,8},{16,12},{20,16},{24,20},{28,24},{32,28},{36,32}... | collective-permute-start | bytes 2408 | tf_op jit(solution)/shard_map/ppermute | solution.py:17
  227.2 99.7 %all-reduce.2 = (f32[]{:T(128)}, f32[]{:T(128)}) all-reduce(f32[]{:T(128)} %multiply_reduce_fusion.2, f32[]{:T(128)} %get-tuple-element.7), channel_id=1, replica_groups=mesh['lat'=8,'lon'=16,'obs'=4] {'lat','lon','obs'}, use_global_device_ids=true, to_apply=%region_1.0 | all-reduce | flops 2 | bytes 16 | tf_op jit(solution)/shard_map/psum | solution.py:103
  328.9 94.2 %psum.31 = f32[]{:T(128)} all-reduce(f32[]{:T(128)} %get-tuple-element.5), channel_id=1, replica_groups=mesh['lat'=8,'lon'=16,'obs'=4] {'lat','lon','obs'}, use_global_device_ids=true, to_apply=%region_11.12 | all-reduce | flops 1 | bytes 8 | tf_op jit(solution)/shard_map/psum | solution.py:109
  (130 shorter events, 65.6 us)
Async XLA Ops:
  0.7 24.6 %collective-permute-start.4 = (f32[25,8,1]{2,1,0:T(8,128)S(1)}, f32[25,8,1]{2,1,0:T(8,128)S(1)}, u32[]{:S(2)}, u32[]{:S(2)}) collective-permute-start(f32[25,8,1]{2,1,0:T(8,128)S(1)} %broadcast.57), channel_id=1, source_target_pairs={{4,0},{8,4},{12,8},{16,12},{20,16},{24,20},{28,24},{32,28},{36,32}... | collective-permute-start | bytes 2408 | tf_op jit(solution)/shard_map/ppermute | solution.py:17
  9.5 15.8 %collective-permute-start.5 = (f32[25,8,1]{2,1,0:T(8,128)S(1)}, f32[25,8,1]{2,1,0:T(8,128)S(1)}, u32[]{:S(2)}, u32[]{:S(2)}) collective-permute-start(f32[25,8,1]{2,1,0:T(8,128)S(1)} %broadcast.57), channel_id=1, source_target_pairs={{0,4},{4,8},{8,12},{12,16},{16,20},{20,24},{24,28},{28,32},{32,36}... | collective-permute-start | bytes 2408 | tf_op jit(solution)/shard_map/ppermute | solution.py:16
  11.5 6.5 %collective-permute-start.1 = (f32[3,8,4]{2,1,0:T(8,128)S(1)}, f32[3,8,4]{2,1,0:T(8,128)S(1)}, u32[]{:S(2)}, u32[]{:S(2)}) collective-permute-start(f32[3,8,4]{2,1,0:T(8,128)S(1)} %get-tuple-element.49), channel_id=1, source_target_pairs={{4,0},{8,4},{12,8},{16,12},{20,16},{24,20},{28,24},{32,28},{36,32}... | collective-permute-start | bytes 1160 | tf_op jit(solution)/shard_map/ppermute | solution.py:17
  13.9 5.9 %collective-permute-start = (f32[3,8,4]{2,1,0:T(8,128)S(1)}, f32[3,8,4]{2,1,0:T(8,128)S(1)}, u32[]{:S(2)}, u32[]{:S(2)}) collective-permute-start(f32[3,8,4]{2,1,0:T(8,128)S(1)} %get-tuple-element.48), channel_id=1, source_target_pairs={{0,4},{4,8},{8,12},{12,16},{16,20},{20,24},{24,28},{28,32},{32,36}... | collective-permute-start | bytes 1160 | tf_op jit(solution)/shard_map/ppermute | solution.py:16
  20.0 9.3 %collective-permute-start.3 = (f32[3,4,136]{2,1,0:T(4,128)S(1)}, f32[3,4,136]{2,1,0:T(4,128)S(1)}, u32[]{:S(2)}, u32[]{:S(2)}) collective-permute-start(f32[3,4,136]{2,1,0:T(4,128)S(1)} %get-tuple-element.42), channel_id=1, source_target_pairs={{64,0},{128,64},{192,128},{256,192},{320,256},{384,320},{448,384},... | collective-permute-start | bytes 19592 | tf_op jit(solution)/shard_map/ppermute | solution.py:17
  21.3 8.1 %collective-permute-start.2 = (f32[3,4,136]{2,1,0:T(4,128)S(1)}, f32[3,4,136]{2,1,0:T(4,128)S(1)}, u32[]{:S(2)}, u32[]{:S(2)}) collective-permute-start(f32[3,4,136]{2,1,0:T(4,128)S(1)} %get-tuple-element.41), channel_id=1, source_target_pairs={{0,64},{64,128},{128,192},{192,256},{256,320},{320,384},{384,448},... | collective-permute-start | bytes 19592 | tf_op jit(solution)/shard_map/ppermute | solution.py:16
  28.0 5.2 %collective-permute-start.6 = (f32[25,1,130]{2,1,0:T(1,128)S(1)}, f32[25,1,130]{2,1,0:T(1,128)S(1)}, u32[]{:S(2)}, u32[]{:S(2)}) collective-permute-start(f32[25,1,130]{2,1,0:T(1,128)S(1)} %get-tuple-element.23), channel_id=1, source_target_pairs={{64,0},{128,64},{192,128},{256,192},{320,256},{384,320},{448,384},... | collective-permute-start | bytes 39008 | tf_op jit(solution)/shard_map/ppermute | solution.py:17
  33.5 9.9 %collective-permute-start.8 = (f32[25,8,1]{2,1,0:T(8,128)S(1)}, f32[25,8,1]{2,1,0:T(8,128)S(1)}, u32[]{:S(2)}, u32[]{:S(2)}) collective-permute-start(f32[25,8,1]{2,1,0:T(8,128)S(1)} %get-tuple-element.38), channel_id=1, source_target_pairs={{4,0},{8,4},{12,8},{16,12},{20,16},{24,20},{28,24},{32,28},{36,32}... | collective-permute-start | bytes 2408 | tf_op jit(solution)/shard_map/ppermute | solution.py:17
  45.3 6.6 %collective-permute-start.11 = (f32[25,1,130]{2,1,0:T(1,128)S(1)}, f32[25,1,130]{2,1,0:T(1,128)S(1)}, u32[]{:S(2)}, u32[]{:S(2)}) collective-permute-start(f32[25,1,130]{2,1,0:T(1,128)S(1)} %get-tuple-element.22), channel_id=1, source_target_pairs={{0,64},{64,128},{128,192},{192,256},{256,320},{320,384},{384,448},... | collective-permute-start | bytes 39008 | tf_op jit(solution)/shard_map/ppermute | solution.py:16
  50.5 4.9 %collective-permute-start.10 = (f32[25,1,130]{2,1,0:T(1,128)S(1)}, f32[25,1,130]{2,1,0:T(1,128)S(1)}, u32[]{:S(2)}, u32[]{:S(2)}) collective-permute-start(f32[25,1,130]{2,1,0:T(1,128)S(1)} %get-tuple-element.21), channel_id=1, source_target_pairs={{64,0},{128,64},{192,128},{256,192},{320,256},{384,320},{448,384},... | collective-permute-start | bytes 39008 | tf_op jit(solution)/shard_map/ppermute | solution.py:17
  55.7 9.7 %collective-permute-start.12 = (f32[25,8,1]{2,1,0:T(8,128)S(1)}, f32[25,8,1]{2,1,0:T(8,128)S(1)}, u32[]{:S(2)}, u32[]{:S(2)}) collective-permute-start(f32[25,8,1]{2,1,0:T(8,128)S(1)} %get-tuple-element.36), channel_id=1, source_target_pairs={{4,0},{8,4},{12,8},{16,12},{20,16},{24,20},{28,24},{32,28},{36,32}... | collective-permute-start | bytes 2408 | tf_op jit(solution)/shard_map/ppermute | solution.py:17
  67.1 6.2 %collective-permute-start.15 = (f32[25,1,130]{2,1,0:T(1,128)S(1)}, f32[25,1,130]{2,1,0:T(1,128)S(1)}, u32[]{:S(2)}, u32[]{:S(2)}) collective-permute-start(f32[25,1,130]{2,1,0:T(1,128)S(1)} %get-tuple-element.20), channel_id=1, source_target_pairs={{0,64},{64,128},{128,192},{192,256},{256,320},{320,384},{384,448},... | collective-permute-start | bytes 39008 | tf_op jit(solution)/shard_map/ppermute | solution.py:16
  72.0 4.9 %collective-permute-start.14 = (f32[25,1,130]{2,1,0:T(1,128)S(1)}, f32[25,1,130]{2,1,0:T(1,128)S(1)}, u32[]{:S(2)}, u32[]{:S(2)}) collective-permute-start(f32[25,1,130]{2,1,0:T(1,128)S(1)} %get-tuple-element.19), channel_id=1, source_target_pairs={{64,0},{128,64},{192,128},{256,192},{320,256},{384,320},{448,384},... | collective-permute-start | bytes 39008 | tf_op jit(solution)/shard_map/ppermute | solution.py:17
  77.2 9.5 %collective-permute-start.16 = (f32[25,8,1]{2,1,0:T(8,128)S(1)}, f32[25,8,1]{2,1,0:T(8,128)S(1)}, u32[]{:S(2)}, u32[]{:S(2)}) collective-permute-start(f32[25,8,1]{2,1,0:T(8,128)S(1)} %get-tuple-element.34), channel_id=1, source_target_pairs={{4,0},{8,4},{12,8},{16,12},{20,16},{24,20},{28,24},{32,28},{36,32}... | collective-permute-start | bytes 2408 | tf_op jit(solution)/shard_map/ppermute | solution.py:17
  88.6 5.1 %collective-permute-start.19 = (f32[25,1,130]{2,1,0:T(1,128)S(1)}, f32[25,1,130]{2,1,0:T(1,128)S(1)}, u32[]{:S(2)}, u32[]{:S(2)}) collective-permute-start(f32[25,1,130]{2,1,0:T(1,128)S(1)} %get-tuple-element.18), channel_id=1, source_target_pairs={{0,64},{64,128},{128,192},{192,256},{256,320},{320,384},{384,448},... | collective-permute-start | bytes 39008 | tf_op jit(solution)/shard_map/ppermute | solution.py:16
  92.2 4.6 %collective-permute-start.18 = (f32[25,1,130]{2,1,0:T(1,128)S(1)}, f32[25,1,130]{2,1,0:T(1,128)S(1)}, u32[]{:S(2)}, u32[]{:S(2)}) collective-permute-start(f32[25,1,130]{2,1,0:T(1,128)S(1)} %get-tuple-element.17), channel_id=1, source_target_pairs={{64,0},{128,64},{192,128},{256,192},{320,256},{384,320},{448,384},... | collective-permute-start | bytes 39008 | tf_op jit(solution)/shard_map/ppermute | solution.py:17
  147.2 22.3 %all-to-all-start.1 = ((f32[25,128,4]{0,2,1:T(4,128)}), f32[25,128,4]{0,2,1:T(4,128)S(1)}, u32[]{:S(2)}, u32[]{:S(2)}) async-start(f32[25,128,4]{0,2,1:T(4,128)} %bitcast.23), calls=%async_computation.1 | async-start | bytes 524288 | tf_op jit(solution)/shard_map/all_to_all | solution.py:92
  172.5 6.0 %collective-permute-start.20 = (f32[25,8,1]{2,1,0:T(8,128)S(1)}, f32[25,8,1]{2,1,0:T(8,128)S(1)}, u32[]{:S(2)}, u32[]{:S(2)}) collective-permute-start(f32[25,8,1]{2,1,0:T(8,128)S(1)} %get-tuple-element.32), channel_id=1, source_target_pairs={{4,0},{8,4},{12,8},{16,12},{20,16},{24,20},{28,24},{32,28},{36,32}... | collective-permute-start | bytes 2408 | tf_op jit(solution)/shard_map/ppermute | solution.py:17
  174.8 5.2 %collective-permute-start.21 = (f32[25,8,1]{2,1,0:T(8,128)S(1)}, f32[25,8,1]{2,1,0:T(8,128)S(1)}, u32[]{:S(2)}, u32[]{:S(2)}) collective-permute-start(f32[25,8,1]{2,1,0:T(8,128)S(1)} %get-tuple-element.31), channel_id=1, source_target_pairs={{0,4},{4,8},{8,12},{12,16},{16,20},{20,24},{24,28},{28,32},{32,36}... | collective-permute-start | bytes 2408 | tf_op jit(solution)/shard_map/ppermute | solution.py:16
  183.0 4.6 %collective-permute-start.22 = (f32[25,1,130]{2,1,0:T(1,128)S(1)}, f32[25,1,130]{2,1,0:T(1,128)S(1)}, u32[]{:S(2)}, u32[]{:S(2)}) collective-permute-start(f32[25,1,130]{2,1,0:T(1,128)S(1)} %get-tuple-element.15), channel_id=1, source_target_pairs={{64,0},{128,64},{192,128},{256,192},{320,256},{384,320},{448,384},... | collective-permute-start | bytes 39008 | tf_op jit(solution)/shard_map/ppermute | solution.py:17
  188.0 10.3 %collective-permute-start.24 = (f32[25,8,1]{2,1,0:T(8,128)S(1)}, f32[25,8,1]{2,1,0:T(8,128)S(1)}, u32[]{:S(2)}, u32[]{:S(2)}) collective-permute-start(f32[25,8,1]{2,1,0:T(8,128)S(1)} %get-tuple-element.30), channel_id=1, source_target_pairs={{4,0},{8,4},{12,8},{16,12},{20,16},{24,20},{28,24},{32,28},{36,32}... | collective-permute-start | bytes 2408 | tf_op jit(solution)/shard_map/ppermute | solution.py:17
  206.8 9.9 %collective-permute-start.28 = (f32[25,8,1]{2,1,0:T(8,128)S(1)}, f32[25,8,1]{2,1,0:T(8,128)S(1)}, u32[]{:S(2)}, u32[]{:S(2)}) collective-permute-start(f32[25,8,1]{2,1,0:T(8,128)S(1)} %get-tuple-element.28), channel_id=1, source_target_pairs={{4,0},{8,4},{12,8},{16,12},{20,16},{24,20},{28,24},{32,28},{36,32}... | collective-permute-start | bytes 2408 | tf_op jit(solution)/shard_map/ppermute | solution.py:17
  218.7 4.8 %collective-permute-start.31 = (f32[25,1,130]{2,1,0:T(1,128)S(1)}, f32[25,1,130]{2,1,0:T(1,128)S(1)}, u32[]{:S(2)}, u32[]{:S(2)}) collective-permute-start(f32[25,1,130]{2,1,0:T(1,128)S(1)} %get-tuple-element.12), channel_id=1, source_target_pairs={{0,64},{64,128},{128,192},{192,256},{256,320},{320,384},{384,448},... | collective-permute-start | bytes 39008 | tf_op jit(solution)/shard_map/ppermute | solution.py:16
  221.5 4.9 %collective-permute-start.30 = (f32[25,1,130]{2,1,0:T(1,128)S(1)}, f32[25,1,130]{2,1,0:T(1,128)S(1)}, u32[]{:S(2)}, u32[]{:S(2)}) collective-permute-start(f32[25,1,130]{2,1,0:T(1,128)S(1)} %get-tuple-element.11), channel_id=1, source_target_pairs={{64,0},{128,64},{192,128},{256,192},{320,256},{384,320},{448,384},... | collective-permute-start | bytes 39008 | tf_op jit(solution)/shard_map/ppermute | solution.py:17
  (23 other events, 320.2 us)
where the time goes:
time: 427 us; the launch traced here: 425 us
  blocking collectives  241 us (56%)
  starting transfers between devices  118 us (28%)
  waiting for transfers between devices  47.6 us (11%)
  other arithmetic  11.4 us (3%)
    psum x1, blocking collectives, local(): lax.psum((jnp.sum(residual * residual), jnp.sum(direction * image)), ('la...  99.7 us
    psum x1, blocking collectives, local(): lax.psum(jnp.sum(residual_next * residual_next), ('lat', 'lon', 'obs'))  94.2 us
    ppermute x16, starting transfers between devices, padded_2(): after = lax.ppermute(initial, axis, down)  63.1 us
    ppermute x16, starting transfers between devices, padded_2(): before = lax.ppermute(last, axis, up)  45.7 us
    all_to_all x1, blocking collectives, local(): lax.all_to_all(outgoing, ('lat', 'lon'), split_axis=1, concat_axis=1, til...  24.2 us
    ppermute x16, waiting for transfers between devices, padded_2(): after = lax.ppermute(initial, axis, down)  23.5 us
    psum x1, blocking collectives, local(): full_column = lax.psum(received, 'obs')  22.5 us
    all_to_all x1, waiting for transfers between devices, local(): lax.all_to_all(weighted_all, ('lat', 'lon'), split_axis=1, concat_axis=1,...  12.8 us
  transfers between devices with their start and end apart: 33, of which 16 were waited for; matrix products, arithmetic and copies ran while one was open for 0% of the time, Pallas kernels for 0%

commit v1 on v0

v1 whole, which is shorter than its diff:
```python
import functools

import jax
import jax.numpy as jnp
from jax import lax
from jax.experimental import pallas as pl
from jax.experimental.pallas import tpu as pltpu
from jax.sharding import PartitionSpec as P

LEV = 25
PADLEV = 32
ROWS = 8
COLS = 128
SLOTS = 256
SHIFT = 4
SWEEPS = 4
GROUP = 5

M_FLAG, M_EAST, M_NORTH, M_SIGMA, M_WEIGHT, M_PLACE, M_TILES = 25, 26, 27, 28, 29, 37, 38
LIMIT = 48 * 1024 * 1024


def shifted(x, by, axis):
    return pltpu.roll(x, by % x.shape[axis], axis)


def split(x, parts):
    out = []
    for _ in range(parts):
        part = x.astype(jnp.bfloat16)
        out.append(part)
        x = x - part.astype(jnp.float32)
    return out


def frame(refs, tile):
    low = jnp.concatenate([refs[0][tile], refs[1][tile]], axis=-1)
    high = jnp.concatenate([refs[2][tile], refs[3][tile]], axis=-1)
    return jnp.concatenate([low, high], axis=-2)


def scaled_faces(ke, kn):
    kw = shifted(ke, 1, 1)
    ks = shifted(kn, 1, 0)
    inverse = 1.0 / (1.0 + ke + kw + kn + ks)
    return inverse, ke * inverse, kw * inverse, kn * inverse, ks * inverse


def diffuse(source, scaled):
    inverse, ke, kw, kn, ks = [term[None] for term in scaled]
    scaled_source = source * inverse
    x = scaled_source
    for _ in range(SWEEPS - 1):
        x = (
            scaled_source
            + ke * shifted(x, -1, 2)
            + kw * shifted(x, 1, 2)
            + kn * shifted(x, -1, 1)
            + ks * shifted(x, 1, 1)
        )
    return x


def south_west(x):
    axis = x.ndim - 2
    x = shifted(shifted(x, SHIFT, axis + 1), SHIFT, axis)
    return x[..., ROWS:, COLS:]


def north_east(x):
    axis = x.ndim - 2
    x = shifted(shifted(x, -SHIFT, axis + 1), -SHIFT, axis)
    return x[..., :ROWS, :COLS]


def place_rows(refs, half):
    picked = []
    for west in (0, 1):
        ref = refs[2 * half + (1 - west)]
        cell = ref[M_PLACE, 0:2, :].astype(jnp.int32)
        row, col = cell // COLS, cell % COLS
        if half == 1:
            inside = row < ROWS - SHIFT
        else:
            inside = row >= SHIFT
            row = row - SHIFT
        if west:
            inside = inside & (col >= COLS - SHIFT)
            col = col - (COLS - SHIFT)
        else:
            inside = inside & (col < COLS - SHIFT)
            col = col + SHIFT
        place = jnp.where(inside, row * COLS + col, -1)
        picked += [place[0:1], place[1:2]]
    return jnp.concatenate(picked, axis=1)


def weights_of(refs, half):
    picked = []
    for west in (0, 1):
        ref = refs[2 * half + (1 - west)]
        for part in (0, 1):
            first = M_WEIGHT + 4 * part
            picked.append(ref[first : first + 4].reshape(PADLEV, COLS))
    return jnp.concatenate(picked, axis=1)


def owners_of(refs, half):
    picked = []
    for west in (0, 1):
        ref = refs[2 * half + (1 - west)]
        owner = ref[M_PLACE, 2:4, :].astype(jnp.int32)
        picked += [owner[0:1], owner[1:2]]
    return jnp.concatenate(picked, axis=1)


def one_hot(index, length):
    rows = lax.broadcasted_iota(jnp.int32, (length, index.shape[1]), 0)
    return jnp.where(rows == index, 1.0, 0.0).astype(jnp.bfloat16)


def pack_kernel(d, flag, east, north, sigma, weight, cell, owner, table, msg, tables, wide):
    msg[0:LEV] = d[...]
    msg[M_FLAG] = flag[...].astype(jnp.float32)
    msg[M_EAST] = east[...]
    msg[M_NORTH] = north[...]
    msg[M_SIGMA] = sigma[...]
    for part in (0, 1):
        first = M_WEIGHT + 4 * part
        columns = slice(part * COLS, (part + 1) * COLS)
        for i in range(3):
            msg[first + i] = weight[8 * i : 8 * i + 8, columns]
        msg[first + 3] = jnp.zeros((ROWS, COLS), jnp.float32)
        msg[first + 3, 0:1, :] = weight[24:25, columns]
    msg[M_PLACE] = jnp.zeros((ROWS, COLS), jnp.float32)
    msg[M_PLACE, 0:2, :] = cell[...].astype(jnp.float32)
    msg[M_PLACE, 2:4, :] = owner[...].astype(jnp.float32)
    wide[...] = jnp.zeros_like(wide)
    wide[0:LEV, 0:LEV] = table[...]
    tile = jnp.zeros((ROWS, COLS), jnp.float32)
    for q in range(4):
        tile = tile + shifted(wide[pl.ds(q, 8, stride=4), :], 32 * q, 1)
    tables[...] = jnp.broadcast_to(tile[None], tables.shape)


def pick_kernel(sw, s, w, o, part, aux, held):
    refs = (sw, s, w, o)
    flag = frame(refs, M_FLAG)
    ke = frame(refs, M_EAST) * flag * shifted(flag, -1, 1)
    kn = frame(refs, M_NORTH) * flag * shifted(flag, -1, 0)
    row = lax.broadcasted_iota(jnp.int32, kn.shape, 0)
    edge = (row == ROWS - 1) & (lax.axis_index("lat") == 0)
    kn = jnp.where(edge, 0.0, kn)
    spread = frame(refs, M_SIGMA) * flag
    aux[0] = south_west(spread)
    aux[1] = south_west(ke)
    aux[2] = south_west(kn)
    scaled = scaled_faces(ke, kn)
    spread_here = aux[0]
    held[LEV * ROWS :, :] = jnp.zeros((held.shape[0] - LEV * ROWS, COLS), jnp.float32)
    for g in range(LEV // GROUP):
        source = frame(refs, slice(g * GROUP, (g + 1) * GROUP))
        x = south_west(diffuse(source, scaled)) * spread_here[None]
        held[g * GROUP * ROWS : (g + 1) * GROUP * ROWS, :] = x.reshape(GROUP * ROWS, COLS)
    for half in (1, 0):
        first = SHIFT * half
        state = jnp.concatenate(
            [held[pl.ds(first + r, PADLEV, stride=ROWS), :] for r in range(SHIFT)], axis=1
        )
        hot = one_hot(place_rows(refs, half), SHIFT * COLS)
        stacked = jnp.concatenate(split(state, 3), axis=0)
        got = jnp.dot(stacked, hot, preferred_element_type=jnp.float32)
        got = got[0:PADLEV] + got[PADLEV : 2 * PADLEV] + got[2 * PADLEV :]
        got = got * weights_of(refs, half)
        for c in range(4):
            at = (4 * half + c) * LEV
            part[at : at + LEV, :] = got[0:LEV, c * COLS : (c + 1) * COLS]


def spread_kernel(fields, owners, sw, s, w, o, parts, tables, aux, out, column, held):
    refs = (sw, s, w, o)
    chunk = LEV * ROWS
    total = parts[0:chunk, :]
    for f in range(1, fields):
        total = total + parts[f * chunk : (f + 1) * chunk, :]
    column[...] = total
    turned = []
    for r in range(7):
        turned.append(jnp.transpose(tables[pl.ds(r, owners, stride=ROWS), :]))
    turned = jnp.concatenate(turned, axis=0)
    turned = jnp.concatenate(split(turned, 2), axis=1)
    for half in (1, 0):
        owner = owners_of(refs, half)
        pieces = []
        for n in (0, 1):
            hot = one_hot(owner[:, n * SLOTS : (n + 1) * SLOTS], owners)
            hot = jnp.concatenate([hot, hot], axis=0)
            rows = jnp.dot(turned, hot, preferred_element_type=jnp.float32)
            sums = jnp.zeros((PADLEV, SLOTS), jnp.float32)
            for m in range(LEV):
                at = (4 * half + 2 * n) * LEV + m
                value = jnp.concatenate(
                    [column[at : at + 1, :], column[at + LEV : at + LEV + 1, :]], axis=1
                )
                sums = sums + rows[m * PADLEV : (m + 1) * PADLEV] * value
            pieces.append(sums)
        weighted = jnp.concatenate(pieces, axis=1) * weights_of(refs, half)
        hot = one_hot(place_rows(refs, half), SHIFT * COLS)
        stacked = jnp.concatenate(split(weighted, 3), axis=0)
        got = lax.dot_general(
            stacked, hot, (((1,), (1,)), ((), ())), preferred_element_type=jnp.float32
        )
        got = got[0:PADLEV] + got[PADLEV : 2 * PADLEV] + got[2 * PADLEV :]
        for r in range(SHIFT):
            held[pl.ds(SHIFT * half + r, PADLEV, stride=ROWS), :] = got[:, r * COLS : (r + 1) * COLS]
    out[0:LEV] = held[0 : LEV * ROWS, :].reshape(LEV, ROWS, COLS) * aux[0][None]
    out[LEV] = aux[1]
    out[LEV + 1] = aux[2]


def image_kernel(o, e, n, ne, d, res, image, sums):
    refs = (o, e, n, ne)
    scaled = scaled_faces(frame(refs, LEV), frame(refs, LEV + 1))
    zero = jnp.zeros((ROWS, COLS), jnp.float32)
    norm, curve, cross, square = zero, zero, zero, zero
    for g in range(LEV // GROUP):
        levels = slice(g * GROUP, (g + 1) * GROUP)
        here = d[levels]
        old = res[levels]
        x = here + north_east(diffuse(frame(refs, levels), scaled))
        image[levels] = x
        norm = norm + jnp.sum(old * old, axis=0)
        curve = curve + jnp.sum(here * x, axis=0)
        cross = cross + jnp.sum(old * x, axis=0)
        square = square + jnp.sum(x * x, axis=0)
    lane = lax.broadcasted_iota(jnp.int32, (1, COLS), 1)
    line = jnp.zeros((1, COLS), jnp.float32)
    for i, value in enumerate((norm, curve, cross, square)):
        line = jnp.where(lane == i, jnp.sum(value), line)
    sums[...] = jnp.broadcast_to(line, sums.shape)


def sum_kernel(given, out):
    out[...] = jnp.broadcast_to(jnp.sum(given[...], axis=0, keepdims=True), out.shape)


def step_kernel(given, control, res, d, image, control_next, res_next, d_next):
    line = jnp.sum(given[...], axis=0, keepdims=True)
    norm, curve, cross, square = line[:, 0:1], line[:, 1:2], line[:, 2:3], line[:, 3:4]
    alpha = norm / curve
    norm_next = jnp.maximum(norm - 2.0 * alpha * cross + alpha * alpha * square, 0.0)
    beta = norm_next / norm
    alpha = jnp.broadcast_to(alpha, (ROWS, COLS))[None]
    beta = jnp.broadcast_to(beta, (ROWS, COLS))[None]
    here = d[...]
    control_next[...] = control[...] + alpha * here
    new = res[...] - alpha * image[...]
    res_next[...] = new
    d_next[...] = new + beta * here


def call(kernel, outs, scratch=(), flops=1000000):
    whole = pl.BlockSpec(memory_space=pltpu.VMEM)
    return lambda *given: pl.pallas_call(
        kernel,
        out_shape=tuple(jax.ShapeDtypeStruct(shape, jnp.float32) for shape in outs),
        in_specs=[whole] * len(given),
        out_specs=tuple([whole] * len(outs)),
        scratch_shapes=[pltpu.VMEM(shape, jnp.float32) for shape in scratch],
        compiler_params=pltpu.CompilerParams(vmem_limit_bytes=LIMIT),
        cost_estimate=pl.CostEstimate(flops=flops, bytes_accessed=1000000, transcendentals=0),
    )(*given)


def neighbours(x, sign):
    lats, lons = lax.axis_size("lat"), lax.axis_size("lon")
    along_lat = lax.ppermute(x, "lat", [(i, (i + sign) % lats) for i in range(lats)])
    along_lon = lax.ppermute(x, "lon", [(i, (i + sign) % lons) for i in range(lons)])
    both = [
        (i * lons + j, (i + sign) % lats * lons + (j + sign) % lons)
        for i in range(lats)
        for j in range(lons)
    ]
    return along_lat, along_lon, lax.ppermute(x, ("lat", "lon"), both)


def local(
    control,
    residual,
    direction,
    land_mask,
    kappa_east,
    kappa_north,
    sigma,
    obs_weight,
    obs_cell,
    obs_owner,
    error_inverse,
):
    lats, lons, fields = lax.axis_size("lat"), lax.axis_size("lon"), lax.axis_size("obs")
    owners = lats * lons
    block = (LEV, ROWS, COLS)
    d = direction.reshape(block)
    res = residual.reshape(block)
    msg, tables = call(
        pack_kernel,
        ((M_TILES, ROWS, COLS), (owners, ROWS, COLS)),
        ((PADLEV, COLS),),
    )(
        d,
        land_mask,
        kappa_east,
        kappa_north,
        sigma.reshape(ROWS, COLS),
        obs_weight.reshape(LEV, SLOTS),
        obs_cell.reshape(2, COLS),
        obs_owner.reshape(2, COLS),
        error_inverse.reshape(LEV, LEV),
    )
    tables = lax.all_to_all(tables, ("lat", "lon"), 0, 0, tiled=True)
    south, west, both = neighbours(msg, 1)
    part, aux = call(
        pick_kernel,
        ((LEV * ROWS, COLS), (3, ROWS, COLS)),
        ((PADLEV * ROWS, COLS),),
    )(both, south, west, msg)
    parts = lax.all_gather(part, "obs", tiled=True)
    (source,) = call(
        functools.partial(spread_kernel, fields, owners),
        ((LEV + 2, ROWS, COLS),),
        ((LEV * ROWS, COLS), (PADLEV * ROWS, COLS)),
    )(both, south, west, msg, parts, tables.reshape(owners * ROWS, COLS), aux)
    north, east, both = neighbours(source, -1)
    image, sums = call(image_kernel, (block, (fields * lons, COLS)))(
        source, east, north, both, d, res
    )
    sums = lax.all_to_all(sums, ("obs", "lon"), 0, 0, tiled=True)
    (sums,) = call(sum_kernel, ((lats, COLS),))(sums)
    sums = lax.all_to_all(sums, "lat", 0, 0, tiled=True)
    outs = call(step_kernel, (block, block, block))(
        sums, control.reshape(block), res, d, image
    )
    return tuple(out.reshape(direction.shape) for out in outs)


def solution(mesh):
    state = P("obs", None, "lat", "lon")
    placed = (
        state,
        state,
        state,
        P("lat", "lon"),
        P("lat", "lon"),
        P("lat", "lon"),
        P("obs", "lat", "lon"),
        P("obs", None, ("lat", "lon")),
        P(("lat", "lon")),
        P(("lat", "lon"), None),
        P(("lat", "lon"), None, None),
    )
    return jax.shard_map(
        local, mesh=mesh, in_specs=placed, out_specs=(state, state, state), check_vma=False
    )
```

time: 427 us -> 105 us (0.25)
  blocking collectives: 241 us -> 44.6 us
  starting transfers between devices: 118 us -> 38.8 us
  waiting for transfers between devices: 47.6 us -> 12.4 us
  other arithmetic: 11.4 us -> 0 us
  Pallas kernels: 0 us -> 5.81 us
    psum x3 -> x0, blocking collectives: 216 us -> none  [the longest x1 99.7 us: local(): lax.psum((jnp.sum(residual * residual), jnp.sum(direction * image)), ('la...]
    ppermute x32 -> x6, starting transfers between devices: 109 us -> 22.2 us  [the longest x2 8.94 us: neighbours(): lax.ppermute(x, 'lon', [(i, (i + sign) % lons) for i in range(lons)])]
    ppermute x32 -> x6, waiting for transfers between devices: 34.9 us -> 12.4 us  [the longest x2 7.91 us: neighbours(): lax.ppermute(x, 'lat', [(i, (i + sign) % lats) for i in range(lats)])]
    all_gather x0 -> x1, blocking collectives: none -> 14.2 us  [local(): parts = lax.all_gather(part, 'obs', tiled=True)]
    all_to_all x1, waiting for transfers between devices: 12.8 us -> 0.01 us  [local(): tables = lax.all_to_all(tables, ('lat', 'lon'), 0, 0, tiled=True)]
    all_to_all x1, starting transfers between devices: 9.47 us -> 16.6 us  [local(): tables = lax.all_to_all(tables, ('lat', 'lon'), 0, 0, tiled=True)]
    all_to_all x1 -> x2, blocking collectives: 24.2 us -> 30.4 us  [the longest x1 21.5 us: local(): sums = lax.all_to_all(sums, ('obs', 'lon'), 0, 0, tiled=True)]
    pallas_call x0 -> x6, Pallas kernels: none -> 5.81 us  [call(): pl.pallas_call(kernel, out_shape=tuple((jax.ShapeDtypeStruct(shape, jnp.f...]
  transfers between devices with their start and end apart: 33 -> 7, of which waited for: 16 -> 3; matrix products, arithmetic and copies ran while one was open for 0% -> 0% of each run, Pallas kernels for 0% -> 1%
where the time goes in v1:
time: 105 us
  blocking collectives  44.6 us (42%)
  starting transfers between devices  38.8 us (37%)
  waiting for transfers between devices  12.4 us (12%)
  Pallas kernels  5.81 us (6%)
  local copies, waits for them, and re-layouts  2.36 us (2%)
    all_to_all x1, blocking collectives, local(): sums = lax.all_to_all(sums, ('obs', 'lon'), 0, 0, tiled=True)  21.5 us
    all_to_all x1, starting transfers between devices, local(): tables = lax.all_to_all(tables, ('lat', 'lon'), 0, 0, tiled=True)  16.6 us
    all_gather x1, blocking collectives, local(): parts = lax.all_gather(part, 'obs', tiled=True)  14.2 us
    ppermute x2, starting transfers between devices, neighbours(): lax.ppermute(x, 'lon', [(i, (i + sign) % lons) for i in range(lons)])  8.94 us
    all_to_all x1, blocking collectives, local(): sums = lax.all_to_all(sums, 'lat', 0, 0, tiled=True)  8.89 us
    ppermute x2, waiting for transfers between devices, neighbours(): lax.ppermute(x, 'lat', [(i, (i + sign) % lats) for i in range(lats)])  7.91 us
    ppermute x2, starting transfers between devices, neighbours(): return (along_lat, along_lon, lax.ppermute(x, ('lat', 'lon'), both))  7.15 us
    ppermute x2, starting transfers between devices, neighbours(): lax.ppermute(x, 'lat', [(i, (i + sign) % lats) for i in range(lats)])  6.08 us
  transfers between devices with their start and end apart: 7, of which 3 were waited for; matrix products, arithmetic and copies ran while one was open for 0% of the time, Pallas kernels for 1%

profile of v1, /device:TPU:1, one launch (start us, length us, event | category | flops | bytes accessed | tf_op | source)
XLA Modules:
  0.0 104.7 jit_solution(1742272199157671012)
XLA Ops:
  0.6 0.7 copy.21
  1.4 0.6 copy-done.6
  2.1 0.0 copy-done.7
  2.1 0.0 copy-done.5
  2.1 0.0 copy-done.4
  2.1 0.9 copy-done
  3.0 0.9 shard_map.130
  3.9 16.6 %all-to-all-start = ((f32[128,8,128]{2,1,0:T(8,128)}), f32[128,8,128]{2,1,0:T(8,128)S(1)}, u32[]{:S(2)}, u32[]{:S(2)}) async-start(f32[128,8,128]{2,1,0:T(8,128)} %get-tuple-element.14), calls=%async_computation | async-start | bytes 1048576 | tf_op jit(solution)/shard_map/all_to_all | solution.py:320
  20.6 3.5 %collective-permute-start.2 = (f32[38,8,128]{2,1,0:T(8,128)S(1)}, f32[38,8,128]{2,1,0:T(8,128)S(1)}, u32[]{:S(2)}, u32[]{:S(2)}) collective-permute-start(f32[38,8,128]{2,1,0:T(8,128)S(1)} %get-tuple-element.12.o), channel_id=1, source_target_pairs={{0,4},{4,8},{8,12},{12,16},{16,20},{20,24},{24,28},{28,32},{32,36}... | collective-permute-start | bytes 466952 | tf_op jit(solution)/shard_map/ppermute | solution.py:278
  24.1 3.1 %collective-permute-start.1 = (f32[38,8,128]{2,1,0:T(8,128)S(1)}, f32[38,8,128]{2,1,0:T(8,128)S(1)}, u32[]{:S(2)}, u32[]{:S(2)}) collective-permute-start(f32[38,8,128]{2,1,0:T(8,128)S(1)} %get-tuple-element.12.o), channel_id=1, source_target_pairs={{0,64},{64,128},{128,192},{192,256},{256,320},{320,384},{384,448},... | collective-permute-start | bytes 466952 | tf_op jit(solution)/shard_map/ppermute | solution.py:277
  27.2 3.3 %collective-permute-start = (f32[38,8,128]{2,1,0:T(8,128)S(1)}, f32[38,8,128]{2,1,0:T(8,128)S(1)}, u32[]{:S(2)}, u32[]{:S(2)}) collective-permute-start(f32[38,8,128]{2,1,0:T(8,128)S(1)} %get-tuple-element.12.o), channel_id=1, source_target_pairs={{0,68},{4,72},{8,76},{12,80},{16,84},{20,88},{24,92},{28,96},{32,1... | collective-permute-start | bytes 466952 | tf_op jit(solution)/shard_map/ppermute | solution.py:284
  30.6 7.9 %collective-permute-done.1.s = f32[38,8,128]{2,1,0:T(8,128)S(1)} collective-permute-done((f32[38,8,128]{2,1,0:T(8,128)S(1)}, f32[38,8,128]{2,1,0:T(8,128)S(1)}, u32[]{:S(2)}, u32[]{:S(2)}) %collective-permute-start.1) | collective-permute-done | bytes 155680 | tf_op jit(solution)/shard_map/ppermute | solution.py:277
  38.5 3.5 %collective-permute-done.sw = f32[38,8,128]{2,1,0:T(8,128)S(1)} collective-permute-done((f32[38,8,128]{2,1,0:T(8,128)S(1)}, f32[38,8,128]{2,1,0:T(8,128)S(1)}, u32[]{:S(2)}, u32[]{:S(2)}) %collective-permute-start) | collective-permute-done | bytes 155680 | tf_op jit(solution)/shard_map/ppermute | solution.py:284
  42.0 1.4 %shard_map.131 = (f32[200,128]{1,0:T(8,128)S(1)}, f32[3,8,128]{2,1,0:T(8,128)S(1)}) custom-call(f32[38,8,128]{2,1,0:T(8,128)S(1)} %collective-permute-done.sw, f32[38,8,128]{2,1,0:T(8,128)S(1)} %collective-permute-done.1.s, f32[38,8,128]{2,1,0:T(8,128)S(1)} %collective-permute-done.2.w, f32[38,8,128]{2,1,0:T(8,128)S(1)} %get-tuple-element.12.o), custom_call_target="tpu_custom_call" | custom-call | flops 1000000 | bytes 1000000 | tf_op jit(solution)/shard_map/pallas_call | solution.py:264
  43.5 14.2 %all_gather.3.parts = f32[800,128]{1,0:T(8,128)S(1)} all-gather(f32[200,128]{1,0:T(8,128)S(1)} %get-tuple-element.13), channel_id=1, replica_groups=mesh['lat'=8,'lon'=16,'obs'=4] {'obs'}, dimensions={0}, use_global_device_ids=true | all-gather | bytes 512000 | tf_op jit(solution)/shard_map/all_gather | solution.py:327
  57.7 1.1 %shard_map.132.o = f32[27,8,128]{2,1,0:T(8,128)S(1)} custom-call(f32[38,8,128]{2,1,0:T(8,128)S(1)} %collective-permute-done.sw, f32[38,8,128]{2,1,0:T(8,128)S(1)} %collective-permute-done.1.s, f32[38,8,128]{2,1,0:T(8,128)S(1)} %collective-permute-done.2.w, f32[38,8,128]{2,1,0:T(8,128)S(1)} %get-tuple-element.12.o, f32[800,128]{1,0:T(8,128)S(1)} %all_gather.3.parts, ...), custom_call_target="tpu_custom_call" | custom-call | flops 1000000 | bytes 1000000 | tf_op jit(solution)/shard_map/pallas_call | solution.py:264
  58.8 3.8 %collective-permute-start.5 = (f32[27,8,128]{2,1,0:T(8,128)S(1)}, f32[27,8,128]{2,1,0:T(8,128)S(1)}, u32[]{:S(2)}, u32[]{:S(2)}) collective-permute-start(f32[27,8,128]{2,1,0:T(8,128)S(1)} %shard_map.132.o), channel_id=1, source_target_pairs={{0,508},{4,448},{8,452},{12,456},{16,460},{20,464},{24,468},{28,47... | collective-permute-start | bytes 331784 | tf_op jit(solution)/shard_map/ppermute | solution.py:284
  62.6 3.0 %collective-permute-start.4 = (f32[27,8,128]{2,1,0:T(8,128)S(1)}, f32[27,8,128]{2,1,0:T(8,128)S(1)}, u32[]{:S(2)}, u32[]{:S(2)}) collective-permute-start(f32[27,8,128]{2,1,0:T(8,128)S(1)} %shard_map.132.o), channel_id=1, source_target_pairs={{0,448},{64,0},{128,64},{192,128},{256,192},{320,256},{384,320},{4... | collective-permute-start | bytes 331784 | tf_op jit(solution)/shard_map/ppermute | solution.py:277
  65.6 5.4 %collective-permute-start.3 = (f32[27,8,128]{2,1,0:T(8,128)S(1)}, f32[27,8,128]{2,1,0:T(8,128)S(1)}, u32[]{:S(2)}, u32[]{:S(2)}) collective-permute-start(f32[27,8,128]{2,1,0:T(8,128)S(1)} %shard_map.132.o), channel_id=1, source_target_pairs={{0,60},{4,0},{8,4},{12,8},{16,12},{20,16},{24,20},{28,24},{32,28},... | collective-permute-start | bytes 331784 | tf_op jit(solution)/shard_map/ppermute | solution.py:278
  71.1 0.9 collective-permute-done.3.e
  72.0 1.5 %shard_map.133 = (f32[25,8,128]{2,1,0:T(8,128)S(1)}, f32[64,128]{1,0:T(8,128)S(1)}) custom-call(f32[27,8,128]{2,1,0:T(8,128)S(1)} %shard_map.132.o, f32[27,8,128]{2,1,0:T(8,128)S(1)} %collective-permute-done.3.e, f32[27,8,128]{2,1,0:T(8,128)S(1)} %collective-permute-done.4.n, f32[27,8,128]{2,1,0:T(8,128)S(1)} %collective-permute-done.5.ne, ...), custom_call_target="tpu_custom_call" | custom-call | flops 1000000 | bytes 1000000 | tf_op jit(solution)/shard_map/pallas_call | solution.py:264
  73.5 21.5 %all_to_all.27 = f32[64,1,128]{2,1,0:T(1,128)S(1)} all-to-all(f32[64,1,128]{2,1,0:T(1,128)S(1)} %bitcast.34), channel_id=1, replica_groups=mesh['lat'=8,'lon'=16,'obs'=4] {'obs','lon'}, dimensions={0} | all-to-all | bytes 65536 | tf_op jit(solution)/shard_map/all_to_all | solution.py:337
  95.0 8.9 %all_to_all.28 = f32[8,1,128]{2,1,0:T(1,128)S(1)} all-to-all(f32[8,1,128]{2,1,0:T(1,128)S(1)} %bitcast.36), channel_id=1, replica_groups=mesh['lat'=8,'lon'=16,'obs'=4] {'lat'}, dimensions={0} | all-to-all | bytes 8192 | tf_op jit(solution)/shard_map/all_to_all | solution.py:339
  103.9 0.8 shard_map.135
  (23 shorter events, 0.1 us)
Async XLA Ops:
  0.6 0.7 copy-start.10
  1.4 0.7 copy-start.6
  1.4 0.7 copy-start.7
  1.4 0.7 copy-start.9
  1.4 0.7 copy-start.5
  1.4 0.7 copy-start.4
  1.4 0.7 copy-start.8
  2.1 0.9 copy-start
  3.9 53.7 %all-to-all-start = ((f32[128,8,128]{2,1,0:T(8,128)}), f32[128,8,128]{2,1,0:T(8,128)S(1)}, u32[]{:S(2)}, u32[]{:S(2)}) async-start(f32[128,8,128]{2,1,0:T(8,128)} %get-tuple-element.14), calls=%async_computation | async-start | bytes 1048576 | tf_op jit(solution)/shard_map/all_to_all | solution.py:320
  20.6 10.0 %collective-permute-start.2 = (f32[38,8,128]{2,1,0:T(8,128)S(1)}, f32[38,8,128]{2,1,0:T(8,128)S(1)}, u32[]{:S(2)}, u32[]{:S(2)}) collective-permute-start(f32[38,8,128]{2,1,0:T(8,128)S(1)} %get-tuple-element.12.o), channel_id=1, source_target_pairs={{0,4},{4,8},{8,12},{12,16},{16,20},{20,24},{24,28},{28,32},{32,36}... | collective-permute-start | bytes 466952 | tf_op jit(solution)/shard_map/ppermute | solution.py:278
  24.1 14.4 %collective-permute-start.1 = (f32[38,8,128]{2,1,0:T(8,128)S(1)}, f32[38,8,128]{2,1,0:T(8,128)S(1)}, u32[]{:S(2)}, u32[]{:S(2)}) collective-permute-start(f32[38,8,128]{2,1,0:T(8,128)S(1)} %get-tuple-element.12.o), channel_id=1, source_target_pairs={{0,64},{64,128},{128,192},{192,256},{256,320},{320,384},{384,448},... | collective-permute-start | bytes 466952 | tf_op jit(solution)/shard_map/ppermute | solution.py:277
  27.2 14.8 %collective-permute-start = (f32[38,8,128]{2,1,0:T(8,128)S(1)}, f32[38,8,128]{2,1,0:T(8,128)S(1)}, u32[]{:S(2)}, u32[]{:S(2)}) collective-permute-start(f32[38,8,128]{2,1,0:T(8,128)S(1)} %get-tuple-element.12.o), channel_id=1, source_target_pairs={{0,68},{4,72},{8,76},{12,80},{16,84},{20,88},{24,92},{28,96},{32,1... | collective-permute-start | bytes 466952 | tf_op jit(solution)/shard_map/ppermute | solution.py:284
  57.7 14.3 %copy-start.1 = (f32[1,25,8,128]{3,2,1,0:T(8,128)S(1)}, f32[1,25,8,128]{3,2,1,0:T(8,128)}, u32[]{:S(2)}) copy-start(f32[1,25,8,128]{3,2,1,0:T(8,128)} %param.13) | copy-start | bytes 307204
  57.7 14.3 %copy-start.2 = (f32[1,25,8,128]{3,2,1,0:T(8,128)S(1)}, f32[1,25,8,128]{3,2,1,0:T(8,128)}, u32[]{:S(2)}) copy-start(f32[1,25,8,128]{3,2,1,0:T(8,128)} %param.12) | copy-start | bytes 307204
  58.8 12.2 %collective-permute-start.5 = (f32[27,8,128]{2,1,0:T(8,128)S(1)}, f32[27,8,128]{2,1,0:T(8,128)S(1)}, u32[]{:S(2)}, u32[]{:S(2)}) collective-permute-start(f32[27,8,128]{2,1,0:T(8,128)S(1)} %shard_map.132.o), channel_id=1, source_target_pairs={{0,508},{4,448},{8,452},{12,456},{16,460},{20,464},{24,468},{28,47... | collective-permute-start | bytes 331784 | tf_op jit(solution)/shard_map/ppermute | solution.py:284
  62.6 8.4 %collective-permute-start.4 = (f32[27,8,128]{2,1,0:T(8,128)S(1)}, f32[27,8,128]{2,1,0:T(8,128)S(1)}, u32[]{:S(2)}, u32[]{:S(2)}) collective-permute-start(f32[27,8,128]{2,1,0:T(8,128)S(1)} %shard_map.132.o), channel_id=1, source_target_pairs={{0,448},{64,0},{128,64},{192,128},{256,192},{320,256},{384,320},{4... | collective-permute-start | bytes 331784 | tf_op jit(solution)/shard_map/ppermute | solution.py:277
  65.6 6.4 %collective-permute-start.3 = (f32[27,8,128]{2,1,0:T(8,128)S(1)}, f32[27,8,128]{2,1,0:T(8,128)S(1)}, u32[]{:S(2)}, u32[]{:S(2)}) collective-permute-start(f32[27,8,128]{2,1,0:T(8,128)S(1)} %shard_map.132.o), channel_id=1, source_target_pairs={{0,60},{4,0},{8,4},{12,8},{16,12},{20,16},{24,20},{28,24},{32,28},... | collective-permute-start | bytes 331784 | tf_op jit(solution)/shard_map/ppermute | solution.py:278
  73.5 30.4 %copy-start.3 = (f32[1,25,8,128]{3,2,1,0:T(8,128)S(1)}, f32[1,25,8,128]{3,2,1,0:T(8,128)}, u32[]{:S(2)}) copy-start(f32[1,25,8,128]{3,2,1,0:T(8,128)} %param.11) | copy-start | bytes 307204

commit v2 on v1

v2 whole, which is shorter than its diff:
```python
import functools

import jax
import jax.numpy as jnp
from jax import lax
from jax.experimental import pallas as pl
from jax.experimental.pallas import tpu as pltpu
from jax.sharding import PartitionSpec as P

LEV = 25
PADLEV = 32
ROWS = 8
COLS = 128
SLOTS = 256
SHIFT = 4
WEST = COLS - SHIFT
SWEEPS = 4
GROUP = 5
DIAGS = LEV // 2 + 1

T_FLAG, T_EAST, T_NORTH, T_SIGMA, T_FIELDS, T_OBS = 25, 26, 27, 28, 29, 7
R_CELL, R_OWNER = 2 * LEV, 2 * LEV + 2
EDGE = 8
PER_TILE = COLS // EDGE
T_OWN = T_FIELDS + T_OBS
T_EDGES = -(-T_FIELDS // PER_TILE)
T_SIDE = T_EDGES + T_OBS
T_BAND = T_OWN + 2 * T_SIDE
T_BACK = LEV + 2
T_BACKS = T_BACK + -(-T_BACK // PER_TILE)
BLOCKS = 6
CANDIDATES = BLOCKS * SLOTS
PART_ROWS = 304
LIMIT = 48 * 1024 * 1024


def shifted(x, by, axis):
    by = by % x.shape[axis]
    return pltpu.roll(x, by, axis) if by else x


def split(x, parts):
    out = []
    for _ in range(parts):
        part = x.astype(jnp.bfloat16)
        out.append(part)
        x = x - part.astype(jnp.float32)
    return out


def lanes():
    return lax.broadcasted_iota(jnp.int32, (ROWS, COLS), 1)


def pack_edges(tiles, first):
    slot = lanes() // EDGE
    packed = []
    for start in range(0, len(tiles), PER_TILE):
        out = jnp.zeros((ROWS, COLS), jnp.float32)
        for i, tile in enumerate(tiles[start : start + PER_TILE]):
            out = jnp.where(slot == i, shifted(tile, EDGE * i - first, 1), out)
        packed.append(out)
    return packed


def frame(low, low_edge, high, high_edge):
    low = jnp.concatenate([low, low_edge], axis=-1)
    high = jnp.concatenate([high, high_edge], axis=-1)
    return jnp.concatenate([low, high], axis=-2)


def scaled_faces(ke, kn):
    kw = shifted(ke, 1, 1)
    ks = shifted(kn, 1, 0)
    inverse = 1.0 / (1.0 + ke + kw + kn + ks)
    return inverse, ke * inverse, kw * inverse, kn * inverse, ks * inverse


def diffuse(source, scaled):
    inverse, ke, kw, kn, ks = [term[None] for term in scaled]
    scaled_source = source * inverse
    x = scaled_source
    for _ in range(SWEEPS - 1):
        x = (
            scaled_source
            + ke * shifted(x, -1, 2)
            + kw * shifted(x, 1, 2)
            + kn * shifted(x, -1, 1)
            + ks * shifted(x, 1, 1)
        )
    return x


def one_hot(index, length):
    rows = lax.broadcasted_iota(jnp.int32, (length, index.shape[1]), 0)
    return jnp.where(rows == index, 1.0, 0.0).astype(jnp.bfloat16)


def side_by_side(rows):
    return jnp.concatenate([rows[0:1], rows[1:2]], axis=1)


def place(cell, south, side):
    row, col = cell // COLS, cell % COLS
    if south:
        inside = row >= ROWS - SHIFT
        row = row - (ROWS - SHIFT)
    else:
        inside = row < SHIFT
    if side == 1:
        inside = inside & (col >= WEST)
        index = row * EDGE + col - WEST
    elif side == 2:
        inside = inside & (col < SHIFT)
        index = row * EDGE + col + SHIFT
    else:
        index = row * COLS + col
    return jnp.where(inside, index, -1)


def diagonals(table, wide, turned):
    wide[...] = jnp.zeros_like(wide)
    turned[...] = jnp.zeros_like(turned)
    for i in range(LEV):
        wide[i : i + 1, 0:LEV] = table[i]
    both = wide[...]
    wide[...] = both + shifted(both, LEV, 1)
    for i in range(LEV):
        turned[i : i + 1, :] = shifted(wide[i : i + 1, :], -i, 1)
    turned[...] = jnp.transpose(turned[...])
    tile = jnp.zeros((4, COLS), jnp.float32)
    for q in range(4):
        tile = tile + shifted(turned[pl.ds(q, 4, stride=4), :], PADLEV * q, 1)
    return tile


def pack_kernel(
    d, flag, east, north, sigma, weight, cell, owner, table,
    band, to_east, to_west, tables,
    whole, lines, matrix, wide, turned, sems,
):
    obs = ROWS * T_FIELDS
    tile = lambda t: band.at[pl.ds(ROWS * t, ROWS), :]
    copies = [
        pltpu.make_async_copy(d, band.at[pl.ds(0, ROWS * LEV), :], sems.at[0]),
        pltpu.make_async_copy(flag, whole.at[pl.ds(0, ROWS), :], sems.at[1]),
        pltpu.make_async_copy(east, tile(T_EAST), sems.at[2]),
        pltpu.make_async_copy(north, tile(T_NORTH), sems.at[3]),
        pltpu.make_async_copy(sigma, tile(T_SIGMA), sems.at[4]),
        pltpu.make_async_copy(weight, lines, sems.at[5]),
        pltpu.make_async_copy(cell, whole.at[pl.ds(ROWS, 2), :], sems.at[6]),
        pltpu.make_async_copy(owner, whole.at[pl.ds(2 * ROWS, 2), :], sems.at[7]),
        pltpu.make_async_copy(table, matrix, sems.at[8]),
    ]
    for copy in copies:
        copy.start()
    for copy in copies:
        copy.wait()
    for l in range(LEV):
        for p in (0, 1):
            at = obs + 2 * l + p
            band[at : at + 1, :] = lines[l, :, p * COLS : (p + 1) * COLS]
    band[ROWS * T_FLAG : ROWS * (T_FLAG + 1), :] = whole[0:ROWS, :].astype(jnp.float32)
    band[obs + R_CELL : obs + R_CELL + 2, :] = whole[ROWS : ROWS + 2, :].astype(jnp.float32)
    band[obs + R_OWNER : obs + R_OWNER + 2, :] = whole[2 * ROWS : 2 * ROWS + 2, :].astype(jnp.float32)
    band[obs + R_OWNER + 2 : ROWS * T_OWN, :] = jnp.zeros((2, COLS), jnp.float32)
    tiles = [band[ROWS * t : ROWS * (t + 1), :] for t in range(T_FIELDS)]
    for out, first in ((to_east, COLS - EDGE), (to_west, 0)):
        for i, packed in enumerate(pack_edges(tiles, first)):
            out[ROWS * i : ROWS * (i + 1), :] = packed
        out[ROWS * T_EDGES :, :] = band[obs : ROWS * T_OWN, :]
    tile = diagonals(matrix, wide, turned)
    for i in range(tables.shape[0] // 4):
        tables[4 * i : 4 * i + 4, :] = tile


def band_kernel(band, west, east, given, out, tables):
    out[0 : ROWS * T_OWN, :] = band[...]
    out[ROWS * T_OWN : ROWS * (T_OWN + T_SIDE), :] = west[...]
    out[ROWS * (T_OWN + T_SIDE) : ROWS * T_BAND, :] = east[...]
    count = given.shape[0]
    for i in range(tables.shape[0] // count):
        tables[count * i : count * (i + 1), :] = given[...]


def pick_kernel(
    lats, lons, own, south, part, aux, weights, marks, edges, held, held_edge
):

    lane = lanes()
    for b, band in enumerate((south, own)):
        for t in range(T_FIELDS):
            at = T_OWN + t // PER_TILE
            slot = EDGE * (t % PER_TILE)
            west = band[ROWS * at : ROWS * (at + 1), :]
            east = band[ROWS * (at + T_SIDE) : ROWS * (at + T_SIDE + 1), :]
            west = shifted(west, COLS - EDGE - slot, 1)
            east = shifted(east, -slot, 1)
            edge = jnp.where(lane < EDGE, east, jnp.where(lane >= COLS - EDGE, west, 0.0))
            edges[b, t] = edge

    def framed(first, count):
        rows = slice(ROWS * first, ROWS * (first + count))
        whole = (count, ROWS, COLS)
        levels = slice(first, first + count)
        return frame(
            south[rows, :].reshape(whole), edges[0, levels], own[rows, :].reshape(whole), edges[1, levels]
        )

    flag, east, north, sigma = [framed(t, 1)[0] for t in (T_FLAG, T_EAST, T_NORTH, T_SIGMA)]
    ke = east * flag * shifted(flag, -1, 1)
    kn = north * flag * shifted(flag, -1, 0)
    row = lax.broadcasted_iota(jnp.int32, kn.shape, 0)
    kn = jnp.where((row == ROWS - 1) & (lax.axis_index("lat") == 0), 0.0, kn)
    spread = sigma * flag

    def lower(x):
        axis = x.ndim - 2
        return shifted(x, -SHIFT, axis)[..., :ROWS, :]

    for i, x in enumerate((spread, ke, kn)):
        aux[i] = lower(x)
    scaled = scaled_faces(ke, kn)
    spread = aux[0]
    held[LEV * ROWS :, :] = jnp.zeros(((PADLEV - LEV) * ROWS, COLS), jnp.float32)
    held_edge[LEV * ROWS :, :] = jnp.zeros(((PADLEV - LEV) * ROWS, COLS), jnp.float32)
    for g in range(LEV // GROUP):
        x = lower(diffuse(framed(g * GROUP, GROUP), scaled)) * spread[None]
        rows = slice(g * GROUP * ROWS, (g + 1) * GROUP * ROWS)
        held[rows, :] = x[:, :, :COLS].reshape(GROUP * ROWS, COLS)
        held_edge[rows, :] = x[:, :, COLS:].reshape(GROUP * ROWS, COLS)

    weights[LEV:, :] = jnp.zeros((PADLEV - LEV, CANDIDATES), jnp.float32)
    marks[...] = jnp.zeros_like(marks)
    for b in range(BLOCKS):
        band, side = (own, south)[b // 3], b % 3
        obs = ROWS * (T_FIELDS, T_OWN + T_EDGES, T_OWN + T_SIDE + T_EDGES)[side]
        for p in (0, 1):
            columns = slice(b * SLOTS + p * COLS, b * SLOTS + (p + 1) * COLS)
            weights[0:LEV, columns] = band[pl.ds(obs + p, LEV, stride=2), :]
        columns = slice(b * SLOTS, (b + 1) * SLOTS)
        cell = side_by_side(band[obs + R_CELL : obs + R_CELL + 2, :].astype(jnp.int32))
        marks[0:1, columns] = place(cell, b >= 3, side)
        owner = side_by_side(band[obs + R_OWNER : obs + R_OWNER + 2, :].astype(jnp.int32))
        marks[1:2, columns] = owner % lons * lats + owner // lons

    slot = lax.broadcasted_iota(jnp.int32, (PADLEV, COLS), 1) // EDGE
    for half in (0, 1):
        first = SHIFT * (1 - half)
        centre, edge = [], jnp.zeros((PADLEV, COLS), jnp.float32)
        for r in range(SHIFT):
            centre.append(held[pl.ds(first + r, PADLEV, stride=ROWS), :])
            rolled = shifted(held_edge[pl.ds(first + r, PADLEV, stride=ROWS), :], SHIFT + EDGE * r, 1)
            edge = jnp.where(slot == r, rolled, edge)
        centre = jnp.concatenate(centre, axis=1)
        base = 3 * half * SLOTS
        for state, start, width in ((centre, base, SLOTS), (edge, base + SLOTS, 2 * SLOTS)):
            hot = one_hot(marks[0:1, start : start + width], state.shape[1])
            stacked = jnp.concatenate(split(state, 3), axis=0)
            got = jnp.dot(stacked, hot, preferred_element_type=jnp.float32)
            got = got[0:PADLEV] + got[PADLEV : 2 * PADLEV] + got[2 * PADLEV :]
            got = got * weights[:, start : start + width]
            for c in range(width // COLS):
                at = (start // COLS + c) * LEV
                part[0, at : at + LEV, :] = got[0:LEV, c * COLS : (c + 1) * COLS]
    filled = 2 * BLOCKS * LEV
    part[0, filled:, :] = jnp.zeros((PART_ROWS - filled, COLS), jnp.float32)
    for f in range(1, part.shape[0]):
        part[f] = part[0]


def spread_kernel(
    fields, owners, parts, tables, weights, marks, aux, out, column, double, circled, held, held_edge
):
    total = parts[0]
    for f in range(1, fields):
        total = total + parts[f]
    column[...] = total
    rows = [jnp.transpose(tables[pl.ds(r, owners, stride=4), :]) for r in range(4)]
    rows = jnp.concatenate(rows, axis=0)
    turned = [rows[PADLEV * e : PADLEV * (e + 1)] for e in range(DIAGS)]
    double[...] = jnp.zeros_like(double)
    for e in range(DIAGS, LEV):
        other = turned[LEV - e]
        double[0:LEV, :] = other[0:LEV]
        double[LEV : 2 * LEV, :] = other[0:LEV]
        turned.append(double[e : e + PADLEV, :])
    turned = jnp.concatenate(turned, axis=0)
    turned = jnp.concatenate(split(turned, 2), axis=1)
    circled[...] = jnp.zeros_like(circled)
    weighted = []
    for b in range(BLOCKS):
        columns = slice(b * SLOTS, (b + 1) * SLOTS)
        hot = one_hot(marks[1:2, columns], owners)
        hot = jnp.concatenate([hot, hot], axis=0)
        rows = jnp.dot(turned, hot, preferred_element_type=jnp.float32)
        for p in (0, 1):
            at = (2 * b + p) * LEV
            here = column[at : at + LEV, :]
            circled[0:LEV, p * COLS : (p + 1) * COLS] = here
            circled[LEV : 2 * LEV, p * COLS : (p + 1) * COLS] = here
        sums = rows[0:PADLEV] * circled[0:PADLEV, :]
        for e in range(1, LEV):
            sums = sums + rows[PADLEV * e : PADLEV * (e + 1)] * circled[e : e + PADLEV, :]
        weighted.append(sums * weights[:, columns])
    slot = lax.broadcasted_iota(jnp.int32, (PADLEV, COLS), 1)
    inner = (slot < SHIFT) | (slot >= WEST)
    for half in (0, 1):
        first = SHIFT * (1 - half)
        centre = weighted[3 * half]
        edge = jnp.concatenate(weighted[3 * half + 1 : 3 * half + 3], axis=1)
        base = 3 * half * SLOTS
        found = []
        for value, start, length in ((centre, base, SHIFT * COLS), (edge, base + SLOTS, COLS)):
            hot = one_hot(marks[0:1, start : start + value.shape[1]], length)
            stacked = jnp.concatenate(split(value, 3), axis=0)
            got = lax.dot_general(
                stacked, hot, (((1,), (1,)), ((), ())), preferred_element_type=jnp.float32
            )
            found.append(got[0:PADLEV] + got[PADLEV : 2 * PADLEV] + got[2 * PADLEV :])
        for r in range(SHIFT):
            at = pl.ds(first + r, PADLEV, stride=ROWS)
            held[at, :] = found[0][:, r * COLS : (r + 1) * COLS]
            held_edge[at, :] = jnp.where(inner, shifted(found[1], -SHIFT - EDGE * r, 1), 0.0)
    spread = aux[0]
    tiles = []
    for t in range(LEV):
        rows = slice(ROWS * t, ROWS * (t + 1))
        out[t] = held[rows, :] * spread[:, :COLS]
        tiles.append(held_edge[rows, :] * spread[:, COLS:])
    for i in (1, 2):
        out[LEV + i - 1] = aux[i, :, :COLS]
        tiles.append(aux[i, :, COLS:])
    for i, packed in enumerate(pack_edges(tiles, WEST)):
        out[T_BACK + i] = packed


def image_kernel(own, north, d, res, image, sums, edges):
    lane = lanes()
    inner = (lane < SHIFT) | (lane >= WEST)
    for b, block in enumerate((own, north)):
        for t in range(T_BACK):
            packed = block[T_BACK + t // PER_TILE]
            edge = shifted(packed, -SHIFT - EDGE * (t % PER_TILE), 1)
            edges[b, t] = jnp.where(inner, edge, 0.0)

    def framed(levels):
        return frame(own[levels], edges[0, levels], north[levels], edges[1, levels])

    scaled = scaled_faces(framed(LEV), framed(LEV + 1))
    zero = jnp.zeros((ROWS, COLS), jnp.float32)
    norm, curve, cross, square = zero, zero, zero, zero
    for g in range(LEV // GROUP):
        levels = slice(g * GROUP, (g + 1) * GROUP)
        here = d[levels]
        old = res[levels]
        x = diffuse(framed(levels), scaled)
        x = here + shifted(x[:, :, :COLS], -SHIFT, 1)[:, :ROWS]
        image[levels] = x
        norm = norm + jnp.sum(old * old, axis=0)
        curve = curve + jnp.sum(here * x, axis=0)
        cross = cross + jnp.sum(old * x, axis=0)
        square = square + jnp.sum(x * x, axis=0)
    lane = lax.broadcasted_iota(jnp.int32, (1, COLS), 1)
    line = jnp.zeros((1, COLS), jnp.float32)
    for i, value in enumerate((norm, curve, cross, square)):
        line = jnp.where(lane == i, jnp.sum(value), line)
    sums[...] = jnp.broadcast_to(line, sums.shape)


def sum_kernel(given, out):
    out[...] = jnp.broadcast_to(jnp.sum(given[...], axis=0, keepdims=True), out.shape)


def step_kernel(given, control, res, d, image, control_next, res_next, d_next):
    line = jnp.sum(given[...], axis=0, keepdims=True)
    norm, curve, cross, square = line[:, 0:1], line[:, 1:2], line[:, 2:3], line[:, 3:4]
    alpha = norm / curve
    norm_next = jnp.maximum(norm - 2.0 * alpha * cross + alpha * alpha * square, 0.0)
    beta = norm_next / norm
    alpha = jnp.broadcast_to(alpha, (ROWS, COLS))[None]
    beta = jnp.broadcast_to(beta, (ROWS, COLS))[None]
    here = d[...]
    control_next[...] = control[...] + alpha * here
    new = res[...] - alpha * image[...]
    res_next[...] = new
    d_next[...] = new + beta * here


VMEM = pl.BlockSpec(memory_space=pltpu.VMEM)
ANY = pl.BlockSpec(memory_space=pl.ANY)


def call(kernel, outs, scratch=(), given=VMEM, limit=LIMIT, flops=1000000):
    def shape_of(out):
        shape, dtype = out if isinstance(out[1], type) else (out, jnp.float32)
        return jax.ShapeDtypeStruct(shape, dtype)

    return lambda *arrays: pl.pallas_call(
        kernel,
        out_shape=tuple(shape_of(out) for out in outs),
        in_specs=[given] * len(arrays),
        out_specs=tuple([VMEM] * len(outs)),
        scratch_shapes=[pltpu.VMEM(s, jnp.float32) if isinstance(s, tuple) else s for s in scratch],
        compiler_params=pltpu.CompilerParams(vmem_limit_bytes=limit),
        cost_estimate=pl.CostEstimate(flops=flops, bytes_accessed=1000000, transcendentals=0),
    )(*arrays)


def step(x, axis, by):
    size = lax.axis_size(axis)
    return lax.ppermute(x, axis, [(i, (i + by) % size) for i in range(size)])


def exchange(x, axis):
    size = lax.axis_size(axis)
    blocks = x.reshape(size, x.shape[0] // size, COLS)
    return lax.all_to_all(blocks, axis, 0, 0, tiled=True).reshape(x.shape)


def local(
    control,
    residual,
    direction,
    land_mask,
    kappa_east,
    kappa_north,
    sigma,
    obs_weight,
    obs_cell,
    obs_owner,
    error_inverse,
):
    lats, lons, fields = lax.axis_size("lat"), lax.axis_size("lon"), lax.axis_size("obs")
    owners = lats * lons
    block = (LEV, ROWS, COLS)
    d = direction.reshape(block)
    res = residual.reshape(block)
    band, to_east, to_west, tables = call(
        pack_kernel,
        (
            (ROWS * T_OWN, COLS),
            (ROWS * T_SIDE, COLS),
            (ROWS * T_SIDE, COLS),
            (4 * lats, COLS),
        ),
        (
            pltpu.VMEM((3 * ROWS, COLS), jnp.int32),
            (LEV, 1, SLOTS),
            (LEV, 1, LEV),
            (PADLEV, COLS),
            (COLS, COLS),
            pltpu.SemaphoreType.DMA((9,)),
        ),
        given=ANY,
        limit=56 * 1024 * 1024,
    )(
        direction.reshape(LEV * ROWS, COLS),
        land_mask,
        kappa_east,
        kappa_north,
        sigma.reshape(ROWS, COLS),
        jnp.transpose(obs_weight, (1, 0, 2)),
        obs_cell.reshape(2, COLS),
        obs_owner.reshape(2, COLS),
        jnp.transpose(error_inverse, (1, 0, 2)),
    )
    tables = exchange(tables, "lat")
    west = step(to_east, "lon", 1)
    east = step(to_west, "lon", -1)
    band, tables = call(band_kernel, ((ROWS * T_BAND, COLS), (4 * owners, COLS)))(
        band, west, east, tables
    )
    south = step(band, "lat", 1)
    tables = exchange(tables, "lon")
    part, aux, weights, marks = call(
        functools.partial(pick_kernel, lats, lons),
        (
            (fields, PART_ROWS, COLS),
            (3, ROWS, 2 * COLS),
            (PADLEV, CANDIDATES),
            ((8, CANDIDATES), jnp.int32),
        ),
        (
            (2, T_FIELDS, ROWS, COLS),
            (PADLEV * ROWS, COLS),
            (PADLEV * ROWS, COLS),
        ),
    )(band, south)
    parts = lax.all_to_all(part, "obs", 0, 0, tiled=True)
    (source,) = call(
        functools.partial(spread_kernel, fields, owners),
        ((T_BACKS, ROWS, COLS),),
        (
            (PART_ROWS, COLS),
            (2 * PADLEV, owners),
            (2 * PADLEV, SLOTS),
            (PADLEV * ROWS, COLS),
            (PADLEV * ROWS, COLS),
        ),
    )(parts, tables, weights, marks, aux)
    north = step(source, "lat", -1)
    image, sums = call(
        image_kernel, (block, (fields * lons, COLS)), ((2, T_BACK, ROWS, COLS),)
    )(source, north, d, res)
    sums = lax.all_to_all(sums, ("obs", "lon"), 0, 0, tiled=True)
    (sums,) = call(sum_kernel, ((lats, COLS),))(sums)
    sums = lax.all_to_all(sums, "lat", 0, 0, tiled=True)
    outs = call(step_kernel, (block, block, block))(sums, control.reshape(block), res, d, image)
    return tuple(out.reshape(direction.shape) for out in outs)


def solution(mesh):
    state = P("obs", None, "lat", "lon")
    placed = (
        state,
        state,
        state,
        P("lat", "lon"),
        P("lat", "lon"),
        P("lat", "lon"),
        P("obs", "lat", "lon"),
        P("obs", None, ("lat", "lon")),
        P(("lat", "lon")),
        P(("lat", "lon"), None),
        P(("lat", "lon"), None, None),
    )
    return jax.shard_map(
        local, mesh=mesh, in_specs=placed, out_specs=(state, state, state), check_vma=False
    )
```

time: 105 us -> 108 us (1.029)
  blocking collectives: 44.6 us -> 63.9 us
  starting transfers between devices: 38.8 us -> 22.4 us
  Pallas kernels: 5.81 us -> 7.95 us
  local copies, waits for them, and re-layouts: 2.36 us -> 0.92 us
  waiting for transfers between devices: 12.4 us -> 11.3 us
    all_to_all x0 -> x2, blocking collectives: none -> 33.3 us  [the longest x1 20.9 us: local(): parts = lax.all_to_all(part, 'obs', 0, 0, tiled=True)]
    all_gather x1 -> x0, blocking collectives: 14.2 us -> none  [local(): parts = lax.all_gather(part, 'obs', tiled=True)]
    all_to_all x1, starting transfers between devices: 16.6 us -> 7.49 us  [exchange(): return lax.all_to_all(blocks, axis, 0, 0, tiled=True).reshape(x.shape)]
    ppermute x6 -> x4, starting transfers between devices: 22.2 us -> 14.9 us  [step(): return lax.ppermute(x, axis, [(i, (i + by) % size) for i in range(size)])]
    pallas_call x6 -> x7, Pallas kernels: 5.81 us -> 7.95 us  [call(): pl.pallas_call(kernel, out_shape=tuple((shape_of(out) for out in outs)),...]
    unnamed x24 -> x8, local copies, waits for them, and re-layouts: 2.36 us -> 0.92 us
    ppermute x6 -> x4, waiting for transfers between devices: 12.4 us -> 11.3 us  [step(): return lax.ppermute(x, axis, [(i, (i + by) % size) for i in range(size)])]
  transfers between devices with their start and end apart: 7 -> 5, of which waited for: 3 -> 2; matrix products, arithmetic and copies ran while one was open for 0% -> 0% of each run, Pallas kernels for 1% -> 1%
where the time goes in v2:
time: 108 us; the launch traced here: 107 us
  blocking collectives  63.9 us (59%)
  starting transfers between devices  22.4 us (21%)
  waiting for transfers between devices  11.3 us (10%)
  Pallas kernels  7.95 us (7%)
    all_to_all x1, blocking collectives, local(): sums = lax.all_to_all(sums, ('obs', 'lon'), 0, 0, tiled=True)  21.6 us
    all_to_all x1, blocking collectives, local(): parts = lax.all_to_all(part, 'obs', 0, 0, tiled=True)  20.9 us
    ppermute x4, starting transfers between devices, step(): return lax.ppermute(x, axis, [(i, (i + by) % size) for i in range(size)])  14.9 us
    all_to_all x1, blocking collectives, exchange(): return lax.all_to_all(blocks, axis, 0, 0, tiled=True).reshape(x.shape)  12.4 us
    ppermute x4, waiting for transfers between devices, step(): return lax.ppermute(x, axis, [(i, (i + by) % size) for i in range(size)])  11.3 us
    all_to_all x1, blocking collectives, local(): sums = lax.all_to_all(sums, 'lat', 0, 0, tiled=True)  8.89 us
    pallas_call x7, Pallas kernels, call(): pl.pallas_call(kernel, out_shape=tuple((shape_of(out) for out in outs)),...  7.95 us
    all_to_all x1, starting transfers between devices, exchange(): return lax.all_to_all(blocks, axis, 0, 0, tiled=True).reshape(x.shape)  7.49 us
  transfers between devices with their start and end apart: 5, of which 2 were waited for; matrix products, arithmetic and copies ran while one was open for 0% of the time, Pallas kernels for 1%

profile of v2, /device:TPU:1, one launch (start us, length us, event | category | flops | bytes accessed | tf_op | source)
XLA Modules:
  0.0 107.1 jit_solution(9340816962182611717)
XLA Ops:
  0.6 1.9 %shard_map.130 = (f32[288,128]{1,0:T(8,128)}, f32[72,128]{1,0:T(8,128)}, f32[72,128]{1,0:T(8,128)}, f32[32,128]{1,0:T(8,128)}) custom-call(f32[200,128]{1,0:T(8,128)} %bitcast.25, s32[8,128]{1,0:T(8,128)} %flag.1, f32[8,128]{1,0:T(8,128)} %east.1, f32[8,128]{1,0:T(8,128)} %north.1, f32[8,128]{1,0:T(8,128)} %bitcast.39, f32[25,1,256]{2,1,0:T(1,128)} %bitcast.36, ...), custom_call_target="tpu_custom_call" | custom-call | flops 1000000 | bytes 1000000 | tf_op jit(solution)/shard_map/pallas_call | solution.py:399
  2.6 4.5 %collective-permute-start = (f32[72,128]{1,0:T(8,128)}, f32[72,128]{1,0:T(8,128)S(1)}, u32[]{:S(2)}, u32[]{:S(2)}) collective-permute-start(f32[72,128]{1,0:T(8,128)} %get-tuple-element.19), channel_id=1, source_target_pairs={{0,4},{4,8},{8,12},{12,16},{16,20},{20,24},{24,28},{28,32},{32,36}... | collective-permute-start | bytes 110600 | tf_op jit(solution)/shard_map/ppermute | solution.py:412
  7.1 6.2 %collective-permute-start.1 = (f32[72,128]{1,0:T(8,128)}, f32[72,128]{1,0:T(8,128)S(1)}, u32[]{:S(2)}, u32[]{:S(2)}) collective-permute-start(f32[72,128]{1,0:T(8,128)} %get-tuple-element.20), channel_id=1, source_target_pairs={{0,60},{4,0},{8,4},{12,8},{16,12},{20,16},{24,20},{28,24},{32,28},... | collective-permute-start | bytes 110600 | tf_op jit(solution)/shard_map/ppermute | solution.py:412
  13.3 12.4 %all_to_all.37 = f32[8,4,128]{2,1,0:T(4,128)S(1)} all-to-all(f32[8,4,128]{2,1,0:T(4,128)} %bitcast.37), channel_id=1, replica_groups=mesh['lat'=8,'lon'=16,'obs'=4] {'lat'}, dimensions={0} | all-to-all | bytes 32768 | tf_op jit(solution)/shard_map/all_to_all | solution.py:418
  25.7 0.0 collective-permute-done.west
  25.7 0.0 collective-permute-done.1.east
  25.7 0.9 copy-done.2
  26.6 0.7 shard_map.131
  27.4 7.5 %all-to-all-start.2 = ((f32[16,32,128]{2,1,0:T(8,128)}), f32[16,32,128]{2,1,0:T(8,128)S(1)}, u32[]{:S(2)}, u32[]{:S(2)}) async-start(f32[16,32,128]{2,1,0:T(8,128)} %bitcast.8), calls=%async_computation.2 | async-start | bytes 524288 | tf_op jit(solution)/shard_map/all_to_all | solution.py:418
  34.9 2.2 %collective-permute-start.2 = (f32[432,128]{1,0:T(8,128)S(1)}, f32[432,128]{1,0:T(8,128)S(1)}, u32[]{:S(2)}, u32[]{:S(2)}) collective-permute-start(f32[432,128]{1,0:T(8,128)S(1)} %get-tuple-element.22.own), channel_id=1, source_target_pairs={{0,64},{64,128},{128,192},{192,256},{256,320},{320,384},{384,448},... | collective-permute-start | bytes 663560 | tf_op jit(solution)/shard_map/ppermute | solution.py:412
  37.1 7.7 %collective-permute-done.2.south = f32[432,128]{1,0:T(8,128)S(1)} collective-permute-done((f32[432,128]{1,0:T(8,128)S(1)}, f32[432,128]{1,0:T(8,128)S(1)}, u32[]{:S(2)}, u32[]{:S(2)}) %collective-permute-start.2) | collective-permute-done | bytes 221216 | tf_op jit(solution)/shard_map/ppermute | solution.py:412
  44.7 1.6 %shard_map.132 = (f32[4,304,128]{2,1,0:T(8,128)S(1)}, f32[3,8,256]{2,1,0:T(8,128)S(1)}, f32[32,1536]{1,0:T(8,128)S(1)}, s32[8,1536]{1,0:T(8,128)S(1)}) custom-call(f32[432,128]{1,0:T(8,128)S(1)} %get-tuple-element.22.own, f32[432,128]{1,0:T(8,128)S(1)} %collective-permute-done.2.south), custom_call_target="tpu_custom_call" | custom-call | flops 1000000 | bytes 1000000 | tf_op jit(solution)/shard_map/pallas_call | solution.py:399
  46.3 0.0 all-to-all-done.2
  46.3 20.9 %all_to_all.38.parts = f32[4,304,128]{2,1,0:T(8,128)S(1)} all-to-all(f32[4,304,128]{2,1,0:T(8,128)S(1)} %get-tuple-element.23), channel_id=1, replica_groups=mesh['lat'=8,'lon'=16,'obs'=4] {'obs'}, dimensions={0} | all-to-all | bytes 1245184 | tf_op jit(solution)/shard_map/all_to_all | solution.py:490
  67.3 1.5 %shard_map.133.own = f32[29,8,128]{2,1,0:T(8,128)S(1)} custom-call(f32[4,304,128]{2,1,0:T(8,128)S(1)} %all_to_all.38.parts, f32[512,128]{1,0:T(8,128)S(1)} %bitcast.24, f32[32,1536]{1,0:T(8,128)S(1)} %get-tuple-element.25.weights, s32[8,1536]{1,0:T(8,128)S(1)} %get-tuple-element.26.marks, f32[3,8,256]{2,1,0:T(8,128)S(1)} %get-tuple-element.27.aux), custom_call_target="tpu_custom_call" | custom-call | flops 1000000 | bytes 1000000 | tf_op jit(solution)/shard_map/pallas_call | solution.py:399
  68.8 1.9 %collective-permute-start.3 = (f32[29,8,128]{2,1,0:T(8,128)S(1)}, f32[29,8,128]{2,1,0:T(8,128)S(1)}, u32[]{:S(2)}, u32[]{:S(2)}) collective-permute-start(f32[29,8,128]{2,1,0:T(8,128)S(1)} %shard_map.133.own), channel_id=1, source_target_pairs={{0,448},{64,0},{128,64},{192,128},{256,192},{320,256},{384,320},{4... | collective-permute-start | bytes 356360 | tf_op jit(solution)/shard_map/ppermute | solution.py:412
  70.7 3.7 %collective-permute-done.3.north = f32[29,8,128]{2,1,0:T(8,128)S(1)} collective-permute-done((f32[29,8,128]{2,1,0:T(8,128)S(1)}, f32[29,8,128]{2,1,0:T(8,128)S(1)}, u32[]{:S(2)}, u32[]{:S(2)}) %collective-permute-start.3) | collective-permute-done | bytes 118816 | tf_op jit(solution)/shard_map/ppermute | solution.py:412
  74.4 0.0 copy-done
  74.4 0.0 copy-done.1
  74.4 1.4 %shard_map.134 = (f32[25,8,128]{2,1,0:T(8,128)S(1)}, f32[64,128]{1,0:T(8,128)S(1)}) custom-call(f32[29,8,128]{2,1,0:T(8,128)S(1)} %shard_map.133.own, f32[29,8,128]{2,1,0:T(8,128)S(1)} %collective-permute-done.3.north, f32[25,8,128]{2,1,0:T(8,128)S(1)} %bitcast.26, f32[25,8,128]{2,1,0:T(8,128)S(1)} %bitcast.28), custom_call_target="tpu_custom_call" | custom-call | flops 1000000 | bytes 1000000 | tf_op jit(solution)/shard_map/pallas_call | solution.py:399
  75.7 0.0 copy-start.3
  75.7 21.6 %all_to_all.39 = f32[64,1,128]{2,1,0:T(1,128)S(1)} all-to-all(f32[64,1,128]{2,1,0:T(1,128)S(1)} %bitcast.33), channel_id=1, replica_groups=mesh['lat'=8,'lon'=16,'obs'=4] {'obs','lon'}, dimensions={0} | all-to-all | bytes 65536 | tf_op jit(solution)/shard_map/all_to_all | solution.py:506
  97.4 8.9 %all_to_all.40 = f32[8,1,128]{2,1,0:T(1,128)S(1)} all-to-all(f32[8,1,128]{2,1,0:T(1,128)S(1)} %bitcast.35), channel_id=1, replica_groups=mesh['lat'=8,'lon'=16,'obs'=4] {'lat'}, dimensions={0} | all-to-all | bytes 8192 | tf_op jit(solution)/shard_map/all_to_all | solution.py:508
  106.3 0.8 shard_map.136
  (5 shorter events, 0.0 us)
Async XLA Ops:
  2.6 23.1 %collective-permute-start = (f32[72,128]{1,0:T(8,128)}, f32[72,128]{1,0:T(8,128)S(1)}, u32[]{:S(2)}, u32[]{:S(2)}) collective-permute-start(f32[72,128]{1,0:T(8,128)} %get-tuple-element.19), channel_id=1, source_target_pairs={{0,4},{4,8},{8,12},{12,16},{16,20},{20,24},{24,28},{28,32},{32,36}... | collective-permute-start | bytes 110600 | tf_op jit(solution)/shard_map/ppermute | solution.py:412
  7.1 18.6 %collective-permute-start.1 = (f32[72,128]{1,0:T(8,128)}, f32[72,128]{1,0:T(8,128)S(1)}, u32[]{:S(2)}, u32[]{:S(2)}) collective-permute-start(f32[72,128]{1,0:T(8,128)} %get-tuple-element.20), channel_id=1, source_target_pairs={{0,60},{4,0},{8,4},{12,8},{16,12},{20,16},{24,20},{28,24},{32,28},... | collective-permute-start | bytes 110600 | tf_op jit(solution)/shard_map/ppermute | solution.py:412
  25.7 0.9 copy-start.2
  27.4 18.9 %all-to-all-start.2 = ((f32[16,32,128]{2,1,0:T(8,128)}), f32[16,32,128]{2,1,0:T(8,128)S(1)}, u32[]{:S(2)}, u32[]{:S(2)}) async-start(f32[16,32,128]{2,1,0:T(8,128)} %bitcast.8), calls=%async_computation.2 | async-start | bytes 524288 | tf_op jit(solution)/shard_map/all_to_all | solution.py:418
  34.9 9.9 %collective-permute-start.2 = (f32[432,128]{1,0:T(8,128)S(1)}, f32[432,128]{1,0:T(8,128)S(1)}, u32[]{:S(2)}, u32[]{:S(2)}) collective-permute-start(f32[432,128]{1,0:T(8,128)S(1)} %get-tuple-element.22.own), channel_id=1, source_target_pairs={{0,64},{64,128},{128,192},{192,256},{256,320},{320,384},{384,448},... | collective-permute-start | bytes 663560 | tf_op jit(solution)/shard_map/ppermute | solution.py:412
  67.3 7.1 %copy-start = (f32[1,25,8,128]{3,2,1,0:T(8,128)S(1)}, f32[1,25,8,128]{3,2,1,0:T(8,128)}, u32[]{:S(2)}) copy-start(f32[1,25,8,128]{3,2,1,0:T(8,128)} %param.13) | copy-start | bytes 307204
  67.3 7.1 %copy-start.1 = (f32[1,25,8,128]{3,2,1,0:T(8,128)S(1)}, f32[1,25,8,128]{3,2,1,0:T(8,128)}, u32[]{:S(2)}) copy-start(f32[1,25,8,128]{3,2,1,0:T(8,128)} %param.12) | copy-start | bytes 307204
  68.8 5.6 %collective-permute-start.3 = (f32[29,8,128]{2,1,0:T(8,128)S(1)}, f32[29,8,128]{2,1,0:T(8,128)S(1)}, u32[]{:S(2)}, u32[]{:S(2)}) collective-permute-start(f32[29,8,128]{2,1,0:T(8,128)S(1)} %shard_map.133.own), channel_id=1, source_target_pairs={{0,448},{64,0},{128,64},{192,128},{256,192},{320,256},{384,320},{4... | collective-permute-start | bytes 356360 | tf_op jit(solution)/shard_map/ppermute | solution.py:412
  75.7 30.6 %copy-start.3 = (f32[1,25,8,128]{3,2,1,0:T(8,128)S(1)}, f32[1,25,8,128]{3,2,1,0:T(8,128)}, u32[]{:S(2)}) copy-start(f32[1,25,8,128]{3,2,1,0:T(8,128)} %param.11) | copy-start | bytes 307204

commit v3 on v2

--- a/solution.py
+++ b/solution.py
@@ -13,7 +13,6 @@
 COLS = 128
 SLOTS = 256
 SHIFT = 4
-WEST = COLS - SHIFT
 SWEEPS = 4
 GROUP = 5
 DIAGS = LEV // 2 + 1
@@ -25,12 +24,11 @@
 T_OWN = T_FIELDS + T_OBS
 T_EDGES = -(-T_FIELDS // PER_TILE)
 T_SIDE = T_EDGES + T_OBS
-T_BAND = T_OWN + 2 * T_SIDE
 T_BACK = LEV + 2
-T_BACKS = T_BACK + -(-T_BACK // PER_TILE)
-BLOCKS = 6
+T_BACK_SIDE = -(-T_BACK // PER_TILE)
+BLOCKS = 4
 CANDIDATES = BLOCKS * SLOTS
-PART_ROWS = 304
+PART_ROWS = 2 * BLOCKS * LEV
 LIMIT = 48 * 1024 * 1024
 
 
@@ -100,22 +98,20 @@
     return jnp.concatenate([rows[0:1], rows[1:2]], axis=1)
 
 
-def place(cell, south, side):
+def place(cell, south, west):
     row, col = cell // COLS, cell % COLS
     if south:
         inside = row >= ROWS - SHIFT
         row = row - (ROWS - SHIFT)
     else:
         inside = row < SHIFT
-    if side == 1:
-        inside = inside & (col >= WEST)
-        index = row * EDGE + col - WEST
-    elif side == 2:
-        inside = inside & (col < SHIFT)
-        index = row * EDGE + col + SHIFT
+    if west:
+        inside = inside & (col >= COLS - SHIFT)
+        col = col - (COLS - SHIFT)
     else:
-        index = row * COLS + col
-    return jnp.where(inside, index, -1)
+        inside = inside & (col < COLS - SHIFT)
+        col = col + SHIFT
+    return jnp.where(inside, row * COLS + col, -1)
 
 
 def diagonals(table, wide, turned):
@@ -136,17 +132,17 @@
 
 def pack_kernel(
     d, flag, east, north, sigma, weight, cell, owner, table,
-    band, to_east, to_west, tables,
+    band, side, tile,
     whole, lines, matrix, wide, turned, sems,
 ):
     obs = ROWS * T_FIELDS
-    tile = lambda t: band.at[pl.ds(ROWS * t, ROWS), :]
+    place_of = lambda t: band.at[pl.ds(ROWS * t, ROWS), :]
     copies = [
         pltpu.make_async_copy(d, band.at[pl.ds(0, ROWS * LEV), :], sems.at[0]),
         pltpu.make_async_copy(flag, whole.at[pl.ds(0, ROWS), :], sems.at[1]),
-        pltpu.make_async_copy(east, tile(T_EAST), sems.at[2]),
-        pltpu.make_async_copy(north, tile(T_NORTH), sems.at[3]),
-        pltpu.make_async_copy(sigma, tile(T_SIGMA), sems.at[4]),
+        pltpu.make_async_copy(east, place_of(T_EAST), sems.at[2]),
+        pltpu.make_async_copy(north, place_of(T_NORTH), sems.at[3]),
+        pltpu.make_async_copy(sigma, place_of(T_SIGMA), sems.at[4]),
         pltpu.make_async_copy(weight, lines, sems.at[5]),
         pltpu.make_async_copy(cell, whole.at[pl.ds(ROWS, 2), :], sems.at[6]),
         pltpu.make_async_copy(owner, whole.at[pl.ds(2 * ROWS, 2), :], sems.at[7]),
@@ -165,39 +161,28 @@
     band[obs + R_OWNER : obs + R_OWNER + 2, :] = whole[2 * ROWS : 2 * ROWS + 2, :].astype(jnp.float32)
     band[obs + R_OWNER + 2 : ROWS * T_OWN, :] = jnp.zeros((2, COLS), jnp.float32)
     tiles = [band[ROWS * t : ROWS * (t + 1), :] for t in range(T_FIELDS)]
-    for out, first in ((to_east, COLS - EDGE), (to_west, 0)):
-        for i, packed in enumerate(pack_edges(tiles, first)):
-            out[ROWS * i : ROWS * (i + 1), :] = packed
-        out[ROWS * T_EDGES :, :] = band[obs : ROWS * T_OWN, :]
-    tile = diagonals(matrix, wide, turned)
-    for i in range(tables.shape[0] // 4):
-        tables[4 * i : 4 * i + 4, :] = tile
-
-
-def band_kernel(band, west, east, given, out, tables):
-    out[0 : ROWS * T_OWN, :] = band[...]
-    out[ROWS * T_OWN : ROWS * (T_OWN + T_SIDE), :] = west[...]
-    out[ROWS * (T_OWN + T_SIDE) : ROWS * T_BAND, :] = east[...]
-    count = given.shape[0]
-    for i in range(tables.shape[0] // count):
-        tables[count * i : count * (i + 1), :] = given[...]
+    for i, packed in enumerate(pack_edges(tiles, COLS - EDGE)):
+        side[ROWS * i : ROWS * (i + 1), :] = packed
+    side[ROWS * T_EDGES :, :] = band[obs : ROWS * T_OWN, :]
+    tile[...] = diagonals(matrix, wide, turned)
+
+
+def repeat_kernel(tile, tables):
+    pair = jnp.concatenate([tile[...], tile[...]], axis=0)
+    for i in range(tables.shape[0] // ROWS):
+        tables[ROWS * i : ROWS * (i + 1), :] = pair
 
 
 def pick_kernel(
-    lats, lons, own, south, part, aux, weights, marks, edges, held, held_edge
+    own, west, south, both, part, aux, weights, marks, edges, held
 ):
-
     lane = lanes()
-    for b, band in enumerate((south, own)):
+    for b, side in enumerate((both, west)):
         for t in range(T_FIELDS):
-            at = T_OWN + t // PER_TILE
-            slot = EDGE * (t % PER_TILE)
-            west = band[ROWS * at : ROWS * (at + 1), :]
-            east = band[ROWS * (at + T_SIDE) : ROWS * (at + T_SIDE + 1), :]
-            west = shifted(west, COLS - EDGE - slot, 1)
-            east = shifted(east, -slot, 1)
-            edge = jnp.where(lane < EDGE, east, jnp.where(lane >= COLS - EDGE, west, 0.0))
-            edges[b, t] = edge
+            at = ROWS * (t // PER_TILE)
+            packed = side[at : at + ROWS, :]
+            edge = shifted(packed, COLS - EDGE - EDGE * (t % PER_TILE), 1)
+            edges[b, t] = jnp.where(lane >= COLS - EDGE, edge, 0.0)
 
     def framed(first, count):
         rows = slice(ROWS * first, ROWS * (first + count))
@@ -216,6 +201,7 @@
 
     def lower(x):
         axis = x.ndim - 2
+        x = shifted(x, SHIFT, axis + 1)[..., :COLS]
         return shifted(x, -SHIFT, axis)[..., :ROWS, :]
 
     for i, x in enumerate((spread, ke, kn)):
@@ -223,58 +209,47 @@
     scaled = scaled_faces(ke, kn)
     spread = aux[0]
     held[LEV * ROWS :, :] = jnp.zeros(((PADLEV - LEV) * ROWS, COLS), jnp.float32)
-    held_edge[LEV * ROWS :, :] = jnp.zeros(((PADLEV - LEV) * ROWS, COLS), jnp.float32)
     for g in range(LEV // GROUP):
         x = lower(diffuse(framed(g * GROUP, GROUP), scaled)) * spread[None]
         rows = slice(g * GROUP * ROWS, (g + 1) * GROUP * ROWS)
-        held[rows, :] = x[:, :, :COLS].reshape(GROUP * ROWS, COLS)
-        held_edge[rows, :] = x[:, :, COLS:].reshape(GROUP * ROWS, COLS)
+        held[rows, :] = x.reshape(GROUP * ROWS, COLS)
 
     weights[LEV:, :] = jnp.zeros((PADLEV - LEV, CANDIDATES), jnp.float32)
     marks[...] = jnp.zeros_like(marks)
     for b in range(BLOCKS):
-        band, side = (own, south)[b // 3], b % 3
-        obs = ROWS * (T_FIELDS, T_OWN + T_EDGES, T_OWN + T_SIDE + T_EDGES)[side]
+        band = (own, west, south, both)[b]
+        obs = ROWS * (T_EDGES if b % 2 else T_FIELDS)
         for p in (0, 1):
             columns = slice(b * SLOTS + p * COLS, b * SLOTS + (p + 1) * COLS)
             weights[0:LEV, columns] = band[pl.ds(obs + p, LEV, stride=2), :]
         columns = slice(b * SLOTS, (b + 1) * SLOTS)
         cell = side_by_side(band[obs + R_CELL : obs + R_CELL + 2, :].astype(jnp.int32))
-        marks[0:1, columns] = place(cell, b >= 3, side)
+        marks[0:1, columns] = place(cell, b >= 2, b % 2)
         owner = side_by_side(band[obs + R_OWNER : obs + R_OWNER + 2, :].astype(jnp.int32))
-        marks[1:2, columns] = owner % lons * lats + owner // lons
-
-    slot = lax.broadcasted_iota(jnp.int32, (PADLEV, COLS), 1) // EDGE
+        marks[1:2, columns] = owner
+
     for half in (0, 1):
         first = SHIFT * (1 - half)
-        centre, edge = [], jnp.zeros((PADLEV, COLS), jnp.float32)
-        for r in range(SHIFT):
-            centre.append(held[pl.ds(first + r, PADLEV, stride=ROWS), :])
-            rolled = shifted(held_edge[pl.ds(first + r, PADLEV, stride=ROWS), :], SHIFT + EDGE * r, 1)
-            edge = jnp.where(slot == r, rolled, edge)
-        centre = jnp.concatenate(centre, axis=1)
-        base = 3 * half * SLOTS
-        for state, start, width in ((centre, base, SLOTS), (edge, base + SLOTS, 2 * SLOTS)):
-            hot = one_hot(marks[0:1, start : start + width], state.shape[1])
-            stacked = jnp.concatenate(split(state, 3), axis=0)
-            got = jnp.dot(stacked, hot, preferred_element_type=jnp.float32)
-            got = got[0:PADLEV] + got[PADLEV : 2 * PADLEV] + got[2 * PADLEV :]
-            got = got * weights[:, start : start + width]
-            for c in range(width // COLS):
-                at = (start // COLS + c) * LEV
-                part[0, at : at + LEV, :] = got[0:LEV, c * COLS : (c + 1) * COLS]
-    filled = 2 * BLOCKS * LEV
-    part[0, filled:, :] = jnp.zeros((PART_ROWS - filled, COLS), jnp.float32)
-    for f in range(1, part.shape[0]):
-        part[f] = part[0]
+        state = jnp.concatenate(
+            [held[pl.ds(first + r, PADLEV, stride=ROWS), :] for r in range(SHIFT)], axis=1
+        )
+        columns = slice(2 * half * SLOTS, 2 * (half + 1) * SLOTS)
+        hot = one_hot(marks[0:1, columns], SHIFT * COLS)
+        stacked = jnp.concatenate(split(state, 3), axis=0)
+        got = jnp.dot(stacked, hot, preferred_element_type=jnp.float32)
+        got = got[0:PADLEV] + got[PADLEV : 2 * PADLEV] + got[2 * PADLEV :]
+        got = got * weights[:, columns]
+        for c in range(4):
+            at = (4 * half + c) * LEV
+            part[at : at + LEV, :] = got[0:LEV, c * COLS : (c + 1) * COLS]
 
 
 def spread_kernel(
-    fields, owners, parts, tables, weights, marks, aux, out, column, double, circled, held, held_edge
+    fields, owners, parts, tables, weights, marks, aux, out, side, column, double, circled, held
 ):
-    total = parts[0]
+    total = parts[0:PART_ROWS, :]
     for f in range(1, fields):
-        total = total + parts[f]
+        total = total + parts[f * PART_ROWS : (f + 1) * PART_ROWS, :]
     column[...] = total
     rows = [jnp.transpose(tables[pl.ds(r, owners, stride=4), :]) for r in range(4)]
     rows = jnp.concatenate(rows, axis=0)
@@ -303,46 +278,31 @@
         for e in range(1, LEV):
             sums = sums + rows[PADLEV * e : PADLEV * (e + 1)] * circled[e : e + PADLEV, :]
         weighted.append(sums * weights[:, columns])
-    slot = lax.broadcasted_iota(jnp.int32, (PADLEV, COLS), 1)
-    inner = (slot < SHIFT) | (slot >= WEST)
     for half in (0, 1):
         first = SHIFT * (1 - half)
-        centre = weighted[3 * half]
-        edge = jnp.concatenate(weighted[3 * half + 1 : 3 * half + 3], axis=1)
-        base = 3 * half * SLOTS
-        found = []
-        for value, start, length in ((centre, base, SHIFT * COLS), (edge, base + SLOTS, COLS)):
-            hot = one_hot(marks[0:1, start : start + value.shape[1]], length)
-            stacked = jnp.concatenate(split(value, 3), axis=0)
-            got = lax.dot_general(
-                stacked, hot, (((1,), (1,)), ((), ())), preferred_element_type=jnp.float32
-            )
-            found.append(got[0:PADLEV] + got[PADLEV : 2 * PADLEV] + got[2 * PADLEV :])
+        value = jnp.concatenate(weighted[2 * half : 2 * half + 2], axis=1)
+        columns = slice(2 * half * SLOTS, 2 * (half + 1) * SLOTS)
+        hot = one_hot(marks[0:1, columns], SHIFT * COLS)
+        stacked = jnp.concatenate(split(value, 3), axis=0)
+        got = lax.dot_general(
+            stacked, hot, (((1,), (1,)), ((), ())), preferred_element_type=jnp.float32
+        )
+        got = got[0:PADLEV] + got[PADLEV : 2 * PADLEV] + got[2 * PADLEV :]
         for r in range(SHIFT):
-            at = pl.ds(first + r, PADLEV, stride=ROWS)
-            held[at, :] = found[0][:, r * COLS : (r + 1) * COLS]
-            held_edge[at, :] = jnp.where(inner, shifted(found[1], -SHIFT - EDGE * r, 1), 0.0)
-    spread = aux[0]
-    tiles = []
-    for t in range(LEV):
-        rows = slice(ROWS * t, ROWS * (t + 1))
-        out[t] = held[rows, :] * spread[:, :COLS]
-        tiles.append(held_edge[rows, :] * spread[:, COLS:])
-    for i in (1, 2):
-        out[LEV + i - 1] = aux[i, :, :COLS]
-        tiles.append(aux[i, :, COLS:])
-    for i, packed in enumerate(pack_edges(tiles, WEST)):
-        out[T_BACK + i] = packed
-
-
-def image_kernel(own, north, d, res, image, sums, edges):
+            held[pl.ds(first + r, PADLEV, stride=ROWS), :] = got[:, r * COLS : (r + 1) * COLS]
+    tiles = [held[ROWS * t : ROWS * (t + 1), :] * aux[0] for t in range(LEV)] + [aux[1], aux[2]]
+    for t, tile in enumerate(tiles):
+        out[t] = tile
+    for i, packed in enumerate(pack_edges(tiles, 0)):
+        side[i] = packed
+
+
+def image_kernel(own, east, north, both, d, res, image, sums, edges):
     lane = lanes()
-    inner = (lane < SHIFT) | (lane >= WEST)
-    for b, block in enumerate((own, north)):
+    for b, side in enumerate((east, both)):
         for t in range(T_BACK):
-            packed = block[T_BACK + t // PER_TILE]
-            edge = shifted(packed, -SHIFT - EDGE * (t % PER_TILE), 1)
-            edges[b, t] = jnp.where(inner, edge, 0.0)
+            edge = shifted(side[t // PER_TILE], -EDGE * (t % PER_TILE), 1)
+            edges[b, t] = jnp.where(lane < EDGE, edge, 0.0)
 
     def framed(levels):
         return frame(own[levels], edges[0, levels], north[levels], edges[1, levels])
@@ -355,7 +315,8 @@
         here = d[levels]
         old = res[levels]
         x = diffuse(framed(levels), scaled)
-        x = here + shifted(x[:, :, :COLS], -SHIFT, 1)[:, :ROWS]
+        x = shifted(x, -SHIFT, 2)[:, :, :COLS]
+        x = here + shifted(x, -SHIFT, 1)[:, :ROWS]
         image[levels] = x
         norm = norm + jnp.sum(old * old, axis=0)
         curve = curve + jnp.sum(here * x, axis=0)
@@ -412,10 +373,14 @@
     return lax.ppermute(x, axis, [(i, (i + by) % size) for i in range(size)])
 
 
-def exchange(x, axis):
-    size = lax.axis_size(axis)
-    blocks = x.reshape(size, x.shape[0] // size, COLS)
-    return lax.all_to_all(blocks, axis, 0, 0, tiled=True).reshape(x.shape)
+def step_both(x, by):
+    lats, lons = lax.axis_size("lat"), lax.axis_size("lon")
+    pairs = [
+        (i * lons + j, (i + by) % lats * lons + (j + by) % lons)
+        for i in range(lats)
+        for j in range(lons)
+    ]
+    return lax.ppermute(x, ("lat", "lon"), pairs)
 
 
 def local(
@@ -436,13 +401,12 @@
     block = (LEV, ROWS, COLS)
     d = direction.reshape(block)
     res = residual.reshape(block)
-    band, to_east, to_west, tables = call(
+    own, side, tile = call(
         pack_kernel,
         (
             (ROWS * T_OWN, COLS),
             (ROWS * T_SIDE, COLS),
-            (ROWS * T_SIDE, COLS),
-            (4 * lats, COLS),
+            (4, COLS),
         ),
         (
             pltpu.VMEM((3 * ROWS, COLS), jnp.int32),
@@ -465,44 +429,41 @@
         obs_owner.reshape(2, COLS),
         jnp.transpose(error_inverse, (1, 0, 2)),
     )
-    tables = exchange(tables, "lat")
-    west = step(to_east, "lon", 1)
-    east = step(to_west, "lon", -1)
-    band, tables = call(band_kernel, ((ROWS * T_BAND, COLS), (4 * owners, COLS)))(
-        band, west, east, tables
-    )
-    south = step(band, "lat", 1)
-    tables = exchange(tables, "lon")
+    south = step(own, "lat", 1)
+    west = step(side, "lon", 1)
+    both = step_both(side, 1)
+    (tables,) = call(repeat_kernel, ((4 * owners, COLS),))(tile)
+    tables = lax.all_to_all(
+        tables.reshape(owners, 4, COLS), ("lat", "lon"), 0, 0, tiled=True
+    ).reshape(4 * owners, COLS)
     part, aux, weights, marks = call(
-        functools.partial(pick_kernel, lats, lons),
+        pick_kernel,
         (
-            (fields, PART_ROWS, COLS),
-            (3, ROWS, 2 * COLS),
+            (PART_ROWS, COLS),
+            (3, ROWS, COLS),
             (PADLEV, CANDIDATES),
             ((8, CANDIDATES), jnp.int32),
         ),
-        (
-            (2, T_FIELDS, ROWS, COLS),
-            (PADLEV * ROWS, COLS),
-            (PADLEV * ROWS, COLS),
-        ),
-    )(band, south)
-    parts = lax.all_to_all(part, "obs", 0, 0, tiled=True)
-    (source,) = call(
+        ((2, T_FIELDS, ROWS, COLS), (PADLEV * ROWS, COLS)),
+        flops=20000000000,
+    )(own, west, south, both)
+    parts = lax.all_gather(part, "obs", tiled=True)
+    source, side = call(
         functools.partial(spread_kernel, fields, owners),
-        ((T_BACKS, ROWS, COLS),),
+        ((T_BACK, ROWS, COLS), (T_BACK_SIDE, ROWS, COLS)),
         (
             (PART_ROWS, COLS),
             (2 * PADLEV, owners),
             (2 * PADLEV, SLOTS),
             (PADLEV * ROWS, COLS),
-            (PADLEV * ROWS, COLS),
         ),
     )(parts, tables, weights, marks, aux)
     north = step(source, "lat", -1)
+    east = step(side, "lon", -1)
+    both = step_both(side, -1)
     image, sums = call(
         image_kernel, (block, (fields * lons, COLS)), ((2, T_BACK, ROWS, COLS),)
-    )(source, north, d, res)
+    )(source, east, north, both, d, res)
     sums = lax.all_to_all(sums, ("obs", "lon"), 0, 0, tiled=True)
     (sums,) = call(sum_kernel, ((lats, COLS),))(sums)
     sums = lax.all_to_all(sums, "lat", 0, 0, tiled=True)

time: 108 us -> 94.5 us (0.88)
  blocking collectives: 63.9 us -> 43.2 us
  starting transfers between devices: 22.4 us -> 40.7 us
  waiting for transfers between devices: 11.3 us -> 1.36 us
    all_to_all x2 -> x0, blocking collectives: 33.3 us -> none  [the longest x1 20.9 us: local(): parts = lax.all_to_all(part, 'obs', 0, 0, tiled=True)]
    all_gather x0 -> x1, blocking collectives: none -> 14 us  [local(): parts = lax.all_gather(part, 'obs', tiled=True)]
    ppermute x0 -> x2, starting transfers between devices: none -> 11.5 us  [step_both(): return lax.ppermute(x, ('lat', 'lon'), pairs)]
    ppermute x4, waiting for transfers between devices: 11.3 us -> 1.35 us  [step(): return lax.ppermute(x, axis, [(i, (i + by) % size) for i in range(size)])]
    all_to_all x1, starting transfers between devices: 7.49 us -> 13.6 us  [local(): lax.all_to_all(tables.reshape(owners, 4, COLS), ('lat', 'lon'), 0, 0, til...]
    all_to_all x1, blocking collectives: 21.6 us -> 19.6 us  [local(): sums = lax.all_to_all(sums, ('obs', 'lon'), 0, 0, tiled=True)]
  transfers between devices with their start and end apart: 5 -> 7, of which waited for: 2 -> 1; matrix products, arithmetic and copies ran while one was open for 0% -> 0% of each run, Pallas kernels for 1% -> 2%
where the time goes in v3:
time: 94.5 us; the launch traced here: 94 us
  blocking collectives  43.2 us (46%)
  starting transfers between devices  40.7 us (43%)
  Pallas kernels  7.88 us (8%)
  waiting for transfers between devices  1.36 us (1%)
    all_to_all x1, blocking collectives, local(): sums = lax.all_to_all(sums, ('obs', 'lon'), 0, 0, tiled=True)  19.6 us
    ppermute x4, starting transfers between devices, step(): return lax.ppermute(x, axis, [(i, (i + by) % size) for i in range(size)])  15.6 us
    all_gather x1, blocking collectives, local(): parts = lax.all_gather(part, 'obs', tiled=True)  14 us
    all_to_all x1, starting transfers between devices, local(): lax.all_to_all(tables.reshape(owners, 4, COLS), ('lat', 'lon'), 0, 0, til...  13.6 us
    ppermute x2, starting transfers between devices, step_both(): return lax.ppermute(x, ('lat', 'lon'), pairs)  11.5 us
    all_to_all x1, blocking collectives, local(): sums = lax.all_to_all(sums, 'lat', 0, 0, tiled=True)  9.61 us
    pallas_call x7, Pallas kernels, call(): pl.pallas_call(kernel, out_shape=tuple((shape_of(out) for out in outs)),...  7.88 us
  transfers between devices with their start and end apart: 7, of which 1 were waited for; matrix products, arithmetic and copies ran while one was open for 0% of the time, Pallas kernels for 2%

profile of v3, /device:TPU:1, one launch (start us, length us, event | category | flops | bytes accessed | tf_op | source)
XLA Modules:
  0.0 94.0 jit_solution(3241819626374399559)
XLA Ops:
  0.6 1.9 %shard_map.130 = (f32[288,128]{1,0:T(8,128)}, f32[72,128]{1,0:T(8,128)}, f32[4,128]{1,0:T(4,128)}) custom-call(f32[200,128]{1,0:T(8,128)} %bitcast.23, s32[8,128]{1,0:T(8,128)} %flag.1, f32[8,128]{1,0:T(8,128)} %east.1, f32[8,128]{1,0:T(8,128)} %north.1, f32[8,128]{1,0:T(8,128)} %bitcast.35, f32[25,1,256]{2,1,0:T(1,128)} %bitcast.33, s32[2,128]{1,0:T(2,128)} %bitcast.36, ...), custom_call_target="tpu_custom_call" | custom-call | flops 1000000 | bytes 1000000 | tf_op jit(solution)/shard_map/pallas_call | solution.py:360
  2.6 0.0 copy-start.3
  2.6 4.8 %collective-permute-start.1 = (f32[288,128]{1,0:T(8,128)}, f32[288,128]{1,0:T(8,128)S(1)}, u32[]{:S(2)}, u32[]{:S(2)}) collective-permute-start(f32[288,128]{1,0:T(8,128)} %get-tuple-element.17.own), channel_id=1, source_target_pairs={{0,64},{64,128},{128,192},{192,256},{256,320},{320,384},{384,448},... | collective-permute-start | bytes 442376 | tf_op jit(solution)/shard_map/ppermute | solution.py:373
  7.4 5.8 %collective-permute-start.2 = (f32[72,128]{1,0:T(8,128)}, f32[72,128]{1,0:T(8,128)S(1)}, u32[]{:S(2)}, u32[]{:S(2)}) collective-permute-start(f32[72,128]{1,0:T(8,128)} %get-tuple-element.18), channel_id=1, source_target_pairs={{0,68},{4,72},{8,76},{12,80},{16,84},{20,88},{24,92},{28,96},{32,1... | collective-permute-start | bytes 110600 | tf_op jit(solution)/shard_map/ppermute | solution.py:383
  13.2 1.9 %collective-permute-start = (f32[72,128]{1,0:T(8,128)}, f32[72,128]{1,0:T(8,128)S(1)}, u32[]{:S(2)}, u32[]{:S(2)}) collective-permute-start(f32[72,128]{1,0:T(8,128)} %get-tuple-element.18), channel_id=1, source_target_pairs={{0,4},{4,8},{8,12},{12,16},{16,20},{20,24},{24,28},{28,32},{32,36}... | collective-permute-start | bytes 110600 | tf_op jit(solution)/shard_map/ppermute | solution.py:373
  15.1 0.7 shard_map.132
  15.9 13.6 %all-to-all-start = ((f32[128,4,128]{2,1,0:T(4,128)}), f32[128,4,128]{2,1,0:T(4,128)S(1)}, u32[]{:S(2)}, u32[]{:S(2)}) async-start(f32[128,4,128]{2,1,0:T(4,128)} %bitcast.6), calls=%async_computation | async-start | bytes 524288 | tf_op jit(solution)/shard_map/all_to_all | solution.py:436
  29.5 0.0 collective-permute-done.2.both
  29.5 0.0 collective-permute-done.west
  29.5 0.0 collective-permute-done.1.south
  29.5 1.6 %shard_map.131 = (f32[200,128]{1,0:T(8,128)S(1)}, f32[3,8,128]{2,1,0:T(8,128)S(1)}, f32[32,1024]{1,0:T(8,128)S(1)}, s32[8,1024]{1,0:T(8,128)S(1)}) custom-call(f32[288,128]{1,0:T(8,128)S(1)} %copy-done.4, f32[72,128]{1,0:T(8,128)S(1)} %collective-permute-done.west, f32[288,128]{1,0:T(8,128)S(1)} %collective-permute-done.1.south, ...), custom_call_target="tpu_custom_call" | custom-call | flops 20000000000 | bytes 1000000 | tf_op jit(solution)/shard_map/pallas_call | solution.py:360
  31.1 14.0 %all_gather.3.parts = f32[800,128]{1,0:T(8,128)S(1)} all-gather(f32[200,128]{1,0:T(8,128)S(1)} %get-tuple-element.19), channel_id=1, replica_groups=mesh['lat'=8,'lon'=16,'obs'=4] {'obs'}, dimensions={0}, use_global_device_ids=true | all-gather | bytes 512000 | tf_op jit(solution)/shard_map/all_gather | solution.py:450
  45.1 0.0 all-to-all-done
  45.2 1.2 %shard_map.133 = (f32[27,8,128]{2,1,0:T(8,128)S(1)}, f32[2,8,128]{2,1,0:T(8,128)S(1)}) custom-call(f32[800,128]{1,0:T(8,128)S(1)} %all_gather.3.parts, f32[512,128]{1,0:T(8,128)S(1)} %bitcast.22, f32[32,1024]{1,0:T(8,128)S(1)} %get-tuple-element.21.weights, s32[8,1024]{1,0:T(8,128)S(1)} %get-tuple-element.22.marks, f32[3,8,128]{2,1,0:T(8,128)S(1)} %get-tuple-element.23.aux), custom_call_target="tpu_custom_call" | custom-call | flops 1000000 | bytes 1000000 | tf_op jit(solution)/shard_map/pallas_call | solution.py:360
  46.4 5.2 %collective-permute-start.4 = (f32[27,8,128]{2,1,0:T(8,128)S(1)}, f32[27,8,128]{2,1,0:T(8,128)S(1)}, u32[]{:S(2)}, u32[]{:S(2)}) collective-permute-start(f32[27,8,128]{2,1,0:T(8,128)S(1)} %get-tuple-element.24.own), channel_id=1, source_target_pairs={{0,448},{64,0},{128,64},{192,128},{256,192},{320,256},{384,320},{4... | collective-permute-start | bytes 331784 | tf_op jit(solution)/shard_map/ppermute | solution.py:373
  51.6 5.7 %collective-permute-start.5 = (f32[2,8,128]{2,1,0:T(8,128)S(1)}, f32[2,8,128]{2,1,0:T(8,128)S(1)}, u32[]{:S(2)}, u32[]{:S(2)}) collective-permute-start(f32[2,8,128]{2,1,0:T(8,128)S(1)} %get-tuple-element.25), channel_id=1, source_target_pairs={{0,508},{4,448},{8,452},{12,456},{16,460},{20,464},{24,468},{28,47... | collective-permute-start | bytes 24584 | tf_op jit(solution)/shard_map/ppermute | solution.py:383
  57.3 3.6 %collective-permute-start.3 = (f32[2,8,128]{2,1,0:T(8,128)S(1)}, f32[2,8,128]{2,1,0:T(8,128)S(1)}, u32[]{:S(2)}, u32[]{:S(2)}) collective-permute-start(f32[2,8,128]{2,1,0:T(8,128)S(1)} %get-tuple-element.25), channel_id=1, source_target_pairs={{0,60},{4,0},{8,4},{12,8},{16,12},{20,16},{24,20},{28,24},{32,28},... | collective-permute-start | bytes 24584 | tf_op jit(solution)/shard_map/ppermute | solution.py:373
  61.0 0.0 collective-permute-done.5.both
  61.0 1.3 %collective-permute-done.3.east = f32[2,8,128]{2,1,0:T(8,128)S(1)} collective-permute-done((f32[2,8,128]{2,1,0:T(8,128)S(1)}, f32[2,8,128]{2,1,0:T(8,128)S(1)}, u32[]{:S(2)}, u32[]{:S(2)}) %collective-permute-start.3) | collective-permute-done | bytes 8224 | tf_op jit(solution)/shard_map/ppermute | solution.py:373
  62.3 1.6 %shard_map.134 = (f32[25,8,128]{2,1,0:T(8,128)S(1)}, f32[64,128]{1,0:T(8,128)S(1)}) custom-call(f32[27,8,128]{2,1,0:T(8,128)S(1)} %get-tuple-element.24.own, f32[2,8,128]{2,1,0:T(8,128)S(1)} %collective-permute-done.3.east, f32[27,8,128]{2,1,0:T(8,128)S(1)} %collective-permute-done.4.north, f32[2,8,128]{2,1,0:T(8,128)S(1)} %collective-permute-done.5.both, ...), custom_call_target="tpu_custom_call" | custom-call | flops 1000000 | bytes 1000000 | tf_op jit(solution)/shard_map/pallas_call | solution.py:360
  63.9 0.0 copy-start.2
  63.9 19.6 %all_to_all.27 = f32[64,1,128]{2,1,0:T(1,128)S(1)} all-to-all(f32[64,1,128]{2,1,0:T(1,128)S(1)} %bitcast.30), channel_id=1, replica_groups=mesh['lat'=8,'lon'=16,'obs'=4] {'obs','lon'}, dimensions={0} | all-to-all | bytes 65536 | tf_op jit(solution)/shard_map/all_to_all | solution.py:467
  83.5 9.6 %all_to_all.28 = f32[8,1,128]{2,1,0:T(1,128)S(1)} all-to-all(f32[8,1,128]{2,1,0:T(1,128)S(1)} %bitcast.32), channel_id=1, replica_groups=mesh['lat'=8,'lon'=16,'obs'=4] {'lat'}, dimensions={0} | all-to-all | bytes 8192 | tf_op jit(solution)/shard_map/all_to_all | solution.py:469
  93.2 0.8 shard_map.136
  (10 shorter events, 0.0 us)
Async XLA Ops:
  2.6 12.6 %copy-start.3 = (f32[4,128]{1,0:T(4,128)S(1)}, f32[4,128]{1,0:T(4,128)}, u32[]{:S(2)}) copy-start(f32[4,128]{1,0:T(4,128)} %get-tuple-element.20.tile) | copy-start | bytes 6148
  2.6 26.9 %collective-permute-start.1 = (f32[288,128]{1,0:T(8,128)}, f32[288,128]{1,0:T(8,128)S(1)}, u32[]{:S(2)}, u32[]{:S(2)}) collective-permute-start(f32[288,128]{1,0:T(8,128)} %get-tuple-element.17.own), channel_id=1, source_target_pairs={{0,64},{64,128},{128,192},{192,256},{256,320},{320,384},{384,448},... | collective-permute-start | bytes 442376 | tf_op jit(solution)/shard_map/ppermute | solution.py:373
  7.4 22.1 %collective-permute-start.2 = (f32[72,128]{1,0:T(8,128)}, f32[72,128]{1,0:T(8,128)S(1)}, u32[]{:S(2)}, u32[]{:S(2)}) collective-permute-start(f32[72,128]{1,0:T(8,128)} %get-tuple-element.18), channel_id=1, source_target_pairs={{0,68},{4,72},{8,76},{12,80},{16,84},{20,88},{24,92},{28,96},{32,1... | collective-permute-start | bytes 110600 | tf_op jit(solution)/shard_map/ppermute | solution.py:383
  13.2 16.3 %collective-permute-start = (f32[72,128]{1,0:T(8,128)}, f32[72,128]{1,0:T(8,128)S(1)}, u32[]{:S(2)}, u32[]{:S(2)}) collective-permute-start(f32[72,128]{1,0:T(8,128)} %get-tuple-element.18), channel_id=1, source_target_pairs={{0,4},{4,8},{8,12},{12,16},{16,20},{20,24},{24,28},{28,32},{32,36}... | collective-permute-start | bytes 110600 | tf_op jit(solution)/shard_map/ppermute | solution.py:373
  15.9 13.7 %copy-start.4 = (f32[288,128]{1,0:T(8,128)S(1)}, f32[288,128]{1,0:T(8,128)}, u32[]{:S(2)}) copy-start(f32[288,128]{1,0:T(8,128)} %get-tuple-element.17.own) | copy-start | bytes 442372
  15.9 29.3 %all-to-all-start = ((f32[128,4,128]{2,1,0:T(4,128)}), f32[128,4,128]{2,1,0:T(4,128)S(1)}, u32[]{:S(2)}, u32[]{:S(2)}) async-start(f32[128,4,128]{2,1,0:T(4,128)} %bitcast.6), calls=%async_computation | async-start | bytes 524288 | tf_op jit(solution)/shard_map/all_to_all | solution.py:436
  45.1 17.2 %copy-start = (f32[1,25,8,128]{3,2,1,0:T(8,128)S(1)}, f32[1,25,8,128]{3,2,1,0:T(8,128)}, u32[]{:S(2)}) copy-start(f32[1,25,8,128]{3,2,1,0:T(8,128)} %param.13) | copy-start | bytes 307204
  45.2 17.2 %copy-start.1 = (f32[1,25,8,128]{3,2,1,0:T(8,128)S(1)}, f32[1,25,8,128]{3,2,1,0:T(8,128)}, u32[]{:S(2)}) copy-start(f32[1,25,8,128]{3,2,1,0:T(8,128)} %param.12) | copy-start | bytes 307204
  46.4 15.9 %collective-permute-start.4 = (f32[27,8,128]{2,1,0:T(8,128)S(1)}, f32[27,8,128]{2,1,0:T(8,128)S(1)}, u32[]{:S(2)}, u32[]{:S(2)}) collective-permute-start(f32[27,8,128]{2,1,0:T(8,128)S(1)} %get-tuple-element.24.own), channel_id=1, source_target_pairs={{0,448},{64,0},{128,64},{192,128},{256,192},{320,256},{384,320},{4... | collective-permute-start | bytes 331784 | tf_op jit(solution)/shard_map/ppermute | solution.py:373
  51.6 9.3 %collective-permute-start.5 = (f32[2,8,128]{2,1,0:T(8,128)S(1)}, f32[2,8,128]{2,1,0:T(8,128)S(1)}, u32[]{:S(2)}, u32[]{:S(2)}) collective-permute-start(f32[2,8,128]{2,1,0:T(8,128)S(1)} %get-tuple-element.25), channel_id=1, source_target_pairs={{0,508},{4,448},{8,452},{12,456},{16,460},{20,464},{24,468},{28,47... | collective-permute-start | bytes 24584 | tf_op jit(solution)/shard_map/ppermute | solution.py:383
  57.3 5.0 %collective-permute-start.3 = (f32[2,8,128]{2,1,0:T(8,128)S(1)}, f32[2,8,128]{2,1,0:T(8,128)S(1)}, u32[]{:S(2)}, u32[]{:S(2)}) collective-permute-start(f32[2,8,128]{2,1,0:T(8,128)S(1)} %get-tuple-element.25), channel_id=1, source_target_pairs={{0,60},{4,0},{8,4},{12,8},{16,12},{20,16},{24,20},{28,24},{32,28},... | collective-permute-start | bytes 24584 | tf_op jit(solution)/shard_map/ppermute | solution.py:373
  63.9 29.3 %copy-start.2 = (f32[1,25,8,128]{3,2,1,0:T(8,128)S(1)}, f32[1,25,8,128]{3,2,1,0:T(8,128)}, u32[]{:S(2)}) copy-start(f32[1,25,8,128]{3,2,1,0:T(8,128)} %param.11) | copy-start | bytes 307204

commit v4 on v3

--- a/solution.py
+++ b/solution.py
@@ -132,7 +132,7 @@
 
 def pack_kernel(
     d, flag, east, north, sigma, weight, cell, owner, table,
-    band, side, tile,
+    band, side, tables,
     whole, lines, matrix, wide, turned, sems,
 ):
     obs = ROWS * T_FIELDS
@@ -164,18 +164,27 @@
     for i, packed in enumerate(pack_edges(tiles, COLS - EDGE)):
         side[ROWS * i : ROWS * (i + 1), :] = packed
     side[ROWS * T_EDGES :, :] = band[obs : ROWS * T_OWN, :]
-    tile[...] = diagonals(matrix, wide, turned)
-
-
-def repeat_kernel(tile, tables):
-    pair = jnp.concatenate([tile[...], tile[...]], axis=0)
-    for i in range(tables.shape[0] // ROWS):
-        tables[ROWS * i : ROWS * (i + 1), :] = pair
-
-
-def pick_kernel(
-    own, west, south, both, part, aux, weights, marks, edges, held
-):
+    tile = diagonals(matrix, wide, turned)
+    for i in range(tables.shape[0] // 4):
+        tables[4 * i : 4 * i + 4, :] = tile
+
+
+def band_kernel(given, west, out, sem):
+    del given
+    copy = pltpu.make_async_copy(west, out.at[pl.ds(ROWS * T_OWN, ROWS * T_SIDE), :], sem)
+    copy.start()
+    copy.wait()
+
+
+def repeat_kernel(given, tables):
+    count = given.shape[0]
+    for i in range(tables.shape[0] // count):
+        tables[count * i : count * (i + 1), :] = given[...]
+
+
+def pick_kernel(lats, lons, own, south, part, aux, weights, marks, edges, held):
+    west = own.at[pl.ds(ROWS * T_OWN, ROWS * T_SIDE), :]
+    both = south.at[pl.ds(ROWS * T_OWN, ROWS * T_SIDE), :]
     lane = lanes()
     for b, side in enumerate((both, west)):
         for t in range(T_FIELDS):
@@ -226,7 +235,7 @@
         cell = side_by_side(band[obs + R_CELL : obs + R_CELL + 2, :].astype(jnp.int32))
         marks[0:1, columns] = place(cell, b >= 2, b % 2)
         owner = side_by_side(band[obs + R_OWNER : obs + R_OWNER + 2, :].astype(jnp.int32))
-        marks[1:2, columns] = owner
+        marks[1:2, columns] = owner % lons * lats + owner // lons
 
     for half in (0, 1):
         first = SHIFT * (1 - half)
@@ -373,6 +382,12 @@
     return lax.ppermute(x, axis, [(i, (i + by) % size) for i in range(size)])
 
 
+def exchange(x, axis):
+    size = lax.axis_size(axis)
+    blocks = x.reshape(size, x.shape[0] // size, COLS)
+    return lax.all_to_all(blocks, axis, 0, 0, tiled=True).reshape(x.shape)
+
+
 def step_both(x, by):
     lats, lons = lax.axis_size("lat"), lax.axis_size("lon")
     pairs = [
@@ -401,12 +416,12 @@
     block = (LEV, ROWS, COLS)
     d = direction.reshape(block)
     res = residual.reshape(block)
-    own, side, tile = call(
+    own, side, tables = call(
         pack_kernel,
         (
-            (ROWS * T_OWN, COLS),
+            (ROWS * (T_OWN + T_SIDE), COLS),
             (ROWS * T_SIDE, COLS),
-            (4, COLS),
+            (4 * lats, COLS),
         ),
         (
             pltpu.VMEM((3 * ROWS, COLS), jnp.int32),
@@ -429,15 +444,22 @@
         obs_owner.reshape(2, COLS),
         jnp.transpose(error_inverse, (1, 0, 2)),
     )
-    south = step(own, "lat", 1)
     west = step(side, "lon", 1)
-    both = step_both(side, 1)
-    (tables,) = call(repeat_kernel, ((4 * owners, COLS),))(tile)
-    tables = lax.all_to_all(
-        tables.reshape(owners, 4, COLS), ("lat", "lon"), 0, 0, tiled=True
-    ).reshape(4 * owners, COLS)
+    tables = exchange(tables, "lat")
+    band = pl.pallas_call(
+        band_kernel,
+        out_shape=jax.ShapeDtypeStruct(own.shape, jnp.float32),
+        in_specs=[ANY, ANY],
+        out_specs=ANY,
+        scratch_shapes=[pltpu.SemaphoreType.DMA],
+        input_output_aliases={0: 0},
+        compiler_params=pltpu.CompilerParams(vmem_limit_bytes=LIMIT),
+    )(own, west)
+    south = step(band, "lat", 1)
+    (tables,) = call(repeat_kernel, ((4 * owners, COLS),), flops=20000000000)(tables)
+    tables = exchange(tables, "lon")
     part, aux, weights, marks = call(
-        pick_kernel,
+        functools.partial(pick_kernel, lats, lons),
         (
             (PART_ROWS, COLS),
             (3, ROWS, COLS),
@@ -446,7 +468,7 @@
         ),
         ((2, T_FIELDS, ROWS, COLS), (PADLEV * ROWS, COLS)),
         flops=20000000000,
-    )(own, west, south, both)
+    )(band, south)
     parts = lax.all_gather(part, "obs", tiled=True)
     source, side = call(
         functools.partial(spread_kernel, fields, owners),

time: 94.5 us -> 94.3 us (level)
  starting transfers between devices: 40.7 us -> 33.5 us
  waiting for transfers between devices: 1.36 us -> 5.58 us
  Pallas kernels: 7.88 us -> 9.43 us
  blocking collectives: 43.2 us -> 44.5 us
    ppermute x2 -> x1, starting transfers between devices: 11.5 us -> 5.76 us  [step_both(): return lax.ppermute(x, ('lat', 'lon'), pairs)]
    ppermute x4, starting transfers between devices: 15.6 us -> 12 us  [step(): return lax.ppermute(x, axis, [(i, (i + by) % size) for i in range(size)])]
    all_to_all x1 -> x2, waiting for transfers between devices: 0.01 us -> 2.8 us  [exchange(): return lax.all_to_all(blocks, axis, 0, 0, tiled=True).reshape(x.shape)]
    all_to_all x1 -> x2, starting transfers between devices: 13.6 us -> 15.7 us  [exchange(): return lax.all_to_all(blocks, axis, 0, 0, tiled=True).reshape(x.shape)]
    ppermute x4, waiting for transfers between devices: 1.35 us -> 2.78 us  [step(): return lax.ppermute(x, axis, [(i, (i + by) % size) for i in range(size)])]
    all_to_all x1, blocking collectives: 9.61 us -> 11 us  [local(): sums = lax.all_to_all(sums, 'lat', 0, 0, tiled=True)]
    all_to_all x1, blocking collectives: 19.6 us -> 18.4 us  [local(): sums = lax.all_to_all(sums, ('obs', 'lon'), 0, 0, tiled=True)]
    all_gather x1, blocking collectives: 14 us -> 15.1 us  [local(): parts = lax.all_gather(part, 'obs', tiled=True)]
  transfers between devices with their start and end apart: 7 -> 7, of which waited for: 1 -> 2; matrix products, arithmetic and copies ran while one was open for 0% -> 0% of each run, Pallas kernels for 2% -> 4%
where the time goes in v4:
time: 94.3 us; the launch traced here: 93.7 us
  blocking collectives  44.5 us (47%)
  starting transfers between devices  33.5 us (36%)
  Pallas kernels  9.43 us (10%)
  waiting for transfers between devices  5.58 us (6%)
    all_to_all x1, blocking collectives, local(): sums = lax.all_to_all(sums, ('obs', 'lon'), 0, 0, tiled=True)  18.4 us
    all_to_all x2, starting transfers between devices, exchange(): return lax.all_to_all(blocks, axis, 0, 0, tiled=True).reshape(x.shape)  15.7 us
    all_gather x1, blocking collectives, local(): parts = lax.all_gather(part, 'obs', tiled=True)  15.1 us
    ppermute x4, starting transfers between devices, step(): return lax.ppermute(x, axis, [(i, (i + by) % size) for i in range(size)])  12 us
    all_to_all x1, blocking collectives, local(): sums = lax.all_to_all(sums, 'lat', 0, 0, tiled=True)  11 us
    pallas_call x7, Pallas kernels, call(): pl.pallas_call(kernel, out_shape=tuple((shape_of(out) for out in outs)),...  8.81 us
    ppermute x1, starting transfers between devices, step_both(): return lax.ppermute(x, ('lat', 'lon'), pairs)  5.76 us
    all_to_all x2, waiting for transfers between devices, exchange(): return lax.all_to_all(blocks, axis, 0, 0, tiled=True).reshape(x.shape)  2.8 us
  transfers between devices with their start and end apart: 7, of which 2 were waited for; matrix products, arithmetic and copies ran while one was open for 0% of the time, Pallas kernels for 4%

profile of v4, /device:TPU:1, one launch (start us, length us, event | category | flops | bytes accessed | tf_op | source)
XLA Modules:
  0.0 93.7 jit_solution(4658090447119144081)
XLA Ops:
  0.6 1.9 %shard_map.130 = (f32[360,128]{1,0:T(8,128)}, f32[72,128]{1,0:T(8,128)}, f32[32,128]{1,0:T(8,128)}) custom-call(f32[200,128]{1,0:T(8,128)} %bitcast.25, s32[8,128]{1,0:T(8,128)} %flag.1, f32[8,128]{1,0:T(8,128)} %east.1, f32[8,128]{1,0:T(8,128)} %north.1, f32[8,128]{1,0:T(8,128)} %bitcast.39, f32[25,1,256]{2,1,0:T(1,128)} %bitcast.36, s32[2,128]{1,0:T(2,128)} %bitcast.40, ...), custom_call_target="tpu_custom_call" | custom-call | flops 1000000 | bytes 1000000 | tf_op jit(solution)/shard_map/pallas_call | solution.py:369
  2.6 4.5 %collective-permute-start = (f32[72,128]{1,0:T(8,128)}, f32[72,128]{1,0:T(8,128)S(1)}, u32[]{:S(2)}, u32[]{:S(2)}) collective-permute-start(f32[72,128]{1,0:T(8,128)} %get-tuple-element.18), channel_id=1, source_target_pairs={{0,4},{4,8},{8,12},{12,16},{16,20},{20,24},{24,28},{28,32},{32,36}... | collective-permute-start | bytes 110600 | tf_op jit(solution)/shard_map/ppermute | solution.py:382
  7.1 10.0 %all-to-all-start = ((f32[8,4,128]{2,1,0:T(4,128)}), f32[8,4,128]{2,1,0:T(4,128)S(1)}, u32[]{:S(2)}, u32[]{:S(2)}) async-start(f32[8,4,128]{2,1,0:T(4,128)} %bitcast.37), calls=%async_computation | async-start | bytes 32768 | tf_op jit(solution)/shard_map/all_to_all | solution.py:388
  17.1 0.0 collective-permute-done.west
  17.2 0.6 shard_map.131.own
  17.8 3.4 %collective-permute-start.1 = (f32[360,128]{1,0:T(8,128)}, f32[360,128]{1,0:T(8,128)S(1)}, u32[]{:S(2)}, u32[]{:S(2)}) collective-permute-start(f32[360,128]{1,0:T(8,128)} %shard_map.131.own), channel_id=1, source_target_pairs={{0,64},{64,128},{128,192},{192,256},{256,320},{320,384},{384,448},... | collective-permute-start | bytes 552968 | tf_op jit(solution)/shard_map/ppermute | solution.py:382
  21.2 2.8 %all-to-all-done = f32[8,4,128]{2,1,0:T(4,128)S(1)} async-done(((f32[8,4,128]{2,1,0:T(4,128)}), f32[8,4,128]{2,1,0:T(4,128)S(1)}, u32[]{:S(2)}, u32[]{:S(2)}) %all-to-all-start) | async-done | bytes 16416 | tf_op jit(solution)/shard_map/all_to_all | solution.py:388
  24.0 0.7 shard_map.133
  24.7 5.7 %all-to-all-start.1 = ((f32[16,32,128]{2,1,0:T(8,128)}), f32[16,32,128]{2,1,0:T(8,128)S(1)}, u32[]{:S(2)}, u32[]{:S(2)}) async-start(f32[16,32,128]{2,1,0:T(8,128)} %bitcast.8), calls=%async_computation.1 | async-start | bytes 524288 | tf_op jit(solution)/shard_map/all_to_all | solution.py:388
  30.4 0.0 collective-permute-done.1.south
  30.4 2.5 %shard_map.132 = (f32[200,128]{1,0:T(8,128)S(1)}, f32[3,8,128]{2,1,0:T(8,128)S(1)}, f32[32,1024]{1,0:T(8,128)S(1)}, s32[8,1024]{1,0:T(8,128)S(1)}) custom-call(f32[360,128]{1,0:T(8,128)} %shard_map.131.own, f32[360,128]{1,0:T(8,128)S(1)} %collective-permute-done.1.south), custom_call_target="tpu_custom_call" | custom-call | flops 20000000000 | bytes 1000000 | tf_op jit(solution)/shard_map/pallas_call | solution.py:369
  32.9 15.1 %all_gather.3.parts = f32[800,128]{1,0:T(8,128)S(1)} all-gather(f32[200,128]{1,0:T(8,128)S(1)} %get-tuple-element.19), channel_id=1, replica_groups=mesh['lat'=8,'lon'=16,'obs'=4] {'obs'}, dimensions={0}, use_global_device_ids=true | all-gather | bytes 512000 | tf_op jit(solution)/shard_map/all_gather | solution.py:472
  48.0 1.2 %shard_map.134 = (f32[27,8,128]{2,1,0:T(8,128)S(1)}, f32[2,8,128]{2,1,0:T(8,128)S(1)}) custom-call(f32[800,128]{1,0:T(8,128)S(1)} %all_gather.3.parts, f32[512,128]{1,0:T(8,128)S(1)} %bitcast.24, f32[32,1024]{1,0:T(8,128)S(1)} %get-tuple-element.21.weights, s32[8,1024]{1,0:T(8,128)S(1)} %get-tuple-element.22.marks, f32[3,8,128]{2,1,0:T(8,128)S(1)} %get-tuple-element.23.aux), custom_call_target="tpu_custom_call" | custom-call | flops 1000000 | bytes 1000000 | tf_op jit(solution)/shard_map/pallas_call | solution.py:369
  49.2 1.9 %collective-permute-start.3 = (f32[27,8,128]{2,1,0:T(8,128)S(1)}, f32[27,8,128]{2,1,0:T(8,128)S(1)}, u32[]{:S(2)}, u32[]{:S(2)}) collective-permute-start(f32[27,8,128]{2,1,0:T(8,128)S(1)} %get-tuple-element.24.own), channel_id=1, source_target_pairs={{0,448},{64,0},{128,64},{192,128},{256,192},{320,256},{384,320},{4... | collective-permute-start | bytes 331784 | tf_op jit(solution)/shard_map/ppermute | solution.py:382
  51.1 5.8 %collective-permute-start.4 = (f32[2,8,128]{2,1,0:T(8,128)S(1)}, f32[2,8,128]{2,1,0:T(8,128)S(1)}, u32[]{:S(2)}, u32[]{:S(2)}) collective-permute-start(f32[2,8,128]{2,1,0:T(8,128)S(1)} %get-tuple-element.25), channel_id=1, source_target_pairs={{0,508},{4,448},{8,452},{12,456},{16,460},{20,464},{24,468},{28,47... | collective-permute-start | bytes 24584 | tf_op jit(solution)/shard_map/ppermute | solution.py:398
  56.9 2.2 %collective-permute-start.2 = (f32[2,8,128]{2,1,0:T(8,128)S(1)}, f32[2,8,128]{2,1,0:T(8,128)S(1)}, u32[]{:S(2)}, u32[]{:S(2)}) collective-permute-start(f32[2,8,128]{2,1,0:T(8,128)S(1)} %get-tuple-element.25), channel_id=1, source_target_pairs={{0,60},{4,0},{8,4},{12,8},{16,12},{20,16},{24,20},{28,24},{32,28},... | collective-permute-start | bytes 24584 | tf_op jit(solution)/shard_map/ppermute | solution.py:382
  59.1 0.0 collective-permute-done.4.both
  59.1 2.8 %collective-permute-done.2.east = f32[2,8,128]{2,1,0:T(8,128)S(1)} collective-permute-done((f32[2,8,128]{2,1,0:T(8,128)S(1)}, f32[2,8,128]{2,1,0:T(8,128)S(1)}, u32[]{:S(2)}, u32[]{:S(2)}) %collective-permute-start.2) | collective-permute-done | bytes 8224 | tf_op jit(solution)/shard_map/ppermute | solution.py:382
  61.9 0.0 collective-permute-done.3.north
  61.9 1.6 %shard_map.135 = (f32[25,8,128]{2,1,0:T(8,128)S(1)}, f32[64,128]{1,0:T(8,128)S(1)}) custom-call(f32[27,8,128]{2,1,0:T(8,128)S(1)} %get-tuple-element.24.own, f32[2,8,128]{2,1,0:T(8,128)S(1)} %collective-permute-done.2.east, f32[27,8,128]{2,1,0:T(8,128)S(1)} %collective-permute-done.3.north, f32[2,8,128]{2,1,0:T(8,128)S(1)} %collective-permute-done.4.both, ...), custom_call_target="tpu_custom_call" | custom-call | flops 1000000 | bytes 1000000 | tf_op jit(solution)/shard_map/pallas_call | solution.py:369
  63.5 0.0 copy-start.2
  63.5 18.4 %all_to_all.32 = f32[64,1,128]{2,1,0:T(1,128)S(1)} all-to-all(f32[64,1,128]{2,1,0:T(1,128)S(1)} %bitcast.32), channel_id=1, replica_groups=mesh['lat'=8,'lon'=16,'obs'=4] {'obs','lon'}, dimensions={0} | all-to-all | bytes 65536 | tf_op jit(solution)/shard_map/all_to_all | solution.py:489
  81.9 11.0 %all_to_all.33 = f32[8,1,128]{2,1,0:T(1,128)S(1)} all-to-all(f32[8,1,128]{2,1,0:T(1,128)S(1)} %bitcast.34), channel_id=1, replica_groups=mesh['lat'=8,'lon'=16,'obs'=4] {'lat'}, dimensions={0} | all-to-all | bytes 8192 | tf_op jit(solution)/shard_map/all_to_all | solution.py:491
  92.9 0.8 shard_map.137
  (7 shorter events, 0.0 us)
Async XLA Ops:
  2.6 14.6 %collective-permute-start = (f32[72,128]{1,0:T(8,128)}, f32[72,128]{1,0:T(8,128)S(1)}, u32[]{:S(2)}, u32[]{:S(2)}) collective-permute-start(f32[72,128]{1,0:T(8,128)} %get-tuple-element.18), channel_id=1, source_target_pairs={{0,4},{4,8},{8,12},{12,16},{16,20},{20,24},{24,28},{28,32},{32,36}... | collective-permute-start | bytes 110600 | tf_op jit(solution)/shard_map/ppermute | solution.py:382
  7.1 16.9 %all-to-all-start = ((f32[8,4,128]{2,1,0:T(4,128)}), f32[8,4,128]{2,1,0:T(4,128)S(1)}, u32[]{:S(2)}, u32[]{:S(2)}) async-start(f32[8,4,128]{2,1,0:T(4,128)} %bitcast.37), calls=%async_computation | async-start | bytes 32768 | tf_op jit(solution)/shard_map/all_to_all | solution.py:388
  17.8 12.6 %collective-permute-start.1 = (f32[360,128]{1,0:T(8,128)}, f32[360,128]{1,0:T(8,128)S(1)}, u32[]{:S(2)}, u32[]{:S(2)}) collective-permute-start(f32[360,128]{1,0:T(8,128)} %shard_map.131.own), channel_id=1, source_target_pairs={{0,64},{64,128},{128,192},{192,256},{256,320},{320,384},{384,448},... | collective-permute-start | bytes 552968 | tf_op jit(solution)/shard_map/ppermute | solution.py:382
  24.7 23.3 %all-to-all-start.1 = ((f32[16,32,128]{2,1,0:T(8,128)}), f32[16,32,128]{2,1,0:T(8,128)S(1)}, u32[]{:S(2)}, u32[]{:S(2)}) async-start(f32[16,32,128]{2,1,0:T(8,128)} %bitcast.8), calls=%async_computation.1 | async-start | bytes 524288 | tf_op jit(solution)/shard_map/all_to_all | solution.py:388
  48.0 13.9 %copy-start = (f32[1,25,8,128]{3,2,1,0:T(8,128)S(1)}, f32[1,25,8,128]{3,2,1,0:T(8,128)}, u32[]{:S(2)}) copy-start(f32[1,25,8,128]{3,2,1,0:T(8,128)} %param.13) | copy-start | bytes 307204
  48.0 13.9 %copy-start.1 = (f32[1,25,8,128]{3,2,1,0:T(8,128)S(1)}, f32[1,25,8,128]{3,2,1,0:T(8,128)}, u32[]{:S(2)}) copy-start(f32[1,25,8,128]{3,2,1,0:T(8,128)} %param.12) | copy-start | bytes 307204
  49.2 12.7 %collective-permute-start.3 = (f32[27,8,128]{2,1,0:T(8,128)S(1)}, f32[27,8,128]{2,1,0:T(8,128)S(1)}, u32[]{:S(2)}, u32[]{:S(2)}) collective-permute-start(f32[27,8,128]{2,1,0:T(8,128)S(1)} %get-tuple-element.24.own), channel_id=1, source_target_pairs={{0,448},{64,0},{128,64},{192,128},{256,192},{320,256},{384,320},{4... | collective-permute-start | bytes 331784 | tf_op jit(solution)/shard_map/ppermute | solution.py:382
  51.1 8.0 %collective-permute-start.4 = (f32[2,8,128]{2,1,0:T(8,128)S(1)}, f32[2,8,128]{2,1,0:T(8,128)S(1)}, u32[]{:S(2)}, u32[]{:S(2)}) collective-permute-start(f32[2,8,128]{2,1,0:T(8,128)S(1)} %get-tuple-element.25), channel_id=1, source_target_pairs={{0,508},{4,448},{8,452},{12,456},{16,460},{20,464},{24,468},{28,47... | collective-permute-start | bytes 24584 | tf_op jit(solution)/shard_map/ppermute | solution.py:398
  56.9 5.0 %collective-permute-start.2 = (f32[2,8,128]{2,1,0:T(8,128)S(1)}, f32[2,8,128]{2,1,0:T(8,128)S(1)}, u32[]{:S(2)}, u32[]{:S(2)}) collective-permute-start(f32[2,8,128]{2,1,0:T(8,128)S(1)} %get-tuple-element.25), channel_id=1, source_target_pairs={{0,60},{4,0},{8,4},{12,8},{16,12},{20,16},{24,20},{28,24},{32,28},... | collective-permute-start | bytes 24584 | tf_op jit(solution)/shard_map/ppermute | solution.py:382
  63.5 29.4 %copy-start.2 = (f32[1,25,8,128]{3,2,1,0:T(8,128)S(1)}, f32[1,25,8,128]{3,2,1,0:T(8,128)}, u32[]{:S(2)}) copy-start(f32[1,25,8,128]{3,2,1,0:T(8,128)} %param.11) | copy-start | bytes 307204

commit v5 on v4

--- a/solution.py
+++ b/solution.py
@@ -23,12 +23,12 @@
 PER_TILE = COLS // EDGE
 T_OWN = T_FIELDS + T_OBS
 T_EDGES = -(-T_FIELDS // PER_TILE)
-T_SIDE = T_EDGES + T_OBS
+T_BAND = T_OWN + 2 * T_EDGES
 T_BACK = LEV + 2
-T_BACK_SIDE = -(-T_BACK // PER_TILE)
-BLOCKS = 4
+T_BACK_EDGES = -(-T_BACK // PER_TILE)
+BLOCKS = 2
 CANDIDATES = BLOCKS * SLOTS
-PART_ROWS = 2 * BLOCKS * LEV
+PART_ROWS = 104
 LIMIT = 48 * 1024 * 1024
 
 
@@ -98,20 +98,18 @@
     return jnp.concatenate([rows[0:1], rows[1:2]], axis=1)
 
 
-def place(cell, south, west):
-    row, col = cell // COLS, cell % COLS
+def unpack_edges(west, east, index, width):
+    lane = lanes()
+    at, slot = index // PER_TILE, EDGE * (index % PER_TILE)
+    west = shifted(west(at), COLS - EDGE - slot, 1)
+    east = shifted(east(at), -slot, 1)
+    return jnp.where(lane < width, east, jnp.where(lane >= COLS - width, west, 0.0))
+
+
+def place(cell, south):
     if south:
-        inside = row >= ROWS - SHIFT
-        row = row - (ROWS - SHIFT)
-    else:
-        inside = row < SHIFT
-    if west:
-        inside = inside & (col >= COLS - SHIFT)
-        col = col - (COLS - SHIFT)
-    else:
-        inside = inside & (col < COLS - SHIFT)
-        col = col + SHIFT
-    return jnp.where(inside, row * COLS + col, -1)
+        cell = cell - (ROWS - SHIFT) * COLS
+    return jnp.where((cell >= 0) & (cell < SHIFT * COLS), cell, -1)
 
 
 def diagonals(table, wide, turned):
@@ -132,7 +130,7 @@
 
 def pack_kernel(
     d, flag, east, north, sigma, weight, cell, owner, table,
-    band, side, tables,
+    band, to_east, to_west, tables,
     whole, lines, matrix, wide, turned, sems,
 ):
     obs = ROWS * T_FIELDS
@@ -161,37 +159,46 @@
     band[obs + R_OWNER : obs + R_OWNER + 2, :] = whole[2 * ROWS : 2 * ROWS + 2, :].astype(jnp.float32)
     band[obs + R_OWNER + 2 : ROWS * T_OWN, :] = jnp.zeros((2, COLS), jnp.float32)
     tiles = [band[ROWS * t : ROWS * (t + 1), :] for t in range(T_FIELDS)]
-    for i, packed in enumerate(pack_edges(tiles, COLS - EDGE)):
-        side[ROWS * i : ROWS * (i + 1), :] = packed
-    side[ROWS * T_EDGES :, :] = band[obs : ROWS * T_OWN, :]
+    for out, first in ((to_east, COLS - EDGE), (to_west, 0)):
+        for i, packed in enumerate(pack_edges(tiles, first)):
+            out[ROWS * i : ROWS * (i + 1), :] = packed
     tile = diagonals(matrix, wide, turned)
     for i in range(tables.shape[0] // 4):
         tables[4 * i : 4 * i + 4, :] = tile
 
 
-def band_kernel(given, west, out, sem):
+def band_kernel(given, west, east, out, sems):
     del given
-    copy = pltpu.make_async_copy(west, out.at[pl.ds(ROWS * T_OWN, ROWS * T_SIDE), :], sem)
+    rows = ROWS * T_EDGES
+    copies = [
+        pltpu.make_async_copy(west, out.at[pl.ds(ROWS * T_OWN, rows), :], sems.at[0]),
+        pltpu.make_async_copy(east, out.at[pl.ds(ROWS * T_OWN + rows, rows), :], sems.at[1]),
+    ]
+    for copy in copies:
+        copy.start()
+    for copy in copies:
+        copy.wait()
+
+
+def repeat_kernel(given, band, tables, here, sem):
+    copy = pltpu.make_async_copy(band, here, sem)
     copy.start()
-    copy.wait()
-
-
-def repeat_kernel(given, tables):
     count = given.shape[0]
     for i in range(tables.shape[0] // count):
         tables[count * i : count * (i + 1), :] = given[...]
+    copy.wait()
 
 
 def pick_kernel(lats, lons, own, south, part, aux, weights, marks, edges, held):
-    west = own.at[pl.ds(ROWS * T_OWN, ROWS * T_SIDE), :]
-    both = south.at[pl.ds(ROWS * T_OWN, ROWS * T_SIDE), :]
-    lane = lanes()
-    for b, side in enumerate((both, west)):
+    for b, band in enumerate((south, own)):
+        def west(i, band=band):
+            return band[ROWS * (T_OWN + i) : ROWS * (T_OWN + i + 1), :]
+
+        def east(i, band=band):
+            return band[ROWS * (T_OWN + T_EDGES + i) : ROWS * (T_OWN + T_EDGES + i + 1), :]
+
         for t in range(T_FIELDS):
-            at = ROWS * (t // PER_TILE)
-            packed = side[at : at + ROWS, :]
-            edge = shifted(packed, COLS - EDGE - EDGE * (t % PER_TILE), 1)
-            edges[b, t] = jnp.where(lane >= COLS - EDGE, edge, 0.0)
+            edges[b, t] = unpack_edges(west, east, t, EDGE)
 
     def framed(first, count):
         rows = slice(ROWS * first, ROWS * (first + count))
@@ -210,7 +217,7 @@
 
     def lower(x):
         axis = x.ndim - 2
-        x = shifted(x, SHIFT, axis + 1)[..., :COLS]
+        x = x[..., :COLS]
         return shifted(x, -SHIFT, axis)[..., :ROWS, :]
 
     for i, x in enumerate((spread, ke, kn)):
@@ -226,14 +233,14 @@
     weights[LEV:, :] = jnp.zeros((PADLEV - LEV, CANDIDATES), jnp.float32)
     marks[...] = jnp.zeros_like(marks)
     for b in range(BLOCKS):
-        band = (own, west, south, both)[b]
-        obs = ROWS * (T_EDGES if b % 2 else T_FIELDS)
+        band = (own, south)[b]
+        obs = ROWS * T_FIELDS
         for p in (0, 1):
             columns = slice(b * SLOTS + p * COLS, b * SLOTS + (p + 1) * COLS)
             weights[0:LEV, columns] = band[pl.ds(obs + p, LEV, stride=2), :]
         columns = slice(b * SLOTS, (b + 1) * SLOTS)
         cell = side_by_side(band[obs + R_CELL : obs + R_CELL + 2, :].astype(jnp.int32))
-        marks[0:1, columns] = place(cell, b >= 2, b % 2)
+        marks[0:1, columns] = place(cell, b == 1)
         owner = side_by_side(band[obs + R_OWNER : obs + R_OWNER + 2, :].astype(jnp.int32))
         marks[1:2, columns] = owner % lons * lats + owner // lons
 
@@ -242,19 +249,21 @@
         state = jnp.concatenate(
             [held[pl.ds(first + r, PADLEV, stride=ROWS), :] for r in range(SHIFT)], axis=1
         )
-        columns = slice(2 * half * SLOTS, 2 * (half + 1) * SLOTS)
+        columns = slice(half * SLOTS, (half + 1) * SLOTS)
         hot = one_hot(marks[0:1, columns], SHIFT * COLS)
         stacked = jnp.concatenate(split(state, 3), axis=0)
         got = jnp.dot(stacked, hot, preferred_element_type=jnp.float32)
         got = got[0:PADLEV] + got[PADLEV : 2 * PADLEV] + got[2 * PADLEV :]
         got = got * weights[:, columns]
-        for c in range(4):
-            at = (4 * half + c) * LEV
+        for c in range(2):
+            at = (2 * half + c) * LEV
             part[at : at + LEV, :] = got[0:LEV, c * COLS : (c + 1) * COLS]
+    filled = 2 * BLOCKS * LEV
+    part[filled:, :] = jnp.zeros((PART_ROWS - filled, COLS), jnp.float32)
 
 
 def spread_kernel(
-    fields, owners, parts, tables, weights, marks, aux, out, side, column, double, circled, held
+    fields, owners, parts, tables, weights, marks, aux, out, to_east, to_west, column, double, circled, held
 ):
     total = parts[0:PART_ROWS, :]
     for f in range(1, fields):
@@ -289,8 +298,8 @@
         weighted.append(sums * weights[:, columns])
     for half in (0, 1):
         first = SHIFT * (1 - half)
-        value = jnp.concatenate(weighted[2 * half : 2 * half + 2], axis=1)
-        columns = slice(2 * half * SLOTS, 2 * (half + 1) * SLOTS)
+        value = weighted[half]
+        columns = slice(half * SLOTS, (half + 1) * SLOTS)
         hot = one_hot(marks[0:1, columns], SHIFT * COLS)
         stacked = jnp.concatenate(split(value, 3), axis=0)
         got = lax.dot_general(
@@ -302,16 +311,27 @@
     tiles = [held[ROWS * t : ROWS * (t + 1), :] * aux[0] for t in range(LEV)] + [aux[1], aux[2]]
     for t, tile in enumerate(tiles):
         out[t] = tile
-    for i, packed in enumerate(pack_edges(tiles, 0)):
-        side[i] = packed
-
-
-def image_kernel(own, east, north, both, d, res, image, sums, edges):
-    lane = lanes()
-    for b, side in enumerate((east, both)):
+    for out, first in ((to_east, COLS - EDGE), (to_west, 0)):
+        for i, packed in enumerate(pack_edges(tiles, first)):
+            out[i] = packed
+
+
+def back_kernel(source, west, east, out):
+    out[0:T_BACK] = source[...]
+    out[T_BACK : T_BACK + T_BACK_EDGES] = west[...]
+    out[T_BACK + T_BACK_EDGES :] = east[...]
+
+
+def image_kernel(own, north, d, res, image, sums, edges):
+    for b, block in enumerate((own, north)):
+        def west(i, block=block):
+            return block[T_BACK + i]
+
+        def east(i, block=block):
+            return block[T_BACK + T_BACK_EDGES + i]
+
         for t in range(T_BACK):
-            edge = shifted(side[t // PER_TILE], -EDGE * (t % PER_TILE), 1)
-            edges[b, t] = jnp.where(lane < EDGE, edge, 0.0)
+            edges[b, t] = unpack_edges(west, east, t, EDGE)
 
     def framed(levels):
         return frame(own[levels], edges[0, levels], north[levels], edges[1, levels])
@@ -324,8 +344,7 @@
         here = d[levels]
         old = res[levels]
         x = diffuse(framed(levels), scaled)
-        x = shifted(x, -SHIFT, 2)[:, :, :COLS]
-        x = here + shifted(x, -SHIFT, 1)[:, :ROWS]
+        x = here + shifted(x[:, :, :COLS], -SHIFT, 1)[:, :ROWS]
         image[levels] = x
         norm = norm + jnp.sum(old * old, axis=0)
         curve = curve + jnp.sum(here * x, axis=0)
@@ -369,7 +388,7 @@
     return lambda *arrays: pl.pallas_call(
         kernel,
         out_shape=tuple(shape_of(out) for out in outs),
-        in_specs=[given] * len(arrays),
+        in_specs=list(given) if isinstance(given, tuple) else [given] * len(arrays),
         out_specs=tuple([VMEM] * len(outs)),
         scratch_shapes=[pltpu.VMEM(s, jnp.float32) if isinstance(s, tuple) else s for s in scratch],
         compiler_params=pltpu.CompilerParams(vmem_limit_bytes=limit),
@@ -386,16 +405,6 @@
     size = lax.axis_size(axis)
     blocks = x.reshape(size, x.shape[0] // size, COLS)
     return lax.all_to_all(blocks, axis, 0, 0, tiled=True).reshape(x.shape)
-
-
-def step_both(x, by):
-    lats, lons = lax.axis_size("lat"), lax.axis_size("lon")
-    pairs = [
-        (i * lons + j, (i + by) % lats * lons + (j + by) % lons)
-        for i in range(lats)
-        for j in range(lons)
-    ]
-    return lax.ppermute(x, ("lat", "lon"), pairs)
 
 
 def local(
@@ -416,11 +425,12 @@
     block = (LEV, ROWS, COLS)
     d = direction.reshape(block)
     res = residual.reshape(block)
-    own, side, tables = call(
+    band, to_east, to_west, tables = call(
         pack_kernel,
         (
-            (ROWS * (T_OWN + T_SIDE), COLS),
-            (ROWS * T_SIDE, COLS),
+            (ROWS * T_BAND, COLS),
+            (ROWS * T_EDGES, COLS),
+            (ROWS * T_EDGES, COLS),
             (4 * lats, COLS),
         ),
         (
@@ -444,19 +454,27 @@
         obs_owner.reshape(2, COLS),
         jnp.transpose(error_inverse, (1, 0, 2)),
     )
-    west = step(side, "lon", 1)
+    west = step(to_east, "lon", 1)
+    east = step(to_west, "lon", -1)
     tables = exchange(tables, "lat")
     band = pl.pallas_call(
         band_kernel,
-        out_shape=jax.ShapeDtypeStruct(own.shape, jnp.float32),
-        in_specs=[ANY, ANY],
+        out_shape=jax.ShapeDtypeStruct(band.shape, jnp.float32),
+        in_specs=[ANY, ANY, ANY],
         out_specs=ANY,
-        scratch_shapes=[pltpu.SemaphoreType.DMA],
+        scratch_shapes=[pltpu.SemaphoreType.DMA((2,))],
         input_output_aliases={0: 0},
+        cost_estimate=pl.CostEstimate(flops=20000000000, bytes_accessed=1000000, transcendentals=0),
         compiler_params=pltpu.CompilerParams(vmem_limit_bytes=LIMIT),
-    )(own, west)
+    )(band, west, east)
     south = step(band, "lat", 1)
-    (tables,) = call(repeat_kernel, ((4 * owners, COLS),), flops=20000000000)(tables)
+    tables, own = call(
+        repeat_kernel,
+        ((4 * owners, COLS), band.shape),
+        (pltpu.SemaphoreType.DMA,),
+        given=(VMEM, ANY),
+        flops=20000000000,
+    )(tables, band)
     tables = exchange(tables, "lon")
     part, aux, weights, marks = call(
         functools.partial(pick_kernel, lats, lons),
@@ -468,11 +486,15 @@
         ),
         ((2, T_FIELDS, ROWS, COLS), (PADLEV * ROWS, COLS)),
         flops=20000000000,
-    )(band, south)
+    )(own, south)
     parts = lax.all_gather(part, "obs", tiled=True)
-    source, side = call(
+    source, to_east, to_west = call(
         functools.partial(spread_kernel, fields, owners),
-        ((T_BACK, ROWS, COLS), (T_BACK_SIDE, ROWS, COLS)),
+        (
+            (T_BACK, ROWS, COLS),
+            (T_BACK_EDGES, ROWS, COLS),
+            (T_BACK_EDGES, ROWS, COLS),
+        ),
         (
             (PART_ROWS, COLS),
             (2 * PADLEV, owners),
@@ -480,12 +502,13 @@
             (PADLEV * ROWS, COLS),
         ),
     )(parts, tables, weights, marks, aux)
+    west = step(to_east, "lon", 1)
+    east = step(to_west, "lon", -1)
+    (source,) = call(back_kernel, ((T_BACK + 2 * T_BACK_EDGES, ROWS, COLS),))(source, west, east)
     north = step(source, "lat", -1)
-    east = step(side, "lon", -1)
-    both = step_both(side, -1)
     image, sums = call(
         image_kernel, (block, (fields * lons, COLS)), ((2, T_BACK, ROWS, COLS),)
-    )(source, east, north, both, d, res)
+    )(source, north, d, res)
     sums = lax.all_to_all(sums, ("obs", "lon"), 0, 0, tiled=True)
     (sums,) = call(sum_kernel, ((lats, COLS),))(sums)
     sums = lax.all_to_all(sums, "lat", 0, 0, tiled=True)

time: 94.3 us -> 99.6 us (1.056)
  starting transfers between devices: 33.5 us -> 37.9 us
  waiting for transfers between devices: 5.58 us -> 9.71 us
  blocking collectives: 44.5 us -> 41.9 us
    ppermute x4 -> x6, starting transfers between devices: 12 us -> 24.5 us  [step(): return lax.ppermute(x, axis, [(i, (i + by) % size) for i in range(size)])]
    ppermute x1 -> x0, starting transfers between devices: 5.76 us -> none  [step_both(): return lax.ppermute(x, ('lat', 'lon'), pairs)]
    ppermute x4 -> x6, waiting for transfers between devices: 2.78 us -> 6.99 us  [step(): return lax.ppermute(x, axis, [(i, (i + by) % size) for i in range(size)])]
    all_to_all x2, starting transfers between devices: 15.7 us -> 13.4 us  [exchange(): return lax.all_to_all(blocks, axis, 0, 0, tiled=True).reshape(x.shape)]
    all_gather x1, blocking collectives: 15.1 us -> 13.6 us  [local(): parts = lax.all_gather(part, 'obs', tiled=True)]
    all_to_all x1, blocking collectives: 11 us -> 9.61 us  [local(): sums = lax.all_to_all(sums, 'lat', 0, 0, tiled=True)]
    pallas_call x7 -> x8, Pallas kernels: 8.81 us -> 8.15 us  [call(): pl.pallas_call(kernel, out_shape=tuple((shape_of(out) for out in outs)),...]
  transfers between devices with their start and end apart: 7 -> 8, of which waited for: 2 -> 3; matrix products, arithmetic and copies ran while one was open for 0% -> 0% of each run, Pallas kernels for 4% -> 4%
where the time goes in v5:
time: 99.6 us; the launch traced here: 99.1 us
  blocking collectives  41.9 us (42%)
  starting transfers between devices  37.9 us (38%)
  waiting for transfers between devices  9.71 us (10%)
  Pallas kernels  8.76 us (9%)
    ppermute x6, starting transfers between devices, step(): return lax.ppermute(x, axis, [(i, (i + by) % size) for i in range(size)])  24.5 us
    all_to_all x1, blocking collectives, local(): sums = lax.all_to_all(sums, ('obs', 'lon'), 0, 0, tiled=True)  18.7 us
    all_gather x1, blocking collectives, local(): parts = lax.all_gather(part, 'obs', tiled=True)  13.6 us
    all_to_all x2, starting transfers between devices, exchange(): return lax.all_to_all(blocks, axis, 0, 0, tiled=True).reshape(x.shape)  13.4 us
    all_to_all x1, blocking collectives, local(): sums = lax.all_to_all(sums, 'lat', 0, 0, tiled=True)  9.61 us
    pallas_call x8, Pallas kernels, call(): pl.pallas_call(kernel, out_shape=tuple((shape_of(out) for out in outs)),...  8.15 us
    ppermute x6, waiting for transfers between devices, step(): return lax.ppermute(x, axis, [(i, (i + by) % size) for i in range(size)])  6.99 us
    all_to_all x2, waiting for transfers between devices, exchange(): return lax.all_to_all(blocks, axis, 0, 0, tiled=True).reshape(x.shape)  2.72 us
  transfers between devices with their start and end apart: 8, of which 3 were waited for; matrix products, arithmetic and copies ran while one was open for 0% of the time, Pallas kernels for 4%

profile of v5, /device:TPU:1, one launch (start us, length us, event | category | flops | bytes accessed | tf_op | source)
XLA Modules:
  0.0 99.1 jit_solution(5439003411021296743)
XLA Ops:
  0.6 1.9 %shard_map.130 = (f32[320,128]{1,0:T(8,128)}, f32[16,128]{1,0:T(8,128)}, f32[16,128]{1,0:T(8,128)}, f32[32,128]{1,0:T(8,128)}) custom-call(f32[200,128]{1,0:T(8,128)} %bitcast.25, s32[8,128]{1,0:T(8,128)} %flag.1, f32[8,128]{1,0:T(8,128)} %east.1, f32[8,128]{1,0:T(8,128)} %north.1, f32[8,128]{1,0:T(8,128)} %bitcast.39, f32[25,1,256]{2,1,0:T(1,128)} %bitcast.36, ...), custom_call_target="tpu_custom_call" | custom-call | flops 1000000 | bytes 1000000 | tf_op jit(solution)/shard_map/pallas_call | solution.py:388
  2.6 4.5 %collective-permute-start = (f32[16,128]{1,0:T(8,128)}, f32[16,128]{1,0:T(8,128)S(1)}, u32[]{:S(2)}, u32[]{:S(2)}) collective-permute-start(f32[16,128]{1,0:T(8,128)} %get-tuple-element.23), channel_id=1, source_target_pairs={{0,4},{4,8},{8,12},{12,16},{16,20},{20,24},{24,28},{28,32},{32,36}... | collective-permute-start | bytes 24584 | tf_op jit(solution)/shard_map/ppermute | solution.py:401
  7.1 6.2 %collective-permute-start.1 = (f32[16,128]{1,0:T(8,128)}, f32[16,128]{1,0:T(8,128)S(1)}, u32[]{:S(2)}, u32[]{:S(2)}) collective-permute-start(f32[16,128]{1,0:T(8,128)} %get-tuple-element.24), channel_id=1, source_target_pairs={{0,60},{4,0},{8,4},{12,8},{16,12},{20,16},{24,20},{28,24},{32,28},... | collective-permute-start | bytes 24584 | tf_op jit(solution)/shard_map/ppermute | solution.py:401
  13.3 5.8 %all-to-all-start = ((f32[8,4,128]{2,1,0:T(4,128)}), f32[8,4,128]{2,1,0:T(4,128)S(1)}, u32[]{:S(2)}, u32[]{:S(2)}) async-start(f32[8,4,128]{2,1,0:T(4,128)} %bitcast.37), calls=%async_computation | async-start | bytes 32768 | tf_op jit(solution)/shard_map/all_to_all | solution.py:407
  19.1 0.0 collective-permute-done.1.east
  19.1 0.6 shard_map.131.band
  19.7 3.4 %collective-permute-start.2 = (f32[320,128]{1,0:T(8,128)}, f32[320,128]{1,0:T(8,128)S(1)}, u32[]{:S(2)}, u32[]{:S(2)}) collective-permute-start(f32[320,128]{1,0:T(8,128)} %shard_map.131.band), channel_id=1, source_target_pairs={{0,64},{64,128},{128,192},{192,256},{256,320},{320,384},{384,448},... | collective-permute-start | bytes 491528 | tf_op jit(solution)/shard_map/ppermute | solution.py:401
  23.1 2.7 %all-to-all-done = f32[8,4,128]{2,1,0:T(4,128)S(1)} async-done(((f32[8,4,128]{2,1,0:T(4,128)}), f32[8,4,128]{2,1,0:T(4,128)S(1)}, u32[]{:S(2)}, u32[]{:S(2)}) %all-to-all-start) | async-done | bytes 16416 | tf_op jit(solution)/shard_map/all_to_all | solution.py:407
  25.8 1.6 %shard_map.132 = (f32[512,128]{1,0:T(8,128)}, f32[320,128]{1,0:T(8,128)S(1)}) custom-call(f32[32,128]{1,0:T(8,128)S(1)} %bitcast.35, f32[320,128]{1,0:T(8,128)} %shard_map.131.band), custom_call_target="tpu_custom_call" | custom-call | flops 20000000000 | bytes 1000000 | tf_op jit(solution)/shard_map/pallas_call | solution.py:388
  27.4 7.6 %all-to-all-start.1 = ((f32[16,32,128]{2,1,0:T(8,128)}), f32[16,32,128]{2,1,0:T(8,128)S(1)}, u32[]{:S(2)}, u32[]{:S(2)}) async-start(f32[16,32,128]{2,1,0:T(8,128)} %bitcast.8), calls=%async_computation.1 | async-start | bytes 524288 | tf_op jit(solution)/shard_map/all_to_all | solution.py:407
  35.0 1.4 %shard_map.133 = (f32[104,128]{1,0:T(8,128)S(1)}, f32[3,8,128]{2,1,0:T(8,128)S(1)}, f32[32,512]{1,0:T(8,128)S(1)}, s32[8,512]{1,0:T(8,128)S(1)}) custom-call(f32[320,128]{1,0:T(8,128)S(1)} %get-tuple-element.25.own, f32[320,128]{1,0:T(8,128)S(1)} %collective-permute-done.2.south), custom_call_target="tpu_custom_call" | custom-call | flops 20000000000 | bytes 1000000 | tf_op jit(solution)/shard_map/pallas_call | solution.py:388
  36.4 13.6 %all_gather.3.parts = f32[416,128]{1,0:T(8,128)S(1)} all-gather(f32[104,128]{1,0:T(8,128)S(1)} %get-tuple-element.26), channel_id=1, replica_groups=mesh['lat'=8,'lon'=16,'obs'=4] {'obs'}, dimensions={0}, use_global_device_ids=true | all-gather | bytes 266240 | tf_op jit(solution)/shard_map/all_gather | solution.py:490
  50.0 0.0 all-to-all-done.1
  50.0 0.8 shard_map.134
  50.9 6.4 %collective-permute-start.3 = (f32[2,8,128]{2,1,0:T(8,128)S(1)}, f32[2,8,128]{2,1,0:T(8,128)S(1)}, u32[]{:S(2)}, u32[]{:S(2)}) collective-permute-start(f32[2,8,128]{2,1,0:T(8,128)S(1)} %get-tuple-element.32), channel_id=1, source_target_pairs={{0,4},{4,8},{8,12},{12,16},{16,20},{20,24},{24,28},{28,32},{32,36}... | collective-permute-start | bytes 24584 | tf_op jit(solution)/shard_map/ppermute | solution.py:401
  57.3 1.9 %collective-permute-start.4 = (f32[2,8,128]{2,1,0:T(8,128)S(1)}, f32[2,8,128]{2,1,0:T(8,128)S(1)}, u32[]{:S(2)}, u32[]{:S(2)}) collective-permute-start(f32[2,8,128]{2,1,0:T(8,128)S(1)} %get-tuple-element.33), channel_id=1, source_target_pairs={{0,60},{4,0},{8,4},{12,8},{16,12},{20,16},{24,20},{28,24},{32,28},... | collective-permute-start | bytes 24584 | tf_op jit(solution)/shard_map/ppermute | solution.py:401
  59.2 3.0 %collective-permute-done.4.east = f32[2,8,128]{2,1,0:T(8,128)S(1)} collective-permute-done((f32[2,8,128]{2,1,0:T(8,128)S(1)}, f32[2,8,128]{2,1,0:T(8,128)S(1)}, u32[]{:S(2)}, u32[]{:S(2)}) %collective-permute-start.4) | collective-permute-done | bytes 8224 | tf_op jit(solution)/shard_map/ppermute | solution.py:401
  62.3 2.2 %collective-permute-start.5 = (f32[31,8,128]{2,1,0:T(8,128)S(1)}, f32[31,8,128]{2,1,0:T(8,128)S(1)}, u32[]{:S(2)}, u32[]{:S(2)}) collective-permute-start(f32[31,8,128]{2,1,0:T(8,128)S(1)} %shard_map.135.own), channel_id=1, source_target_pairs={{0,448},{64,0},{128,64},{192,128},{256,192},{320,256},{384,320},{4... | collective-permute-start | bytes 380936 | tf_op jit(solution)/shard_map/ppermute | solution.py:401
  64.4 4.0 %collective-permute-done.5.north = f32[31,8,128]{2,1,0:T(8,128)S(1)} collective-permute-done((f32[31,8,128]{2,1,0:T(8,128)S(1)}, f32[31,8,128]{2,1,0:T(8,128)S(1)}, u32[]{:S(2)}, u32[]{:S(2)}) %collective-permute-start.5) | collective-permute-done | bytes 127008 | tf_op jit(solution)/shard_map/ppermute | solution.py:401
  68.4 1.5 %shard_map.136 = (f32[25,8,128]{2,1,0:T(8,128)S(1)}, f32[64,128]{1,0:T(8,128)S(1)}) custom-call(f32[31,8,128]{2,1,0:T(8,128)S(1)} %shard_map.135.own, f32[31,8,128]{2,1,0:T(8,128)S(1)} %collective-permute-done.5.north, f32[25,8,128]{2,1,0:T(8,128)S(1)} %bitcast.26, f32[25,8,128]{2,1,0:T(8,128)S(1)} %bitcast.28), custom_call_target="tpu_custom_call" | custom-call | flops 1000000 | bytes 1000000 | tf_op jit(solution)/shard_map/pallas_call | solution.py:388
  69.9 0.0 copy-start.2
  69.9 18.7 %all_to_all.32 = f32[64,1,128]{2,1,0:T(1,128)S(1)} all-to-all(f32[64,1,128]{2,1,0:T(1,128)S(1)} %bitcast.32), channel_id=1, replica_groups=mesh['lat'=8,'lon'=16,'obs'=4] {'obs','lon'}, dimensions={0} | all-to-all | bytes 65536 | tf_op jit(solution)/shard_map/all_to_all | solution.py:512
  88.6 9.6 %all_to_all.33 = f32[8,1,128]{2,1,0:T(1,128)S(1)} all-to-all(f32[8,1,128]{2,1,0:T(1,128)S(1)} %bitcast.34), channel_id=1, replica_groups=mesh['lat'=8,'lon'=16,'obs'=4] {'lat'}, dimensions={0} | all-to-all | bytes 8192 | tf_op jit(solution)/shard_map/all_to_all | solution.py:514
  98.2 0.8 shard_map.138
  (10 shorter events, 0.0 us)
Async XLA Ops:
  2.6 16.5 %collective-permute-start = (f32[16,128]{1,0:T(8,128)}, f32[16,128]{1,0:T(8,128)S(1)}, u32[]{:S(2)}, u32[]{:S(2)}) collective-permute-start(f32[16,128]{1,0:T(8,128)} %get-tuple-element.23), channel_id=1, source_target_pairs={{0,4},{4,8},{8,12},{12,16},{16,20},{20,24},{24,28},{28,32},{32,36}... | collective-permute-start | bytes 24584 | tf_op jit(solution)/shard_map/ppermute | solution.py:401
  7.1 12.0 %collective-permute-start.1 = (f32[16,128]{1,0:T(8,128)}, f32[16,128]{1,0:T(8,128)S(1)}, u32[]{:S(2)}, u32[]{:S(2)}) collective-permute-start(f32[16,128]{1,0:T(8,128)} %get-tuple-element.24), channel_id=1, source_target_pairs={{0,60},{4,0},{8,4},{12,8},{16,12},{20,16},{24,20},{28,24},{32,28},... | collective-permute-start | bytes 24584 | tf_op jit(solution)/shard_map/ppermute | solution.py:401
  13.3 12.5 %all-to-all-start = ((f32[8,4,128]{2,1,0:T(4,128)}), f32[8,4,128]{2,1,0:T(4,128)S(1)}, u32[]{:S(2)}, u32[]{:S(2)}) async-start(f32[8,4,128]{2,1,0:T(4,128)} %bitcast.37), calls=%async_computation | async-start | bytes 32768 | tf_op jit(solution)/shard_map/all_to_all | solution.py:407
  19.7 15.3 %collective-permute-start.2 = (f32[320,128]{1,0:T(8,128)}, f32[320,128]{1,0:T(8,128)S(1)}, u32[]{:S(2)}, u32[]{:S(2)}) collective-permute-start(f32[320,128]{1,0:T(8,128)} %shard_map.131.band), channel_id=1, source_target_pairs={{0,64},{64,128},{128,192},{192,256},{256,320},{320,384},{384,448},... | collective-permute-start | bytes 491528 | tf_op jit(solution)/shard_map/ppermute | solution.py:401
  27.4 22.6 %all-to-all-start.1 = ((f32[16,32,128]{2,1,0:T(8,128)}), f32[16,32,128]{2,1,0:T(8,128)S(1)}, u32[]{:S(2)}, u32[]{:S(2)}) async-start(f32[16,32,128]{2,1,0:T(8,128)} %bitcast.8), calls=%async_computation.1 | async-start | bytes 524288 | tf_op jit(solution)/shard_map/all_to_all | solution.py:407
  50.9 8.3 %collective-permute-start.3 = (f32[2,8,128]{2,1,0:T(8,128)S(1)}, f32[2,8,128]{2,1,0:T(8,128)S(1)}, u32[]{:S(2)}, u32[]{:S(2)}) collective-permute-start(f32[2,8,128]{2,1,0:T(8,128)S(1)} %get-tuple-element.32), channel_id=1, source_target_pairs={{0,4},{4,8},{8,12},{12,16},{16,20},{20,24},{24,28},{28,32},{32,36}... | collective-permute-start | bytes 24584 | tf_op jit(solution)/shard_map/ppermute | solution.py:401
  57.3 5.0 %collective-permute-start.4 = (f32[2,8,128]{2,1,0:T(8,128)S(1)}, f32[2,8,128]{2,1,0:T(8,128)S(1)}, u32[]{:S(2)}, u32[]{:S(2)}) collective-permute-start(f32[2,8,128]{2,1,0:T(8,128)S(1)} %get-tuple-element.33), channel_id=1, source_target_pairs={{0,60},{4,0},{8,4},{12,8},{16,12},{20,16},{24,20},{28,24},{32,28},... | collective-permute-start | bytes 24584 | tf_op jit(solution)/shard_map/ppermute | solution.py:401
  62.2 6.1 %copy-start = (f32[1,25,8,128]{3,2,1,0:T(8,128)S(1)}, f32[1,25,8,128]{3,2,1,0:T(8,128)}, u32[]{:S(2)}) copy-start(f32[1,25,8,128]{3,2,1,0:T(8,128)} %param.13) | copy-start | bytes 307204
  62.2 6.1 %copy-start.1 = (f32[1,25,8,128]{3,2,1,0:T(8,128)S(1)}, f32[1,25,8,128]{3,2,1,0:T(8,128)}, u32[]{:S(2)}) copy-start(f32[1,25,8,128]{3,2,1,0:T(8,128)} %param.12) | copy-start | bytes 307204
  62.3 6.1 %collective-permute-start.5 = (f32[31,8,128]{2,1,0:T(8,128)S(1)}, f32[31,8,128]{2,1,0:T(8,128)S(1)}, u32[]{:S(2)}, u32[]{:S(2)}) collective-permute-start(f32[31,8,128]{2,1,0:T(8,128)S(1)} %shard_map.135.own), channel_id=1, source_target_pairs={{0,448},{64,0},{128,64},{192,128},{256,192},{320,256},{384,320},{4... | collective-permute-start | bytes 380936 | tf_op jit(solution)/shard_map/ppermute | solution.py:401
  69.9 28.3 %copy-start.2 = (f32[1,25,8,128]{3,2,1,0:T(8,128)S(1)}, f32[1,25,8,128]{3,2,1,0:T(8,128)}, u32[]{:S(2)}) copy-start(f32[1,25,8,128]{3,2,1,0:T(8,128)} %param.11) | copy-start | bytes 307204

commit v6 on v4

--- a/solution.py
+++ b/solution.py
@@ -132,7 +132,7 @@
 
 def pack_kernel(
     d, flag, east, north, sigma, weight, cell, owner, table,
-    band, side, tables,
+    band, side, tables, own,
     whole, lines, matrix, wide, turned, sems,
 ):
     obs = ROWS * T_FIELDS
@@ -148,9 +148,13 @@
         pltpu.make_async_copy(owner, whole.at[pl.ds(2 * ROWS, 2), :], sems.at[7]),
         pltpu.make_async_copy(table, matrix, sems.at[8]),
     ]
-    for copy in copies:
+    for copy in copies[::-1]:
         copy.start()
-    for copy in copies:
+    copies[8].wait()
+    tile = diagonals(matrix, wide, turned)
+    for i in range(tables.shape[0] // 4):
+        tables[4 * i : 4 * i + 4, :] = tile
+    for copy in copies[:8]:
         copy.wait()
     for l in range(LEV):
         for p in (0, 1):
@@ -164,9 +168,7 @@
     for i, packed in enumerate(pack_edges(tiles, COLS - EDGE)):
         side[ROWS * i : ROWS * (i + 1), :] = packed
     side[ROWS * T_EDGES :, :] = band[obs : ROWS * T_OWN, :]
-    tile = diagonals(matrix, wide, turned)
-    for i in range(tables.shape[0] // 4):
-        tables[4 * i : 4 * i + 4, :] = tile
+    own[...] = band[0 : ROWS * T_OWN, :]
 
 
 def band_kernel(given, west, out, sem):
@@ -182,8 +184,7 @@
         tables[count * i : count * (i + 1), :] = given[...]
 
 
-def pick_kernel(lats, lons, own, south, part, aux, weights, marks, edges, held):
-    west = own.at[pl.ds(ROWS * T_OWN, ROWS * T_SIDE), :]
+def pick_kernel(lats, lons, own, west, south, part, aux, weights, marks, edges, held):
     both = south.at[pl.ds(ROWS * T_OWN, ROWS * T_SIDE), :]
     lane = lanes()
     for b, side in enumerate((both, west)):
@@ -254,7 +255,7 @@
 
 
 def spread_kernel(
-    fields, owners, parts, tables, weights, marks, aux, out, side, column, double, circled, held
+    fields, owners, parts, tables, weights, marks, aux, out, column, double, circled, held
 ):
     total = parts[0:PART_ROWS, :]
     for f in range(1, fields):
@@ -303,14 +304,19 @@
     for t, tile in enumerate(tiles):
         out[t] = tile
     for i, packed in enumerate(pack_edges(tiles, 0)):
-        side[i] = packed
-
-
-def image_kernel(own, east, north, both, d, res, image, sums, edges):
+        out[T_BACK + i] = packed
+
+
+def back_kernel(own, north, out):
+    out[0:T_BACK_SIDE] = own[T_BACK:]
+    out[T_BACK_SIDE:] = north[T_BACK:]
+
+
+def image_kernel(own, north, east, d, res, image, sums, edges):
     lane = lanes()
-    for b, side in enumerate((east, both)):
+    for b in (0, 1):
         for t in range(T_BACK):
-            edge = shifted(side[t // PER_TILE], -EDGE * (t % PER_TILE), 1)
+            edge = shifted(east[T_BACK_SIDE * b + t // PER_TILE], -EDGE * (t % PER_TILE), 1)
             edges[b, t] = jnp.where(lane < EDGE, edge, 0.0)
 
     def framed(levels):
@@ -388,16 +394,6 @@
     return lax.all_to_all(blocks, axis, 0, 0, tiled=True).reshape(x.shape)
 
 
-def step_both(x, by):
-    lats, lons = lax.axis_size("lat"), lax.axis_size("lon")
-    pairs = [
-        (i * lons + j, (i + by) % lats * lons + (j + by) % lons)
-        for i in range(lats)
-        for j in range(lons)
-    ]
-    return lax.ppermute(x, ("lat", "lon"), pairs)
-
-
 def local(
     control,
     residual,
@@ -416,12 +412,13 @@
     block = (LEV, ROWS, COLS)
     d = direction.reshape(block)
     res = residual.reshape(block)
-    own, side, tables = call(
+    band, side, tables, own = call(
         pack_kernel,
         (
             (ROWS * (T_OWN + T_SIDE), COLS),
             (ROWS * T_SIDE, COLS),
             (4 * lats, COLS),
+            (ROWS * T_OWN, COLS),
         ),
         (
             pltpu.VMEM((3 * ROWS, COLS), jnp.int32),
@@ -448,13 +445,13 @@
     tables = exchange(tables, "lat")
     band = pl.pallas_call(
         band_kernel,
-        out_shape=jax.ShapeDtypeStruct(own.shape, jnp.float32),
+        out_shape=jax.ShapeDtypeStruct(band.shape, jnp.float32),
         in_specs=[ANY, ANY],
         out_specs=ANY,
         scratch_shapes=[pltpu.SemaphoreType.DMA],
         input_output_aliases={0: 0},
         compiler_params=pltpu.CompilerParams(vmem_limit_bytes=LIMIT),
-    )(own, west)
+    )(band, west)
     south = step(band, "lat", 1)
     (tables,) = call(repeat_kernel, ((4 * owners, COLS),), flops=20000000000)(tables)
     tables = exchange(tables, "lon")
@@ -468,11 +465,11 @@
         ),
         ((2, T_FIELDS, ROWS, COLS), (PADLEV * ROWS, COLS)),
         flops=20000000000,
-    )(band, south)
+    )(own, west, south)
     parts = lax.all_gather(part, "obs", tiled=True)
-    source, side = call(
+    (source,) = call(
         functools.partial(spread_kernel, fields, owners),
-        ((T_BACK, ROWS, COLS), (T_BACK_SIDE, ROWS, COLS)),
+        ((T_BACK + T_BACK_SIDE, ROWS, COLS),),
         (
             (PART_ROWS, COLS),
             (2 * PADLEV, owners),
@@ -481,11 +478,11 @@
         ),
     )(parts, tables, weights, marks, aux)
     north = step(source, "lat", -1)
+    (side,) = call(back_kernel, ((2 * T_BACK_SIDE, ROWS, COLS),))(source, north)
     east = step(side, "lon", -1)
-    both = step_both(side, -1)
     image, sums = call(
         image_kernel, (block, (fields * lons, COLS)), ((2, T_BACK, ROWS, COLS),)
-    )(source, east, north, both, d, res)
+    )(source, north, east, d, res)
     sums = lax.all_to_all(sums, ("obs", "lon"), 0, 0, tiled=True)
     (sums,) = call(sum_kernel, ((lats, COLS),))(sums)
     sums = lax.all_to_all(sums, "lat", 0, 0, tiled=True)

time: 94.3 us -> 92.3 us (0.979)
  waiting for transfers between devices: 5.58 us -> 9.6 us
  starting transfers between devices: 33.5 us -> 30.2 us
  blocking collectives: 44.5 us -> 42.7 us
  Pallas kernels: 9.43 us -> 8.48 us
    ppermute x1 -> x0, starting transfers between devices: 5.76 us -> none  [step_both(): return lax.ppermute(x, ('lat', 'lon'), pairs)]
    ppermute x4, waiting for transfers between devices: 2.78 us -> 6.8 us  [step(): return lax.ppermute(x, axis, [(i, (i + by) % size) for i in range(size)])]
    ppermute x4, starting transfers between devices: 12 us -> 14.3 us  [step(): return lax.ppermute(x, axis, [(i, (i + by) % size) for i in range(size)])]
    all_to_all x1, blocking collectives: 11 us -> 9.99 us  [local(): sums = lax.all_to_all(sums, 'lat', 0, 0, tiled=True)]
    pallas_call x7 -> x8, Pallas kernels: 8.81 us -> 7.85 us  [call(): pl.pallas_call(kernel, out_shape=tuple((shape_of(out) for out in outs)),...]
  transfers between devices with their start and end apart: 7 -> 6, of which waited for: 2 -> 3; matrix products, arithmetic and copies ran while one was open for 0% -> 0% of each run, Pallas kernels for 4% -> 3%
where the time goes in v6:
time: 92.3 us; the launch traced here: 91.7 us
  blocking collectives  42.7 us (46%)
  starting transfers between devices  30.2 us (33%)
  waiting for transfers between devices  9.6 us (10%)
  Pallas kernels  8.48 us (9%)
    all_to_all x1, blocking collectives, local(): sums = lax.all_to_all(sums, ('obs', 'lon'), 0, 0, tiled=True)  17.6 us
    all_to_all x2, starting transfers between devices, exchange(): return lax.all_to_all(blocks, axis, 0, 0, tiled=True).reshape(x.shape)  15.9 us
    all_gather x1, blocking collectives, local(): parts = lax.all_gather(part, 'obs', tiled=True)  15.1 us
    ppermute x4, starting transfers between devices, step(): return lax.ppermute(x, axis, [(i, (i + by) % size) for i in range(size)])  14.3 us
    all_to_all x1, blocking collectives, local(): sums = lax.all_to_all(sums, 'lat', 0, 0, tiled=True)  9.99 us
    pallas_call x8, Pallas kernels, call(): pl.pallas_call(kernel, out_shape=tuple((shape_of(out) for out in outs)),...  7.85 us
    ppermute x4, waiting for transfers between devices, step(): return lax.ppermute(x, axis, [(i, (i + by) % size) for i in range(size)])  6.8 us
    all_to_all x2, waiting for transfers between devices, exchange(): return lax.all_to_all(blocks, axis, 0, 0, tiled=True).reshape(x.shape)  2.79 us
  transfers between devices with their start and end apart: 6, of which 3 were waited for; matrix products, arithmetic and copies ran while one was open for 0% of the time, Pallas kernels for 3%

profile of v6, /device:TPU:1, one launch (start us, length us, event | category | flops | bytes accessed | tf_op | source)
XLA Modules:
  0.0 91.7 jit_solution(11929117130708074294)
XLA Ops:
  0.6 1.9 %shard_map.130 = (f32[360,128]{1,0:T(8,128)}, f32[72,128]{1,0:T(8,128)}, f32[32,128]{1,0:T(8,128)}, f32[288,128]{1,0:T(8,128)}) custom-call(f32[200,128]{1,0:T(8,128)} %bitcast.25, s32[8,128]{1,0:T(8,128)} %flag.1, f32[8,128]{1,0:T(8,128)} %east.1, f32[8,128]{1,0:T(8,128)} %north.1, f32[8,128]{1,0:T(8,128)} %bitcast.39, f32[25,1,256]{2,1,0:T(1,128)} %bitcast.36, ...), custom_call_target="tpu_custom_call" | custom-call | flops 1000000 | bytes 1000000 | tf_op jit(solution)/shard_map/pallas_call | solution.py:375
  2.5 4.5 %collective-permute-start = (f32[72,128]{1,0:T(8,128)}, f32[72,128]{1,0:T(8,128)S(1)}, u32[]{:S(2)}, u32[]{:S(2)}) collective-permute-start(f32[72,128]{1,0:T(8,128)} %get-tuple-element.17), channel_id=1, source_target_pairs={{0,4},{4,8},{8,12},{12,16},{16,20},{20,24},{24,28},{28,32},{32,36}... | collective-permute-start | bytes 110600 | tf_op jit(solution)/shard_map/ppermute | solution.py:388
  7.0 10.0 %all-to-all-start = ((f32[8,4,128]{2,1,0:T(4,128)}), f32[8,4,128]{2,1,0:T(4,128)S(1)}, u32[]{:S(2)}, u32[]{:S(2)}) async-start(f32[8,4,128]{2,1,0:T(4,128)} %bitcast.37), calls=%async_computation | async-start | bytes 32768 | tf_op jit(solution)/shard_map/all_to_all | solution.py:394
  17.1 0.6 shard_map.131
  17.7 3.4 %collective-permute-start.1 = (f32[360,128]{1,0:T(8,128)}, f32[360,128]{1,0:T(8,128)S(1)}, u32[]{:S(2)}, u32[]{:S(2)}) collective-permute-start(f32[360,128]{1,0:T(8,128)} %shard_map.131), channel_id=1, source_target_pairs={{0,64},{64,128},{128,192},{192,256},{256,320},{320,384},{384,448},... | collective-permute-start | bytes 552968 | tf_op jit(solution)/shard_map/ppermute | solution.py:388
  21.1 2.8 %all-to-all-done = f32[8,4,128]{2,1,0:T(4,128)S(1)} async-done(((f32[8,4,128]{2,1,0:T(4,128)}), f32[8,4,128]{2,1,0:T(4,128)S(1)}, u32[]{:S(2)}, u32[]{:S(2)}) %all-to-all-start) | async-done | bytes 16416 | tf_op jit(solution)/shard_map/all_to_all | solution.py:394
  23.9 0.7 shard_map.133
  24.6 5.8 %all-to-all-start.1 = ((f32[16,32,128]{2,1,0:T(8,128)}), f32[16,32,128]{2,1,0:T(8,128)S(1)}, u32[]{:S(2)}, u32[]{:S(2)}) async-start(f32[16,32,128]{2,1,0:T(8,128)} %bitcast.8), calls=%async_computation.1 | async-start | bytes 524288 | tf_op jit(solution)/shard_map/all_to_all | solution.py:394
  30.5 0.0 collective-permute-done.1.south
  30.5 1.6 %shard_map.132 = (f32[200,128]{1,0:T(8,128)S(1)}, f32[3,8,128]{2,1,0:T(8,128)S(1)}, f32[32,1024]{1,0:T(8,128)S(1)}, s32[8,1024]{1,0:T(8,128)S(1)}) custom-call(f32[288,128]{1,0:T(8,128)S(1)} %copy-done.3, f32[72,128]{1,0:T(8,128)S(1)} %collective-permute-done.west, f32[360,128]{1,0:T(8,128)S(1)} %collective-permute-done.1.south), custom_call_target="tpu_custom_call" | custom-call | flops 20000000000 | bytes 1000000 | tf_op jit(solution)/shard_map/pallas_call | solution.py:375
  32.1 15.1 %all_gather.3.parts = f32[800,128]{1,0:T(8,128)S(1)} all-gather(f32[200,128]{1,0:T(8,128)S(1)} %get-tuple-element.19), channel_id=1, replica_groups=mesh['lat'=8,'lon'=16,'obs'=4] {'obs'}, dimensions={0}, use_global_device_ids=true | all-gather | bytes 512000 | tf_op jit(solution)/shard_map/all_gather | solution.py:469
  47.1 0.0 all-to-all-done.1
  47.1 1.2 %shard_map.134.own = f32[29,8,128]{2,1,0:T(8,128)S(1)} custom-call(f32[800,128]{1,0:T(8,128)S(1)} %all_gather.3.parts, f32[512,128]{1,0:T(8,128)S(1)} %bitcast.24, f32[32,1024]{1,0:T(8,128)S(1)} %get-tuple-element.21.weights, s32[8,1024]{1,0:T(8,128)S(1)} %get-tuple-element.22.marks, f32[3,8,128]{2,1,0:T(8,128)S(1)} %get-tuple-element.23.aux), custom_call_target="tpu_custom_call" | custom-call | flops 1000000 | bytes 1000000 | tf_op jit(solution)/shard_map/pallas_call | solution.py:375
  48.4 0.0 copy-start
  48.4 0.0 copy-start.1
  48.4 2.1 %collective-permute-start.2 = (f32[29,8,128]{2,1,0:T(8,128)S(1)}, f32[29,8,128]{2,1,0:T(8,128)S(1)}, u32[]{:S(2)}, u32[]{:S(2)}) collective-permute-start(f32[29,8,128]{2,1,0:T(8,128)S(1)} %shard_map.134.own), channel_id=1, source_target_pairs={{0,448},{64,0},{128,64},{192,128},{256,192},{320,256},{384,320},{4... | collective-permute-start | bytes 356360 | tf_op jit(solution)/shard_map/ppermute | solution.py:388
  50.5 3.6 %collective-permute-done.2.north = f32[29,8,128]{2,1,0:T(8,128)S(1)} collective-permute-done((f32[29,8,128]{2,1,0:T(8,128)S(1)}, f32[29,8,128]{2,1,0:T(8,128)S(1)}, u32[]{:S(2)}, u32[]{:S(2)}) %collective-permute-start.2) | collective-permute-done | bytes 118816 | tf_op jit(solution)/shard_map/ppermute | solution.py:388
  54.1 4.3 %collective-permute-start.3 = (f32[4,8,128]{2,1,0:T(8,128)S(1)}, f32[4,8,128]{2,1,0:T(8,128)S(1)}, u32[]{:S(2)}, u32[]{:S(2)}) collective-permute-start(f32[4,8,128]{2,1,0:T(8,128)S(1)} %shard_map.135), channel_id=1, source_target_pairs={{0,60},{4,0},{8,4},{12,8},{16,12},{20,16},{24,20},{28,24},{32,28},... | collective-permute-start | bytes 49160 | tf_op jit(solution)/shard_map/ppermute | solution.py:388
  58.4 3.2 %collective-permute-done.3.east = f32[4,8,128]{2,1,0:T(8,128)S(1)} collective-permute-done((f32[4,8,128]{2,1,0:T(8,128)S(1)}, f32[4,8,128]{2,1,0:T(8,128)S(1)}, u32[]{:S(2)}, u32[]{:S(2)}) %collective-permute-start.3) | collective-permute-done | bytes 16416 | tf_op jit(solution)/shard_map/ppermute | solution.py:388
  61.7 1.6 %shard_map.136 = (f32[25,8,128]{2,1,0:T(8,128)S(1)}, f32[64,128]{1,0:T(8,128)S(1)}) custom-call(f32[29,8,128]{2,1,0:T(8,128)S(1)} %shard_map.134.own, f32[29,8,128]{2,1,0:T(8,128)S(1)} %collective-permute-done.2.north, f32[4,8,128]{2,1,0:T(8,128)S(1)} %collective-permute-done.3.east, f32[25,8,128]{2,1,0:T(8,128)S(1)} %bitcast.26, f32[25,8,128]{2,1,0:T(8,128)S(1)} %bitcast.28), custom_call_target="tpu_custom_call" | custom-call | flops 1000000 | bytes 1000000 | tf_op jit(solution)/shard_map/pallas_call | solution.py:375
  63.3 0.0 copy-start.2
  63.3 17.6 %all_to_all.32 = f32[64,1,128]{2,1,0:T(1,128)S(1)} all-to-all(f32[64,1,128]{2,1,0:T(1,128)S(1)} %bitcast.32), channel_id=1, replica_groups=mesh['lat'=8,'lon'=16,'obs'=4] {'obs','lon'}, dimensions={0} | all-to-all | bytes 65536 | tf_op jit(solution)/shard_map/all_to_all | solution.py:486
  80.9 10.0 %all_to_all.33 = f32[8,1,128]{2,1,0:T(1,128)S(1)} all-to-all(f32[8,1,128]{2,1,0:T(1,128)S(1)} %bitcast.34), channel_id=1, replica_groups=mesh['lat'=8,'lon'=16,'obs'=4] {'lat'}, dimensions={0} | all-to-all | bytes 8192 | tf_op jit(solution)/shard_map/all_to_all | solution.py:488
  90.9 0.8 shard_map.138
  (8 shorter events, 0.0 us)
Async XLA Ops:
  2.5 14.6 %collective-permute-start = (f32[72,128]{1,0:T(8,128)}, f32[72,128]{1,0:T(8,128)S(1)}, u32[]{:S(2)}, u32[]{:S(2)}) collective-permute-start(f32[72,128]{1,0:T(8,128)} %get-tuple-element.17), channel_id=1, source_target_pairs={{0,4},{4,8},{8,12},{12,16},{16,20},{20,24},{24,28},{28,32},{32,36}... | collective-permute-start | bytes 110600 | tf_op jit(solution)/shard_map/ppermute | solution.py:388
  7.0 16.9 %all-to-all-start = ((f32[8,4,128]{2,1,0:T(4,128)}), f32[8,4,128]{2,1,0:T(4,128)S(1)}, u32[]{:S(2)}, u32[]{:S(2)}) async-start(f32[8,4,128]{2,1,0:T(4,128)} %bitcast.37), calls=%async_computation | async-start | bytes 32768 | tf_op jit(solution)/shard_map/all_to_all | solution.py:394
  17.7 12.7 %collective-permute-start.1 = (f32[360,128]{1,0:T(8,128)}, f32[360,128]{1,0:T(8,128)S(1)}, u32[]{:S(2)}, u32[]{:S(2)}) collective-permute-start(f32[360,128]{1,0:T(8,128)} %shard_map.131), channel_id=1, source_target_pairs={{0,64},{64,128},{128,192},{192,256},{256,320},{320,384},{384,448},... | collective-permute-start | bytes 552968 | tf_op jit(solution)/shard_map/ppermute | solution.py:388
  24.6 5.8 %copy-start.3 = (f32[288,128]{1,0:T(8,128)S(1)}, f32[288,128]{1,0:T(8,128)}, u32[]{:S(2)}) copy-start(f32[288,128]{1,0:T(8,128)} %get-tuple-element.16.own) | copy-start | bytes 442372
  24.6 22.5 %all-to-all-start.1 = ((f32[16,32,128]{2,1,0:T(8,128)}), f32[16,32,128]{2,1,0:T(8,128)S(1)}, u32[]{:S(2)}, u32[]{:S(2)}) async-start(f32[16,32,128]{2,1,0:T(8,128)} %bitcast.8), calls=%async_computation.1 | async-start | bytes 524288 | tf_op jit(solution)/shard_map/all_to_all | solution.py:394
  48.4 13.3 %copy-start = (f32[1,25,8,128]{3,2,1,0:T(8,128)S(1)}, f32[1,25,8,128]{3,2,1,0:T(8,128)}, u32[]{:S(2)}) copy-start(f32[1,25,8,128]{3,2,1,0:T(8,128)} %param.13) | copy-start | bytes 307204
  48.4 13.3 %copy-start.1 = (f32[1,25,8,128]{3,2,1,0:T(8,128)S(1)}, f32[1,25,8,128]{3,2,1,0:T(8,128)}, u32[]{:S(2)}) copy-start(f32[1,25,8,128]{3,2,1,0:T(8,128)} %param.12) | copy-start | bytes 307204
  48.4 5.7 %collective-permute-start.2 = (f32[29,8,128]{2,1,0:T(8,128)S(1)}, f32[29,8,128]{2,1,0:T(8,128)S(1)}, u32[]{:S(2)}, u32[]{:S(2)}) collective-permute-start(f32[29,8,128]{2,1,0:T(8,128)S(1)} %shard_map.134.own), channel_id=1, source_target_pairs={{0,448},{64,0},{128,64},{192,128},{256,192},{320,256},{384,320},{4... | collective-permute-start | bytes 356360 | tf_op jit(solution)/shard_map/ppermute | solution.py:388
  54.1 7.6 %collective-permute-start.3 = (f32[4,8,128]{2,1,0:T(8,128)S(1)}, f32[4,8,128]{2,1,0:T(8,128)S(1)}, u32[]{:S(2)}, u32[]{:S(2)}) collective-permute-start(f32[4,8,128]{2,1,0:T(8,128)S(1)} %shard_map.135), channel_id=1, source_target_pairs={{0,60},{4,0},{8,4},{12,8},{16,12},{20,16},{24,20},{28,24},{32,28},... | collective-permute-start | bytes 49160 | tf_op jit(solution)/shard_map/ppermute | solution.py:388
  63.3 27.6 %copy-start.2 = (f32[1,25,8,128]{3,2,1,0:T(8,128)S(1)}, f32[1,25,8,128]{3,2,1,0:T(8,128)}, u32[]{:S(2)}) copy-start(f32[1,25,8,128]{3,2,1,0:T(8,128)} %param.11) | copy-start | bytes 307204
